TPU v7x, 32 devices: a whole 2x2x4 slice. The times are simulated.
32 devices in a mesh: beam: 2 (over y), inp: 8 (over z, x), span: 2 (over core).
Axes of the slice: x: 2, y: 2, z: 4, core: 2. Of those that a mesh axis runs over, the one named last changes fastest.
Arguments:
- voltages: bfloat16 [2, 8, 1024, 16384], P(None, 'beam', 'inp', 'span'), parts along dimension 1, may hold values from -6 to 6
- gains: float32 [2, 8, 1024, 32], P(None, 'beam', 'inp'), parts along dimension 1, may hold values from -4 to 4
Outputs:
- visibilities: bfloat16 [256, 1024, 1024], P(('beam', 'inp'), 'span'), parts along dimension 0
There are 2 independent parts, one for each index of `beam`. A program takes and returns all parts, laid end to end along the dimension named above; each array names one. Nothing has to cross between parts.
All inputs are finite; a program needn't handle non-finite values.
Results may differ from a plain program's by a relative error of at most 0.0085.
Values may be sent and summed in bfloat16 or wider, within the bound.
No kernel may reach another device: no remote copies, remote signals or barrier semaphores. Data moves between devices by JAX's collectives and lax.ppermute only.
A program may use at most 192 MiB of HBM per device.

v0:
```python
import math

import jax
import jax.numpy as jnp
from jax import lax
from jax.sharding import PartitionSpec as P

FINE = 32
TAPS = 4


def prototype(tap_count, fine_count):
    length = tap_count * fine_count
    offsets = jnp.arange(length).astype(jnp.float32)
    shifted = (offsets - length / 2 + 0.5) / fine_count
    taper = 0.5 - 0.5 * jnp.cos(2.0 * math.pi * (offsets + 0.5) / length)
    window = jnp.sinc(shifted) * taper
    window = window / jnp.sqrt(jnp.sum(window * window))
    return window.reshape(tap_count, fine_count)


def kernels(window, fine_count):
    points = jnp.arange(fine_count)
    phase_steps = points[:, None] * points[None, :] % fine_count
    angles = 2.0 * math.pi * phase_steps.astype(jnp.float32) / fine_count
    cosine = jnp.cos(angles)
    sine_part = jnp.sin(angles)
    result = []
    for tap_index in range(window.shape[0]):
        weights = window[tap_index][:, None]
        hcos = weights * cosine
        hsin = weights * sine_part
        result.append(jnp.stack([jnp.stack([hcos, -hsin]), jnp.stack([hsin, hcos])]))
    return jnp.stack(result)


def packed_rows(left_rows, right_rows, left_all, row_start):
    real_sums = jnp.einsum("cif,cjf->cij", left_rows, left_all, preferred_element_type=jnp.float32)
    imag_sums = jnp.einsum("cif,cjf->cij", right_rows, left_all, preferred_element_type=jnp.float32)
    row_index = row_start + jnp.arange(left_rows.shape[1])
    col_index = jnp.arange(left_all.shape[1])
    upper = row_index[:, None] <= col_index[None, :]
    return jnp.where(upper[None], real_sums, imag_sums)


def local(voltages, gains):
    coarse = voltages.shape[1]
    local_inputs = voltages.shape[2]
    samples = voltages.shape[3]
    frames = samples // FINE
    window = prototype(TAPS, FINE)
    filters = kernels(window, FINE)
    filter_table = jnp.transpose(filters, (1, 0, 3, 2, 4))
    filter_high = filter_table.astype(jnp.bfloat16)
    filter_low = (filter_table - filter_high.astype(jnp.float32)).astype(jnp.bfloat16)
    padded = jnp.pad(voltages, ((0, 0), (0, 0), (0, 0), (0, (TAPS - 1) * FINE)))
    stacked = jnp.stack(
        [padded[..., tap_index * FINE : tap_index * FINE + samples] for tap_index in range(TAPS)],
        axis=1,
    )
    stacked = stacked.reshape(2, TAPS, coarse, local_inputs, frames, FINE)
    spectra = jnp.einsum(
        "atcnmp,atpbk->bcknm", stacked, filter_high, preferred_element_type=jnp.float32
    )
    spectra = spectra + jnp.einsum(
        "atcnmp,atpbk->bcknm", stacked, filter_low, preferred_element_type=jnp.float32
    )
    gain_real = jnp.swapaxes(gains[0], 1, 2)[:, :, :, None]
    gain_imag = jnp.swapaxes(gains[1], 1, 2)[:, :, :, None]
    real_part = spectra[0] * gain_real - spectra[1] * gain_imag
    imag_part = spectra[0] * gain_imag + spectra[1] * gain_real
    outgoing = jnp.stack([real_part, imag_part]).astype(jnp.bfloat16)
    outgoing = outgoing.reshape(2, coarse * FINE, local_inputs, frames)
    turned = lax.all_to_all(outgoing, "inp", split_axis=1, concat_axis=2, tiled=True)
    inputs = turned.shape[2]
    span_count = lax.axis_size("span")
    row_count = inputs // span_count
    frame_scale = 1.0 / (span_count * frames)
    row_start = lax.axis_index("span") * row_count
    frame_piece = lax.all_gather(turned, "span", axis=3, tiled=True)
    left_all = jnp.concatenate([frame_piece[0], frame_piece[1]], axis=-1)
    own_rows = lax.dynamic_slice_in_dim(frame_piece, row_start, row_count, 2)
    left_rows = jnp.concatenate([own_rows[0], own_rows[1]], axis=-1)
    right_rows = jnp.concatenate([own_rows[1], -own_rows[0]], axis=-1)
    summed = packed_rows(left_rows, right_rows, left_all, row_start) * frame_scale
    return summed.astype(jnp.bfloat16)


def solution(mesh):
    placed = (P(None, "beam", "inp", "span"), P(None, "beam", "inp", None))
    return jax.shard_map(
        local,
        mesh=mesh,
        in_specs=placed,
        out_specs=P(("beam", "inp"), "span", None),
        check_vma=False,
    )
```

profile of v0, /device:TPU:0, one launch (start us, length us, event | category | flops | bytes accessed | tf_op | source)
XLA Modules:
  0.0 864.5 jit_solution(2377499240589222631)
XLA Ops:
  6.5 0.0 all-gather.2.cloned.1.call-start
  6.5 0.7 multiply_reduce_fusion
  7.9 0.1 fusion.45
  8.0 21.2 %copy.28 = bf16[2,4,128,8192]{2,3,1,0:T(8,128)(2,1)} copy(bf16[2,4,128,8192]{3,2,1,0:T(8,128)(2,1)} %param.2) | data formatting | bytes 33554432 | tf_op args[0]
  29.2 32.5 %pad_slice_fusion.2 = (bf16[2,4,128,8192]{2,3,1,0:T(8,128)(2,1)}, bf16[2,4,128,8192]{2,3,1,0:T(8,128)(2,1)}, bf16[2,4,128,8192]{2,3,1,0:T(8,128)(2,1)}) fusion(bf16[2,4,128,8192]{2,3,1,0:T(8,128)(2,1)} %copy.28), kind=kLoop, calls=%fused_computation.22 | loop fusion | bytes 67108864 | tf_op jit(solution)/shard_map/slice | solution.py:58
  61.6 30.6 %copy.31 = bf16[2,1,4,128,256,32]{4,5,1,0,3,2:T(8,128)(2,1)} copy(bf16[2,1,4,128,256,32]{3,5,4,2,0,1:T(8,128)(2,1)} %bitcast.137) | data formatting | bytes 33554432 | tf_op jit(solution)/shard_map/stack | solution.py:57
  92.3 30.7 %copy.32 = bf16[2,1,4,128,256,32]{4,5,1,0,3,2:T(8,128)(2,1)} copy(bf16[2,1,4,128,256,32]{3,5,4,2,0,1:T(8,128)(2,1)} %bitcast.136) | data formatting | bytes 33554432 | tf_op jit(solution)/shard_map/stack | solution.py:57
  122.9 30.7 %copy.33 = bf16[2,1,4,128,256,32]{4,5,1,0,3,2:T(8,128)(2,1)} copy(bf16[2,1,4,128,256,32]{3,5,4,2,0,1:T(8,128)(2,1)} %bitcast.135) | data formatting | bytes 33554432 | tf_op jit(solution)/shard_map/stack | solution.py:57
  153.6 30.7 %copy.30 = bf16[2,1,4,128,256,32]{4,5,1,0,3,2:T(8,128)(2,1)} copy(bf16[2,1,4,128,256,32]{3,5,4,2,0,1:T(8,128)(2,1)} %bitcast.132) | data formatting | bytes 33554432 | tf_op jit(solution)/shard_map/stack | solution.py:57
  184.2 0.1 fusion.29
  184.4 0.1 fusion.31
  184.6 36.7 %fusion.1 = f32[2,32,4,128,256,1,1]{4,1,6,5,3,2,0:T(8,128)} fusion(bf16[2,1,4,128,256,32]{4,5,1,0,3,2:T(8,128)(2,1)} %copy.33, bf16[2,1,4,128,256,32]{4,5,1,0,3,2:T(8,128)(2,1)} %copy.32, bf16[2,1,4,128,256,32]{4,5,1,0,3,2:T(8,128)(2,1)} %copy.31, bf16[2,1,4,128,256,32]{4,5,1,0,3,2:T(8,128)(2,1)} %copy.30, ...), kind=kOutput, calls=%fused_computation.5 | convolution fusion | flops 4563521536 | bytes 100728832 | tf_op jit(solution)/shard_map/atcnmp,atpbk->bcknm/dot_general | solution.py:65
  221.3 0.0 copy-start
  221.3 44.4 %fusion = f32[2,4,32,128,256]{4,2,3,1,0:T(8,128)} fusion(f32[2,32,4,128,256,1,1]{4,1,6,5,3,2,0:T(8,128)} %fusion.1, bf16[2,1,4,128,256,32]{4,5,1,0,3,2:T(8,128)(2,1)} %copy.33, bf16[2,1,4,128,256,32]{4,5,1,0,3,2:T(8,128)(2,1)} %copy.32, bf16[2,1,4,128,256,32]{4,5,1,0,3,2:T(8,128)(2,1)} %copy.31, bf16[2,1,4,128,256,32]{4,5,1,0,3,2:T(8,128)(2,1)} %copy.30, ...), kind=kOutput, calls=%fused_computation.3 | convolution fusion | flops 4571926528 | bytes 134283264 | tf_op jit(solution)/shard_map/atcnmp,atpbk->bcknm/dot_general | solution.py:62
  265.6 0.0 copy-done
  265.7 0.1 copy.34
  265.8 0.1 copy.35
  265.9 17.8 %subtract_convert_fusion = (bf16[1,4,32,128,256]{4,2,3,1,0:T(8,128)(2,1)}, bf16[1,4,32,128,256]{4,2,3,1,0:T(8,128)(2,1)}) fusion(f32[2,4,32,128,256]{4,2,3,1,0:T(8,128)} %fusion, f32[4,32,128]{1,2,0:T(8,128)S(1)} %copy.35, f32[4,32,128]{1,2,0:T(8,128)S(1)} %copy.34), kind=kLoop, calls=%fused_computation.19 | loop fusion | flops 33554432 | bytes 50462720 | tf_op jit(solution)/shard_map/convert.3
  283.8 11.5 %copy.36 = bf16[1,4,32,128,256]{4,3,2,1,0:T(8,128)(2,1)} copy(bf16[1,4,32,128,256]{4,2,3,1,0:T(8,128)(2,1)} %get-tuple-element.7) | data formatting | bytes 16777216 | tf_op jit(solution)/shard_map/convert.3
  295.2 11.6 %copy.37 = bf16[1,4,32,128,256]{4,3,2,1,0:T(8,128)(2,1)} copy(bf16[1,4,32,128,256]{4,2,3,1,0:T(8,128)(2,1)} %get-tuple-element.8) | data formatting | bytes 16777216 | tf_op jit(solution)/shard_map/convert.2
  306.9 8.0 pad_maximum_fusion.3
  314.9 2.0 copy.38
  316.9 369.9 %all_to_all.18 = bf16[2,128,128,256]{3,2,0,1:T(8,128)(2,1)S(1)} all-to-all(bf16[2,128,128,256]{3,2,0,1:T(8,128)(2,1)S(1)} %copy.38), channel_id=1, replica_groups=mesh['beam'=2,'inp'=8,'span'=2] {'inp'}, dimensions={1} | all-to-all | bytes 33554432 | tf_op jit(solution)/shard_map/all_to_all | solution.py:74
  686.8 6.5 copy.40
  693.3 0.0 all-gather.2.cloned.1.call-update
  693.3 0.4 iota_compare_fusion
  693.7 50.0 %all-gather.2.cloned.1.call-done = bf16[2,16,1024,512]{3,2,1,0:T(8,128)(2,1)} async-done(((bf16[2,16,1024,256]{3,2,1,0:T(8,128)(2,1)}), bf16[2,16,1024,512]{3,2,1,0:T(8,128)(2,1)}) %all-gather.2.cloned.1.call-update) | async-done | bytes 33554448 | tf_op jit(solution)/shard_map/all_gather | solution.py:80
  743.6 22.5 %slice_bitcast_fusion.1 = (bf16[16,1024,512]{2,1,0:T(8,128)(2,1)}, bf16[16,1024,512]{2,1,0:T(8,128)(2,1)}) fusion(bf16[2,16,1024,512]{3,2,1,0:T(8,128)(2,1)} %all-gather.2.cloned.1.call-done), kind=kLoop, calls=%fused_computation.10 | loop fusion | bytes 67108864 | tf_op jit(solution)/shard_map/squeeze | solution.py:81
  766.1 10.3 %fusion.44 = (bf16[16,512,512]{2,1,0:T(8,128)(2,1)}, bf16[16,512,512]{2,1,0:T(8,128)(2,1)}) fusion(bf16[2,16,1024,512]{3,2,1,0:T(8,128)(2,1)} %all-gather.2.cloned.1.call-done, s32[]{:T(128)S(6)} %select_n.117), kind=kLoop, calls=%fused_computation.91 | loop fusion | flops 12582912 | bytes 25165828 | tf_op jit(solution)/shard_map/neg | solution.py:84
  776.4 7.4 dynamic-slice_bitcast_fusion
  783.8 36.8 %fusion.3 = f32[16,512,1024]{2,1,0:T(8,128)} fusion(bf16[16,1024,512]{2,1,0:T(8,128)(2,1)} %get-tuple-element.10, bf16[16,1024,512]{2,1,0:T(8,128)(2,1)} %get-tuple-element.9, bf16[16,512,512]{2,1,0:T(8,128)(2,1)} %get-tuple-element.5, bf16[16,512,512]{2,1,0:T(8,128)(2,1)} %dynamic-slice_bitcast_fusion), kind=kOutput, calls=%fused_computation.7 | convolution fusion | flops 17280532480 | bytes 83886080 | tf_op jit(solution)/shard_map/cif,cjf->cij/dot_general | solution.py:39
  820.6 37.0 %multiply_convert_fusion = bf16[16,512,1024]{2,1,0:T(8,128)(2,1)} fusion(f32[16,512,1024]{2,1,0:T(8,128)} %fusion.3, pred[512,1024]{1,0:T(8,128)(4,1)S(1)} %iota_compare_fusion, bf16[16,1024,512]{2,1,0:T(8,128)(2,1)} %get-tuple-element.10, bf16[16,1024,512]{2,1,0:T(8,128)(2,1)} %get-tuple-element.9, bf16[16,512,512]{2,1,0:T(8,128)(2,1)} %dynamic-slice_bitcast_fusion, ...), kind=kOutput, calls=%fused_computation.4 | convolution fusion | flops 17305698304 | bytes 101187584 | tf_op jit(solution)/shard_map/cif,cjf->cij/dot_general | solution.py:38
  (10 shorter events, 0.1 us)
Async XLA Ops:
  6.5 737.1 %all-gather.2.cloned.1.call-start = ((), (), s32[]{:S(2)}) async-start(), calls=%async_computation.1 | async-start | bytes 50331648 | tf_op jit(solution)/shard_map/all_gather | solution.py:80
  221.3 44.4 %copy-start = (f32[2,4,128,32]{2,3,1,0:T(8,128)S(1)}, f32[2,4,128,32]{2,3,1,0:T(8,128)}, u32[]{:S(2)}) copy-start(f32[2,4,128,32]{2,3,1,0:T(8,128)} %param.3) | copy-start | bytes 393220
Sparse Core Ops, SparseCore 0:
  693.4 50.1 all-gather.1
where the time goes:
time: 868 us; the launch traced here: 864 us
  blocking collectives  370 us (43%)
  local copies, waits for them, and re-layouts  238 us (27%)
  matrix products  155 us (18%)
  waiting for transfers between devices  50 us (6%)
  other arithmetic  37.4 us (4%)
  between operations  14.2 us (2%)
    all_to_all x1, blocking collectives, local(): lax.all_to_all(outgoing, 'inp', split_axis=1, concat_axis=2, tiled=True)  370 us
    another operation x4, local copies, waits for them, and re-layouts, local(): jnp.stack([padded[..., tap_index * FINE:tap_index * FINE + samples] for t...  123 us
    all_gather x1, waiting for transfers between devices, local(): frame_piece = lax.all_gather(turned, 'span', axis=3, tiled=True)  50 us
    dot_general x1, matrix products, local(): jnp.einsum('atcnmp,atpbk->bcknm', stacked, filter_high, preferred_element...  44.4 us
    dot_general x1, matrix products, packed_rows(): jnp.einsum('cif,cjf->cij', left_rows, left_all, preferred_element_type=jn...  37 us
    dot_general x1, matrix products, packed_rows(): jnp.einsum('cif,cjf->cij', right_rows, left_all, preferred_element_type=j...  36.8 us
    dot_general x1, matrix products, local(): jnp.einsum('atcnmp,atpbk->bcknm', stacked, filter_low, preferred_element_...  36.7 us
    slice x1, local copies, waits for them, and re-layouts, local(): padded[..., tap_index * FINE:tap_index * FINE + samples]  32.5 us
  transfers between devices with their start and end apart: 1, of which 1 were waited for; matrix products, arithmetic and copies ran while one was open for 0% of the time, Pallas kernels for 0%

commit v1 on v0

--- a/solution.py
+++ b/solution.py
@@ -1,12 +1,20 @@
+import functools
 import math
 
 import jax
 import jax.numpy as jnp
+import ml_dtypes
+import numpy as np
 from jax import lax
+from jax.experimental import pallas as pl
+from jax.experimental.pallas import tpu as pltpu
 from jax.sharding import PartitionSpec as P
 
 FINE = 32
 TAPS = 4
+LANES = 128
+GROUP = 8
+VMEM = 48 * 1024 * 1024
 
 
 def prototype(tap_count, fine_count):
@@ -43,7 +51,7 @@
     return jnp.where(upper[None], real_sums, imag_sums)
 
 
-def local(voltages, gains):
+def local_plain(voltages, gains):
     coarse = voltages.shape[1]
     local_inputs = voltages.shape[2]
     samples = voltages.shape[3]
@@ -86,7 +94,298 @@
     return summed.astype(jnp.bfloat16)
 
 
+def filter_rows(halves):
+    length = TAPS * FINE
+    run = -(-(GROUP * FINE + length - FINE) // LANES) * LANES
+    offsets = np.arange(length)
+    window = np.sinc((offsets - length / 2 + 0.5) / FINE)
+    window = window * (0.5 - 0.5 * np.cos(2.0 * np.pi * (offsets + 0.5) / length))
+    window = window / np.sqrt(np.sum(window * window))
+    angles = 2.0 * np.pi * (offsets[None, :] * np.arange(FINE)[:, None] % FINE) / FINE
+    hcos = window * np.cos(angles)
+    hsin = window * np.sin(angles)
+    table = np.zeros((FINE, 2, GROUP, 2, run))
+    for frame in range(GROUP):
+        at = slice(frame * FINE, frame * FINE + length)
+        table[:, 0, frame, 0, at] = hcos
+        table[:, 0, frame, 1, at] = hsin
+        table[:, 1, frame, 0, at] = -hsin
+        table[:, 1, frame, 1, at] = hcos
+    return table.reshape(halves, -1, 2 * run).astype(ml_dtypes.bfloat16)
+
+
+def filter_kernel(halves, chunks, where_ref, now_ref, next_ref, gain_ref, *rest):
+    table_refs = rest[:halves]
+    outs = rest[halves:-2]
+    turned_ref, wide_ref = rest[-2:]
+    step = pl.program_id(0)
+    inputs, samples = now_ref.shape[2], now_ref.shape[3]
+    per_half = FINE // halves
+    run = table_refs[0].shape[2] // 2
+    pair = 2 * GROUP
+
+    @pl.when(step == 0)
+    def _():
+        for part in range(2):
+            turned_ref[part] = gain_ref[part, 0].T
+            for half in range(halves):
+                start = pl.multiple_of(where_ref[1 + half] * per_half, per_half)
+                rows = turned_ref[part, pl.ds(start, per_half), :]
+                wide_ref[part, half] = jnp.broadcast_to(rows[:, None, :], (per_half, pair, inputs))
+
+    last = step == pl.num_programs(0) - 1
+    following = next_ref[:, 0]
+    following = jnp.where(last, jnp.zeros_like(following), following)
+    table = jnp.concatenate([table_refs[half][0] for half in range(halves)], axis=0)
+    for block in range(samples // (pair * FINE)):
+        sets = []
+        for group in range(2):
+            start = (2 * block + group) * GROUP * FINE
+            stop = start + run
+            columns = []
+            for part in range(2):
+                columns.append(now_ref[part, 0, :, start : min(stop, samples)])
+                if stop > samples:
+                    columns.append(following[part, :, : stop - samples])
+            sets.append(jnp.concatenate(columns, axis=1))
+        lines = jnp.concatenate(sets, axis=0)
+        sums = lax.dot_general(
+            table, lines, (((1,), (1,)), ((), ())), preferred_element_type=jnp.float32
+        )
+        sums = sums.reshape(halves, per_half, 2, GROUP, 2 * inputs)
+        sums = jnp.concatenate([sums[..., :inputs], sums[..., inputs:]], axis=3)
+        frames = slice(block * pair, (block + 1) * pair)
+        for half in range(halves):
+            raw_real, raw_imag = sums[half, :, 0], sums[half, :, 1]
+            gain_real, gain_imag = wide_ref[0, half], wide_ref[1, half]
+            real = (raw_real * gain_real - raw_imag * gain_imag).astype(jnp.bfloat16)
+            imag = (raw_real * gain_imag + raw_imag * gain_real).astype(jnp.bfloat16)
+            start = 0
+            for index, count in enumerate(chunks):
+                out = outs[half * len(chunks) + index]
+                out[:, 0, frames, :] = real[start : start + count]
+                out[:, 1, frames, :] = imag[start : start + count]
+                start += count
+
+
+def filter_bank(voltages, gains, tables, where, halves, chunks, samples_step):
+    _, _, inputs, samples = voltages.shape
+    frames = samples // FINE
+    steps = samples // samples_step
+    ratio = samples_step // LANES
+    frames_step = samples_step // FINE
+    _, table_rows, table_columns = tables.shape
+    spec = pltpu.PrefetchScalarGridSpec(
+        num_scalar_prefetch=1,
+        grid=(steps,),
+        in_specs=[
+            pl.BlockSpec((2, 1, inputs, samples_step), lambda t, w: (0, w[0], 0, t)),
+            pl.BlockSpec(
+                (2, 1, inputs, LANES),
+                lambda t, w: (0, w[0], 0, jnp.minimum((t + 1) * ratio, steps * ratio - 1)),
+            ),
+            pl.BlockSpec((2, 1, inputs, FINE), lambda t, w: (0, w[0], 0, 0)),
+        ]
+        + [
+            pl.BlockSpec((1, table_rows, table_columns), lambda t, w, half=half: (w[1 + half], 0, 0))
+            for half in range(halves)
+        ],
+        out_specs=[
+            pl.BlockSpec((count, 2, frames_step, inputs), lambda t, w: (0, 0, t, 0))
+            for _ in range(halves)
+            for count in chunks
+        ],
+        scratch_shapes=[
+            pltpu.VMEM((2, FINE, inputs), jnp.float32),
+            pltpu.VMEM((2, halves, FINE // halves, 2 * GROUP, inputs), jnp.float32),
+        ],
+    )
+    flops = 2 * 2 * FINE * GROUP * table_columns * inputs * (frames // GROUP)
+    outs = pl.pallas_call(
+        functools.partial(filter_kernel, halves, chunks),
+        out_shape=[
+            jax.ShapeDtypeStruct((count, 2, frames, inputs), jnp.bfloat16)
+            for _ in range(halves)
+            for count in chunks
+        ],
+        grid_spec=spec,
+        compiler_params=pltpu.CompilerParams(vmem_limit_bytes=VMEM),
+        cost_estimate=pl.CostEstimate(
+            flops=flops, bytes_accessed=16 * inputs * samples, transcendentals=0
+        ),
+        name="filter_bank",
+    )(where, voltages, voltages, gains, *([tables] * halves))
+    return [outs[half * len(chunks) : (half + 1) * len(chunks)] for half in range(halves)]
+
+
+def correlate_kernel(count, spans, tile, scale, where_ref, *rest):
+    blocks = rest[: count * spans]
+    out_ref, all_ref, rows_ref = rest[-3:]
+    _, _, frames, inputs = blocks[0].shape
+    total = all_ref.shape[2]
+    row_count = out_ref.shape[1]
+    depth = spans * 2 * frames
+    for span in range(spans):
+        for index in range(count):
+            start = pl.multiple_of(where_ref[index] * inputs, inputs)
+            for part in range(2):
+                all_ref[2 * span + part, :, pl.ds(start, inputs)] = blocks[span * count + index][0, part]
+    first_row = pl.multiple_of(where_ref[count] * row_count, row_count)
+    for start in range(0, row_count, LANES):
+        for span in range(spans):
+            for part in range(2):
+                at = pl.multiple_of(first_row + start, LANES)
+                piece = all_ref[2 * span + part, :, pl.ds(at, LANES)].T
+                rows = slice(start, start + LANES)
+                same = slice((2 * span + part) * frames, (2 * span + part + 1) * frames)
+                swap = slice((2 * span + 1 - part) * frames, (2 * span + 2 - part) * frames)
+                rows_ref[0, rows, same] = piece
+                rows_ref[1, rows, swap] = piece if part == 1 else -piece
+    row_tiles, column_tiles = row_count // tile, total // tile
+
+    def one(position, _):
+        row, column = position // column_tiles, position % column_tiles
+        row_at = pl.multiple_of(row * tile, tile)
+        column_at = pl.multiple_of(column * tile, tile)
+        row_global = where_ref[count] * row_tiles + row
+        columns = all_ref[:, :, pl.ds(column_at, tile)].reshape(depth, tile)
+
+        def product(kind):
+            left = rows_ref[kind, pl.ds(row_at, tile), :]
+            return jnp.dot(left, columns, preferred_element_type=jnp.float32)
+
+        @pl.when(row_global != column)
+        def _():
+            kind = jnp.where(column > row_global, 0, 1)
+            sums = product(kind) * scale
+            out_ref[0, pl.ds(row_at, tile), pl.ds(column_at, tile)] = sums.astype(out_ref.dtype)
+
+        @pl.when(row_global == column)
+        def _():
+            upper = lax.broadcasted_iota(jnp.int32, (tile, tile), 0) <= lax.broadcasted_iota(
+                jnp.int32, (tile, tile), 1
+            )
+            sums = jnp.where(upper, product(0), product(1)) * scale
+            out_ref[0, pl.ds(row_at, tile), pl.ds(column_at, tile)] = sums.astype(out_ref.dtype)
+
+        return 0
+
+    lax.fori_loop(0, row_tiles * column_tiles, one, 0)
+
+
+def correlate(pieces, where, held, first, channels, row_count, total, tile, scale):
+    spans, count = len(pieces), len(pieces[0])
+    chunk, _, frames, inputs = pieces[0][0].shape
+    depth = spans * 2 * frames
+    operands = [piece for row in pieces for piece in row]
+    in_specs = [pl.BlockSpec((1, 2, frames, inputs), lambda q, w: (q, 0, 0, 0)) for _ in operands]
+    aliases = {}
+    if held is not None:
+        aliases = {1 + len(operands): 0}
+        operands.append(held)
+        in_specs.append(pl.BlockSpec(memory_space=pl.ANY))
+    return pl.pallas_call(
+        functools.partial(correlate_kernel, count, spans, tile, scale),
+        out_shape=jax.ShapeDtypeStruct((channels, row_count, total), jnp.bfloat16),
+        grid_spec=pltpu.PrefetchScalarGridSpec(
+            num_scalar_prefetch=1,
+            grid=(chunk,),
+            in_specs=in_specs,
+            out_specs=pl.BlockSpec((1, row_count, total), lambda q, w: (first + q, 0, 0)),
+            scratch_shapes=[
+                pltpu.VMEM((2 * spans, frames, total), jnp.bfloat16),
+                pltpu.VMEM((2, row_count, depth), jnp.bfloat16),
+            ],
+        ),
+        input_output_aliases=aliases,
+        compiler_params=pltpu.CompilerParams(vmem_limit_bytes=VMEM),
+        cost_estimate=pl.CostEstimate(
+            flops=chunk * 3 * row_count * total * depth,
+            bytes_accessed=chunk * 2 * (total * depth + row_count * total),
+            transcendentals=0,
+        ),
+        name="correlate",
+    )(where, *operands)
+
+
+def chunk_sizes(channels):
+    sizes, left = [], channels
+    while left > 0:
+        size = max(1, min(channels // 4, left // 2))
+        sizes.append(size)
+        left -= size
+    return sizes
+
+
+def local_kernels(count, spans, voltages, gains):
+    coarse, inputs, samples = voltages.shape[1:]
+    frames = samples // FINE
+    halves = count // coarse
+    channels = FINE // halves
+    chunks = chunk_sizes(channels)
+    total = count * inputs
+    row_count = total // spans
+    tile = min(2 * LANES, row_count)
+    here = lax.axis_index("inp")
+    span_here = lax.axis_index("span")
+    tables = jnp.asarray(filter_rows(halves))
+    pair = 2 * GROUP * FINE
+    samples_step = 2 * pair if samples % (2 * pair) == 0 else pair
+    order = sorted(range(coarse), key=lambda m: -m)
+    own = here % halves
+    spectra = {}
+    for step in order:
+        where = jnp.stack([(here // halves) ^ step] + [own ^ half for half in range(halves)])
+        banks = filter_bank(
+            voltages, gains, tables, where.astype(jnp.int32), halves, chunks, samples_step
+        )
+        for half in range(halves):
+            spectra[step * halves + half] = banks[half]
+    places = jnp.stack([here ^ step for step in range(count)] + [span_here]).astype(jnp.int32)
+    held, first = None, 0
+    for index, size in enumerate(chunks):
+        mine = []
+        for step in range(count):
+            piece = spectra[step][index]
+            if step:
+                piece = lax.ppermute(piece, "inp", [(i, i ^ step) for i in range(count)])
+            mine.append(piece)
+        pieces = [mine]
+        for other in range(1, spans):
+            pieces.append(
+                [lax.ppermute(piece, "span", [(i, i ^ other) for i in range(spans)]) for piece in mine]
+            )
+        held = correlate(
+            pieces, places, held, first, channels, row_count, total, tile, 1.0 / (spans * frames)
+        )
+        first += size
+    return held
+
+
+def power_of_two(number):
+    return number > 0 and number & (number - 1) == 0
+
+
 def solution(mesh):
+    count, spans = mesh.shape["inp"], mesh.shape["span"]
+
+    def local(voltages, gains):
+        coarse, inputs, samples = voltages.shape[1:]
+        fits = (
+            power_of_two(count)
+            and power_of_two(spans)
+            and count % coarse == 0
+            and power_of_two(count // coarse)
+            and FINE % (count // coarse) == 0
+            and (FINE // (count // coarse)) % 8 == 0
+            and inputs == LANES
+            and samples % (2 * GROUP * FINE) == 0
+            and (count * inputs // spans) % (2 * LANES) == 0
+        )
+        if fits:
+            return local_kernels(count, spans, voltages, gains)
+        return local_plain(voltages, gains)
+
     placed = (P(None, "beam", "inp", "span"), P(None, "beam", "inp", None))
     return jax.shard_map(
         local,

time: 868 us -> 541 us (0.62)
  blocking collectives: 370 us -> 0 us
  local copies, waits for them, and re-layouts: 238 us -> 49.8 us
  waiting for transfers between devices: 50 us -> 224 us
  matrix products: 155 us -> 0 us
  starting transfers between devices: 0.01 us -> 142 us
  Pallas kernels: 0 us -> 119 us
  other arithmetic: 37.4 us -> 0.16 us
  between operations: 14.2 us -> 1.12 us
    all_to_all x1 -> x0, blocking collectives: 370 us -> none  [local(): lax.all_to_all(outgoing, 'inp', split_axis=1, concat_axis=2, tiled=True)]
    ppermute x0 -> x90, waiting for transfers between devices: none -> 224 us  [the longest x42 223 us: local_kernels(): piece = lax.ppermute(piece, 'inp', [(i, i ^ step) for i in range(count)])]
    dot_general x4 -> x0, matrix products: 155 us -> none  [the longest x1 44.4 us: local(): jnp.einsum('atcnmp,atpbk->bcknm', stacked, filter_high, preferred_element...]
    another operation x7 -> x1, local copies, waits for them, and re-layouts: 148 us -> 0.08 us  [local_kernels(): jnp.stack([here ^ step for step in range(count)] + [span_here])]
    ppermute x0 -> x90, starting transfers between devices: none -> 142 us  [the longest x42 130 us: local_kernels(): piece = lax.ppermute(piece, 'inp', [(i, i ^ step) for i in range(count)])]
    pallas_call x0 -> x10, Pallas kernels: none -> 119 us  [the longest x6 82.3 us: correlate(): pl.pallas_call(functools.partial(correlate_kernel, count, spans, tile, sc...]
    all_gather x1 -> x0, waiting for transfers between devices: 50 us -> none  [local(): frame_piece = lax.all_gather(turned, 'span', axis=3, tiled=True)]
    slice x2 -> x0, local copies, waits for them, and re-layouts: 32.5 us -> none  [the longest x1 32.5 us: local(): padded[..., tap_index * FINE:tap_index * FINE + samples]]
  transfers between devices with their start and end apart: 1 -> 90, of which waited for: 1 -> 14; matrix products, arithmetic and copies ran while one was open for 0% -> 0% of each run, Pallas kernels for 0% -> 19%
where the time goes in v1:
time: 541 us; the launch traced here: 536 us
  waiting for transfers between devices  224 us (41%)
  starting transfers between devices  142 us (26%)
  Pallas kernels  119 us (22%)
  local copies, waits for them, and re-layouts  49.8 us (9%)
    ppermute x42, waiting for transfers between devices, local_kernels(): piece = lax.ppermute(piece, 'inp', [(i, i ^ step) for i in range(count)])  223 us
    ppermute x42, starting transfers between devices, local_kernels(): piece = lax.ppermute(piece, 'inp', [(i, i ^ step) for i in range(count)])  130 us
    pallas_call x6, Pallas kernels, correlate(): pl.pallas_call(functools.partial(correlate_kernel, count, spans, tile, sc...  82.3 us
    unnamed x303, local copies, waits for them, and re-layouts  49.7 us
    pallas_call x4, Pallas kernels, filter_bank(): pl.pallas_call(functools.partial(filter_kernel, halves, chunks), out_shap...  36.3 us
    ppermute x48, starting transfers between devices, local_kernels(): lax.ppermute(piece, 'span', [(i, i ^ other) for i in range(spans)])  11.3 us
  transfers between devices with their start and end apart: 90, of which 14 were waited for; matrix products, arithmetic and copies ran while one was open for 0% of the time, Pallas kernels for 19%

profile of v1, /device:TPU:0, one launch (start us, length us, event | category | flops | bytes accessed | tf_op | source)
XLA Modules:
  0.0 535.7 jit_solution(15866200632374266438)
XLA Ops:
  0.0 1.1 copy.9.gain_ref
  1.2 1.1 copy-done
  2.3 9.2 %filter_bank.6 = (bf16[4,2,256,128]{3,2,1,0:T(8,128)(2,1)S(1)}, bf16[4,2,256,128]{3,2,1,0:T(8,128)(2,1)S(1)}, bf16[4,2,256,128]{3,2,1,0:T(8,128)(2,1)S(1)}, bf16...) custom-call(s32[3]{0:T(128)S(1)} %get-tuple-element.103.where_ref, ...), custom_call_target="tpu_custom_call" | custom-call | flops 3221225472 | bytes 16777216 | tf_op jit(solution)/shard_map/filter_bank/pallas_call | solution.py:204
  19.1 4.0 collective-permute-start.18
  23.2 1.3 collective-permute-start.19
  24.4 9.3 %filter_bank.7 = (bf16[4,2,256,128]{3,2,1,0:T(8,128)(2,1)}, bf16[4,2,256,128]{3,2,1,0:T(8,128)(2,1)S(1)}, bf16[4,2,256,128]{3,2,1,0:T(8,128)(2,1)S(1)}, bf16[2,2...) custom-call(s32[3]{0:T(128)S(1)} %get-tuple-element.104.where_ref, ...), custom_call_target="tpu_custom_call" | custom-call | flops 3221225472 | bytes 16777216 | tf_op jit(solution)/shard_map/filter_bank/pallas_call | solution.py:204
  35.3 0.9 copy-done.118
  39.7 3.6 collective-permute-start.20
  43.4 8.7 %filter_bank.4 = (bf16[4,2,256,128]{3,2,1,0:T(8,128)(2,1)S(1)}, bf16[4,2,256,128]{3,2,1,0:T(8,128)(2,1)S(1)}, bf16[4,2,256,128]{3,2,1,0:T(8,128)(2,1)S(1)}, bf16...) custom-call(s32[3]{0:T(128)S(1)} %get-tuple-element.101.where_ref, ...), custom_call_target="tpu_custom_call" | custom-call | flops 3221225472 | bytes 16777216 | tf_op jit(solution)/shard_map/filter_bank/pallas_call | solution.py:204
  53.6 1.7 collective-permute-start.15
  55.5 9.1 %filter_bank.5 = (bf16[4,2,256,128]{3,2,1,0:T(8,128)(2,1)S(1)}, bf16[4,2,256,128]{3,2,1,0:T(8,128)(2,1)S(1)}, bf16[4,2,256,128]{3,2,1,0:T(8,128)(2,1)S(1)}, bf16...) custom-call(s32[3]{0:T(128)S(1)} %get-tuple-element.102.where_ref, ...), custom_call_target="tpu_custom_call" | custom-call | flops 3221225472 | bytes 16777216 | tf_op jit(solution)/shard_map/filter_bank/pallas_call | solution.py:204
  64.7 1.8 collective-permute-start.17
  66.5 2.5 collective-permute-start.3
  69.0 1.7 collective-permute-start.4
  70.7 3.7 collective-permute-start.5
  74.4 1.5 collective-permute-start.6
  76.5 1.8 collective-permute-start.2
  78.3 6.5 %collective-permute-done.3.rest_4_ = bf16[1,2,256,128]{3,2,1,0:T(8,128)(2,1)S(1)} collective-permute-done((bf16[1,2,256,128]{3,2,1,0:T(8,128)(2,1)S(1)}, bf16[1,2,256,128]{3,2,1,0:T(8,128)(2,1)S(1)}, u32[]{:S(2)}, u32[]{:S(2)}) %collective-permute-start.3) | collective-permute-done | bytes 131104 | tf_op jit(solution)/shard_map/ppermute | solution.py:351
  84.8 1.4 collective-permute-start
  86.1 2.9 collective-permute-done.4.rest_5_
  89.1 10.1 %collective-permute-start.34 = (bf16[2,2,256,128]{3,2,1,0:T(8,128)(2,1)S(1)}, bf16[2,2,256,128]{3,2,1,0:T(8,128)(2,1)S(1)}, u32[]{:S(2)}, u32[]{:S(2)}) collective-permute-start(bf16[2,2,256,128]{3,2,1,0:T(8,128)(2,1)S(1)} %copy-done.128), channel_id=1, source_target_pairs={{0,10},{2,8},{4,14},{6,12},{8,2},{10,0},{12,6},{14,4},{1,11},{3,9}... | collective-permute-start | bytes 786440 | tf_op jit(solution)/shard_map/ppermute | solution.py:351
  99.8 11.5 %collective-permute-start.1 = (bf16[1,2,256,128]{3,2,1,0:T(8,128)(2,1)S(1)}, bf16[1,2,256,128]{3,2,1,0:T(8,128)(2,1)S(1)}, u32[]{:S(2)}, u32[]{:S(2)}) collective-permute-start(bf16[1,2,256,128]{3,2,1,0:T(8,128)(2,1)S(1)} %get-tuple-element.55), channel_id=1, source_target_pairs={{0,4},{2,6},{4,0},{6,2},{8,12},{10,14},{12,8},{14,10},{1,5},{3,7},... | collective-permute-start | bytes 393224 | tf_op jit(solution)/shard_map/ppermute | solution.py:351
  111.3 15.3 %collective-permute-done.1.rest_2_ = bf16[1,2,256,128]{3,2,1,0:T(8,128)(2,1)S(1)} collective-permute-done((bf16[1,2,256,128]{3,2,1,0:T(8,128)(2,1)S(1)}, bf16[1,2,256,128]{3,2,1,0:T(8,128)(2,1)S(1)}, u32[]{:S(2)}, u32[]{:S(2)}) %collective-permute-start.1) | collective-permute-done | bytes 131104 | tf_op jit(solution)/shard_map/ppermute | solution.py:351
  127.4 4.7 collective-permute-start.30
  132.2 1.5 collective-permute-start.32
  133.7 2.3 collective-permute-done.36.rest_7_
  136.0 7.6 %collective-permute-start.78 = (bf16[4,2,256,128]{3,2,1,0:T(8,128)(2,1)S(1)}, bf16[4,2,256,128]{3,2,1,0:T(8,128)(2,1)S(1)}, u32[]{:S(2)}, u32[]{:S(2)}) collective-permute-start(bf16[4,2,256,128]{3,2,1,0:T(8,128)(2,1)S(1)} %copy-done.125), channel_id=1, source_target_pairs={{0,8},{2,10},{4,12},{6,14},{8,0},{10,2},{12,4},{14,6},{1,9},{3,11}... | collective-permute-start | bytes 1572872 | tf_op jit(solution)/shard_map/ppermute | solution.py:351
  143.6 1.1 collective-permute-start.79
  149.7 3.2 collective-permute-start.80
  154.8 1.5 collective-permute-start.75
  156.4 42.9 %collective-permute-done.78.rest_4_ = bf16[4,2,256,128]{3,2,1,0:T(8,128)(2,1)S(1)} collective-permute-done((bf16[4,2,256,128]{3,2,1,0:T(8,128)(2,1)S(1)}, bf16[4,2,256,128]{3,2,1,0:T(8,128)(2,1)S(1)}, u32[]{:S(2)}, u32[]{:S(2)}) %collective-permute-start.78) | collective-permute-done | bytes 524320 | tf_op jit(solution)/shard_map/ppermute | solution.py:351
  199.3 11.9 %collective-permute-done.79.rest_5_ = bf16[4,2,256,128]{3,2,1,0:T(8,128)(2,1)S(1)} collective-permute-done((bf16[4,2,256,128]{3,2,1,0:T(8,128)(2,1)S(1)}, bf16[4,2,256,128]{3,2,1,0:T(8,128)(2,1)S(1)}, u32[]{:S(2)}, u32[]{:S(2)}) %collective-permute-start.79) | collective-permute-done | bytes 524320 | tf_op jit(solution)/shard_map/ppermute | solution.py:351
  211.3 24.8 %collective-permute-start.63 = (bf16[4,2,256,128]{3,2,1,0:T(8,128)(2,1)S(1)}, bf16[4,2,256,128]{3,2,1,0:T(8,128)(2,1)S(1)}, u32[]{:S(2)}, u32[]{:S(2)}) collective-permute-start(bf16[4,2,256,128]{3,2,1,0:T(8,128)(2,1)S(1)} %copy-done.117), channel_id=1, source_target_pairs={{0,8},{2,10},{4,12},{6,14},{8,0},{10,2},{12,4},{14,6},{1,9},{3,11}... | collective-permute-start | bytes 1572872 | tf_op jit(solution)/shard_map/ppermute | solution.py:351
  236.8 3.1 collective-permute-start.65
  239.9 1.0 collective-permute-start.66
  240.9 0.9 copy-done.38
  241.8 1.2 collective-permute-start.60
  243.0 50.9 %collective-permute-done.63.rest_4_ = bf16[4,2,256,128]{3,2,1,0:T(8,128)(2,1)S(1)} collective-permute-done((bf16[4,2,256,128]{3,2,1,0:T(8,128)(2,1)S(1)}, bf16[4,2,256,128]{3,2,1,0:T(8,128)(2,1)S(1)}, u32[]{:S(2)}, u32[]{:S(2)}) %collective-permute-start.63) | collective-permute-done | bytes 524320 | tf_op jit(solution)/shard_map/ppermute | solution.py:351
  293.8 11.9 %collective-permute-done.64.rest_5_ = bf16[4,2,256,128]{3,2,1,0:T(8,128)(2,1)S(1)} collective-permute-done((bf16[4,2,256,128]{3,2,1,0:T(8,128)(2,1)S(1)}, bf16[4,2,256,128]{3,2,1,0:T(8,128)(2,1)S(1)}, u32[]{:S(2)}, u32[]{:S(2)}) %collective-permute-start.64) | collective-permute-done | bytes 524320 | tf_op jit(solution)/shard_map/ppermute | solution.py:351
  305.8 26.6 %collective-permute-start.48 = (bf16[4,2,256,128]{3,2,1,0:T(8,128)(2,1)S(1)}, bf16[4,2,256,128]{3,2,1,0:T(8,128)(2,1)S(1)}, u32[]{:S(2)}, u32[]{:S(2)}) collective-permute-start(bf16[4,2,256,128]{3,2,1,0:T(8,128)(2,1)S(1)} %copy-done.111), channel_id=1, source_target_pairs={{0,8},{2,10},{4,12},{6,14},{8,0},{10,2},{12,4},{14,6},{1,9},{3,11}... | collective-permute-start | bytes 1572872 | tf_op jit(solution)/shard_map/ppermute | solution.py:351
  336.1 3.4 collective-permute-start.51
  340.3 1.1 collective-permute-start.45
  341.5 47.7 %collective-permute-done.48.rest_4_ = bf16[4,2,256,128]{3,2,1,0:T(8,128)(2,1)S(1)} collective-permute-done((bf16[4,2,256,128]{3,2,1,0:T(8,128)(2,1)S(1)}, bf16[4,2,256,128]{3,2,1,0:T(8,128)(2,1)S(1)}, u32[]{:S(2)}, u32[]{:S(2)}) %collective-permute-start.48) | collective-permute-done | bytes 524320 | tf_op jit(solution)/shard_map/ppermute | solution.py:351
  389.1 11.6 %collective-permute-done.49.rest_5_ = bf16[4,2,256,128]{3,2,1,0:T(8,128)(2,1)S(1)} collective-permute-done((bf16[4,2,256,128]{3,2,1,0:T(8,128)(2,1)S(1)}, bf16[4,2,256,128]{3,2,1,0:T(8,128)(2,1)S(1)}, u32[]{:S(2)}, u32[]{:S(2)}) %collective-permute-start.49) | collective-permute-done | bytes 524320 | tf_op jit(solution)/shard_map/ppermute | solution.py:351
  403.1 8.5 %collective-permute-done.46.rest_2_ = bf16[4,2,256,128]{3,2,1,0:T(8,128)(2,1)S(1)} collective-permute-done((bf16[4,2,256,128]{3,2,1,0:T(8,128)(2,1)S(1)}, bf16[4,2,256,128]{3,2,1,0:T(8,128)(2,1)S(1)}, u32[]{:S(2)}, u32[]{:S(2)}) %collective-permute-start.46) | collective-permute-done | bytes 524320 | tf_op jit(solution)/shard_map/ppermute | solution.py:351
  412.4 10.7 %collective-permute-done.47.rest_3_ = bf16[4,2,256,128]{3,2,1,0:T(8,128)(2,1)S(1)} collective-permute-done((bf16[4,2,256,128]{3,2,1,0:T(8,128)(2,1)S(1)}, bf16[4,2,256,128]{3,2,1,0:T(8,128)(2,1)S(1)}, u32[]{:S(2)}, u32[]{:S(2)}) %collective-permute-start.47) | collective-permute-done | bytes 524320 | tf_op jit(solution)/shard_map/ppermute | solution.py:351
  423.1 0.8 copy-done.28
  429.6 0.9 copy-done.36
  436.1 1.0 copy-done.25
  437.2 1.0 copy-done.27
  438.2 1.0 copy-done.29
  439.3 1.0 copy-done.31
  440.3 1.0 copy-done.33
  441.3 1.0 copy-done.35
  442.4 1.0 copy-done.37
  443.4 1.0 copy-done.39
  444.5 1.0 copy-done.41
  445.5 1.0 copy-done.43
  446.6 20.1 %correlate.6.rest_16_ = bf16[16,512,1024]{2,1,0:T(8,128)(2,1)} custom-call(s32[9]{0:T(128)S(1)} %stack.75.where_ref, bf16[4,2,256,128]{3,2,1,0:T(8,128)(2,1)S(1)} %copy-done.25, bf16[4,2,256,128]{3,2,1,0:T(8,128)(2,1)S(1)} %copy-done.35, bf16[4,2,256,128]{3,2,1,0:T(8,128)(2,1)S(1)} %copy-done.37, bf16[4,2,256,128]{3,2,1,0:T(8,128)(2,1)} %collective-permute-done.77.rest_3_, ...), custom_call_target="tpu_custom_call" | custom-call | flops 6442450944 | bytes 12582912 | tf_op jit(solution)/shard_map/correlate/pallas_call | solution.py:287
  468.3 20.3 %correlate.7.rest_16_ = bf16[16,512,1024]{2,1,0:T(8,128)(2,1)} custom-call(s32[9]{0:T(128)S(1)} %stack.75.where_ref, bf16[4,2,256,128]{3,2,1,0:T(8,128)(2,1)S(1)} %get-tuple-element.85.rest_0_, bf16[4,2,256,128]{3,2,1,0:T(8,128)(2,1)S(1)} %copy-done.7, bf16[4,2,256,128]{3,2,1,0:T(8,128)(2,1)S(1)} %copy-done.11, ...), custom_call_target="tpu_custom_call", output_to_operand_aliasing={{}: (17, {})} | custom-call | flops 6442450944 | bytes 12582912 | tf_op jit(solution)/shard_map/correlate/pallas_call | solution.py:287
  490.7 20.1 %correlate.8.rest_16_ = bf16[16,512,1024]{2,1,0:T(8,128)(2,1)} custom-call(s32[9]{0:T(128)S(1)} %stack.75.where_ref, bf16[4,2,256,128]{3,2,1,0:T(8,128)(2,1)S(1)} %get-tuple-element.77.rest_0_, bf16[4,2,256,128]{3,2,1,0:T(8,128)(2,1)S(1)} %copy-done.13, bf16[4,2,256,128]{3,2,1,0:T(8,128)(2,1)S(1)} %copy-done.17, ...), custom_call_target="tpu_custom_call", output_to_operand_aliasing={{}: (17, {})} | custom-call | flops 6442450944 | bytes 12582912 | tf_op jit(solution)/shard_map/correlate/pallas_call | solution.py:287
  512.4 10.2 %correlate.9.rest_16_ = bf16[16,512,1024]{2,1,0:T(8,128)(2,1)} custom-call(s32[9]{0:T(128)S(1)} %stack.75.where_ref, bf16[2,2,256,128]{3,2,1,0:T(8,128)(2,1)S(1)} %get-tuple-element.69.rest_0_, bf16[2,2,256,128]{3,2,1,0:T(8,128)(2,1)S(1)} %copy-done.53, bf16[2,2,256,128]{3,2,1,0:T(8,128)(2,1)S(1)} %copy-done.55, ...), custom_call_target="tpu_custom_call", output_to_operand_aliasing={{}: (17, {})} | custom-call | flops 3221225472 | bytes 6291456 | tf_op jit(solution)/shard_map/correlate/pallas_call | solution.py:287
  524.0 5.8 %correlate.10.rest_16_ = bf16[16,512,1024]{2,1,0:T(8,128)(2,1)} custom-call(s32[9]{0:T(128)S(1)} %stack.75.where_ref, bf16[1,2,256,128]{3,2,1,0:T(8,128)(2,1)S(1)} %copy-done.73, bf16[1,2,256,128]{3,2,1,0:T(8,128)(2,1)S(1)} %copy-done.75, bf16[1,2,256,128]{3,2,1,0:T(8,128)(2,1)S(1)} %copy-done.79, ...), custom_call_target="tpu_custom_call", output_to_operand_aliasing={{}: (17, {})} | custom-call | flops 1610612736 | bytes 3145728 | tf_op jit(solution)/shard_map/correlate/pallas_call | solution.py:287
  529.8 5.8 %correlate.11 = bf16[16,512,1024]{2,1,0:T(8,128)(2,1)} custom-call(s32[9]{0:T(128)S(1)} %stack.75.where_ref, bf16[1,2,256,128]{3,2,1,0:T(8,128)(2,1)S(1)} %copy-done.67, bf16[1,2,256,128]{3,2,1,0:T(8,128)(2,1)S(1)} %copy-done.93, bf16[1,2,256,128]{3,2,1,0:T(8,128)(2,1)S(1)} %copy-done.95, ...), custom_call_target="tpu_custom_call", output_to_operand_aliasing={{}: (17, {})} | custom-call | flops 1610612736 | bytes 3145728 | tf_op jit(solution)/shard_map/correlate/pallas_call | solution.py:287
  (432 shorter events, 49.6 us)
Async XLA Ops:
  19.1 45.5 %collective-permute-start.18 = (bf16[1,2,256,128]{3,2,1,0:T(8,128)(2,1)}, bf16[1,2,256,128]{3,2,1,0:T(8,128)(2,1)S(1)}, u32[]{:S(2)}, u32[]{:S(2)}) collective-permute-start(bf16[1,2,256,128]{3,2,1,0:T(8,128)(2,1)} %get-tuple-element.65), channel_id=1, source_target_pairs={{0,8},{2,10},{4,12},{6,14},{8,0},{10,2},{12,4},{14,6},{1,9},{3,11}... | collective-permute-start | bytes 393224 | tf_op jit(solution)/shard_map/ppermute | solution.py:351
  23.2 41.5 %collective-permute-start.19 = (bf16[1,2,256,128]{3,2,1,0:T(8,128)(2,1)}, bf16[1,2,256,128]{3,2,1,0:T(8,128)(2,1)S(1)}, u32[]{:S(2)}, u32[]{:S(2)}) collective-permute-start(bf16[1,2,256,128]{3,2,1,0:T(8,128)(2,1)} %get-tuple-element.66), channel_id=1, source_target_pairs={{0,10},{2,8},{4,14},{6,12},{8,2},{10,0},{12,6},{14,4},{1,11},{3,9}... | collective-permute-start | bytes 393224 | tf_op jit(solution)/shard_map/ppermute | solution.py:351
  39.7 26.8 %collective-permute-start.20 = (bf16[1,2,256,128]{3,2,1,0:T(8,128)(2,1)}, bf16[1,2,256,128]{3,2,1,0:T(8,128)(2,1)S(1)}, u32[]{:S(2)}, u32[]{:S(2)}) collective-permute-start(bf16[1,2,256,128]{3,2,1,0:T(8,128)(2,1)} %get-tuple-element.67), channel_id=1, source_target_pairs={{0,12},{2,14},{4,8},{6,10},{8,4},{10,6},{12,0},{14,2},{1,13},{3,15... | collective-permute-start | bytes 393224 | tf_op jit(solution)/shard_map/ppermute | solution.py:351
  43.3 23.2 %collective-permute-start.21 = (bf16[1,2,256,128]{3,2,1,0:T(8,128)(2,1)}, bf16[1,2,256,128]{3,2,1,0:T(8,128)(2,1)S(1)}, u32[]{:S(2)}, u32[]{:S(2)}) collective-permute-start(bf16[1,2,256,128]{3,2,1,0:T(8,128)(2,1)} %get-tuple-element.68), channel_id=1, source_target_pairs={{0,14},{2,12},{4,10},{6,8},{8,6},{10,4},{12,2},{14,0},{1,15},{3,13... | collective-permute-start | bytes 393224 | tf_op jit(solution)/shard_map/ppermute | solution.py:351
  53.6 15.4 %collective-permute-start.15 = (bf16[1,2,256,128]{3,2,1,0:T(8,128)(2,1)S(1)}, bf16[1,2,256,128]{3,2,1,0:T(8,128)(2,1)S(1)}, u32[]{:S(2)}, u32[]{:S(2)}) collective-permute-start(bf16[1,2,256,128]{3,2,1,0:T(8,128)(2,1)S(1)} %get-tuple-element.62), channel_id=1, source_target_pairs={{0,2},{2,0},{4,6},{6,4},{8,10},{10,8},{12,14},{14,12},{1,3},{3,1},... | collective-permute-start | bytes 393224 | tf_op jit(solution)/shard_map/ppermute | solution.py:351
  66.5 18.2 %collective-permute-start.3 = (bf16[1,2,256,128]{3,2,1,0:T(8,128)(2,1)S(1)}, bf16[1,2,256,128]{3,2,1,0:T(8,128)(2,1)S(1)}, u32[]{:S(2)}, u32[]{:S(2)}) collective-permute-start(bf16[1,2,256,128]{3,2,1,0:T(8,128)(2,1)S(1)} %copy-done.138), channel_id=1, source_target_pairs={{0,8},{2,10},{4,12},{6,14},{8,0},{10,2},{12,4},{14,6},{1,9},{3,11}... | collective-permute-start | bytes 393224 | tf_op jit(solution)/shard_map/ppermute | solution.py:351
  69.0 20.0 %collective-permute-start.4 = (bf16[1,2,256,128]{3,2,1,0:T(8,128)(2,1)S(1)}, bf16[1,2,256,128]{3,2,1,0:T(8,128)(2,1)S(1)}, u32[]{:S(2)}, u32[]{:S(2)}) collective-permute-start(bf16[1,2,256,128]{3,2,1,0:T(8,128)(2,1)S(1)} %copy-done.136), channel_id=1, source_target_pairs={{0,10},{2,8},{4,14},{6,12},{8,2},{10,0},{12,6},{14,4},{1,11},{3,9}... | collective-permute-start | bytes 393224 | tf_op jit(solution)/shard_map/ppermute | solution.py:351
  70.7 18.4 %collective-permute-start.5 = (bf16[1,2,256,128]{3,2,1,0:T(8,128)(2,1)S(1)}, bf16[1,2,256,128]{3,2,1,0:T(8,128)(2,1)S(1)}, u32[]{:S(2)}, u32[]{:S(2)}) collective-permute-start(bf16[1,2,256,128]{3,2,1,0:T(8,128)(2,1)S(1)} %copy-done.142), channel_id=1, source_target_pairs={{0,12},{2,14},{4,8},{6,10},{8,4},{10,6},{12,0},{14,2},{1,13},{3,15... | collective-permute-start | bytes 393224 | tf_op jit(solution)/shard_map/ppermute | solution.py:351
  74.4 24.9 %collective-permute-start.6 = (bf16[1,2,256,128]{3,2,1,0:T(8,128)(2,1)S(1)}, bf16[1,2,256,128]{3,2,1,0:T(8,128)(2,1)S(1)}, u32[]{:S(2)}, u32[]{:S(2)}) collective-permute-start(bf16[1,2,256,128]{3,2,1,0:T(8,128)(2,1)S(1)} %copy-done.140), channel_id=1, source_target_pairs={{0,14},{2,12},{4,10},{6,8},{8,6},{10,4},{12,2},{14,0},{1,15},{3,13... | collective-permute-start | bytes 393224 | tf_op jit(solution)/shard_map/ppermute | solution.py:351
  76.5 23.2 %collective-permute-start.2 = (bf16[1,2,256,128]{3,2,1,0:T(8,128)(2,1)S(1)}, bf16[1,2,256,128]{3,2,1,0:T(8,128)(2,1)S(1)}, u32[]{:S(2)}, u32[]{:S(2)}) collective-permute-start(bf16[1,2,256,128]{3,2,1,0:T(8,128)(2,1)S(1)} %get-tuple-element.56), channel_id=1, source_target_pairs={{0,6},{2,4},{4,2},{6,0},{8,14},{10,12},{12,10},{14,8},{1,7},{3,5},... | collective-permute-start | bytes 393224 | tf_op jit(solution)/shard_map/ppermute | solution.py:351
  84.8 26.5 %collective-permute-start = (bf16[1,2,256,128]{3,2,1,0:T(8,128)(2,1)S(1)}, bf16[1,2,256,128]{3,2,1,0:T(8,128)(2,1)S(1)}, u32[]{:S(2)}, u32[]{:S(2)}) collective-permute-start(bf16[1,2,256,128]{3,2,1,0:T(8,128)(2,1)S(1)} %get-tuple-element.54), channel_id=1, source_target_pairs={{0,2},{2,0},{4,6},{6,4},{8,10},{10,8},{12,14},{14,12},{1,3},{3,1},... | collective-permute-start | bytes 393224 | tf_op jit(solution)/shard_map/ppermute | solution.py:351
  89.1 43.0 %collective-permute-start.33 = (bf16[2,2,256,128]{3,2,1,0:T(8,128)(2,1)S(1)}, bf16[2,2,256,128]{3,2,1,0:T(8,128)(2,1)S(1)}, u32[]{:S(2)}, u32[]{:S(2)}) collective-permute-start(bf16[2,2,256,128]{3,2,1,0:T(8,128)(2,1)S(1)} %copy-done.130), channel_id=1, source_target_pairs={{0,8},{2,10},{4,12},{6,14},{8,0},{10,2},{12,4},{14,6},{1,9},{3,11}... | collective-permute-start | bytes 786440 | tf_op jit(solution)/shard_map/ppermute | solution.py:351
  89.1 43.1 %collective-permute-start.34 = (bf16[2,2,256,128]{3,2,1,0:T(8,128)(2,1)S(1)}, bf16[2,2,256,128]{3,2,1,0:T(8,128)(2,1)S(1)}, u32[]{:S(2)}, u32[]{:S(2)}) collective-permute-start(bf16[2,2,256,128]{3,2,1,0:T(8,128)(2,1)S(1)} %copy-done.128), channel_id=1, source_target_pairs={{0,10},{2,8},{4,14},{6,12},{8,2},{10,0},{12,6},{14,4},{1,11},{3,9}... | collective-permute-start | bytes 786440 | tf_op jit(solution)/shard_map/ppermute | solution.py:351
  99.3 34.4 %collective-permute-start.35 = (bf16[2,2,256,128]{3,2,1,0:T(8,128)(2,1)S(1)}, bf16[2,2,256,128]{3,2,1,0:T(8,128)(2,1)S(1)}, u32[]{:S(2)}, u32[]{:S(2)}) collective-permute-start(bf16[2,2,256,128]{3,2,1,0:T(8,128)(2,1)S(1)} %copy-done.134), channel_id=1, source_target_pairs={{0,12},{2,14},{4,8},{6,10},{8,4},{10,6},{12,0},{14,2},{1,13},{3,15... | collective-permute-start | bytes 786440 | tf_op jit(solution)/shard_map/ppermute | solution.py:351
  99.8 26.9 %collective-permute-start.1 = (bf16[1,2,256,128]{3,2,1,0:T(8,128)(2,1)S(1)}, bf16[1,2,256,128]{3,2,1,0:T(8,128)(2,1)S(1)}, u32[]{:S(2)}, u32[]{:S(2)}) collective-permute-start(bf16[1,2,256,128]{3,2,1,0:T(8,128)(2,1)S(1)} %get-tuple-element.55), channel_id=1, source_target_pairs={{0,4},{2,6},{4,0},{6,2},{8,12},{10,14},{12,8},{14,10},{1,5},{3,7},... | collective-permute-start | bytes 393224 | tf_op jit(solution)/shard_map/ppermute | solution.py:351
  111.3 15.5 %collective-permute-start.7 = (bf16[1,2,256,128]{3,2,1,0:T(8,128)(2,1)S(1)}, bf16[1,2,256,128]{3,2,1,0:T(8,128)(2,1)S(1)}, u32[]{:S(2)}, u32[]{:S(2)}) collective-permute-start(bf16[1,2,256,128]{3,2,1,0:T(8,128)(2,1)S(1)} %get-tuple-element.53.rest_0_), channel_id=1, source_target_pairs={{0,1},{1,0},{2,3},{3,2},{4,5},{5,4},{6,7},{7,6},{8,9},{9,8},{10,11... | collective-permute-start | bytes 393224 | tf_op jit(solution)/shard_map/ppermute | solution.py:356
  127.4 16.2 %collective-permute-start.30 = (bf16[2,2,256,128]{3,2,1,0:T(8,128)(2,1)S(1)}, bf16[2,2,256,128]{3,2,1,0:T(8,128)(2,1)S(1)}, u32[]{:S(2)}, u32[]{:S(2)}) collective-permute-start(bf16[2,2,256,128]{3,2,1,0:T(8,128)(2,1)S(1)} %get-tuple-element.70), channel_id=1, source_target_pairs={{0,2},{2,0},{4,6},{6,4},{8,10},{10,8},{12,14},{14,12},{1,3},{3,1},... | collective-permute-start | bytes 786440 | tf_op jit(solution)/shard_map/ppermute | solution.py:351
  132.1 12.6 %collective-permute-start.31 = (bf16[2,2,256,128]{3,2,1,0:T(8,128)(2,1)S(1)}, bf16[2,2,256,128]{3,2,1,0:T(8,128)(2,1)S(1)}, u32[]{:S(2)}, u32[]{:S(2)}) collective-permute-start(bf16[2,2,256,128]{3,2,1,0:T(8,128)(2,1)S(1)} %get-tuple-element.71), channel_id=1, source_target_pairs={{0,4},{2,6},{4,0},{6,2},{8,12},{10,14},{12,8},{14,10},{1,5},{3,7},... | collective-permute-start | bytes 786440 | tf_op jit(solution)/shard_map/ppermute | solution.py:351
  132.2 12.5 %collective-permute-start.32 = (bf16[2,2,256,128]{3,2,1,0:T(8,128)(2,1)S(1)}, bf16[2,2,256,128]{3,2,1,0:T(8,128)(2,1)S(1)}, u32[]{:S(2)}, u32[]{:S(2)}) collective-permute-start(bf16[2,2,256,128]{3,2,1,0:T(8,128)(2,1)S(1)} %get-tuple-element.72), channel_id=1, source_target_pairs={{0,6},{2,4},{4,2},{6,0},{8,14},{10,12},{12,10},{14,8},{1,7},{3,5},... | collective-permute-start | bytes 786440 | tf_op jit(solution)/shard_map/ppermute | solution.py:351
  133.7 12.2 %collective-permute-start.37 = (bf16[2,2,256,128]{3,2,1,0:T(8,128)(2,1)S(1)}, bf16[2,2,256,128]{3,2,1,0:T(8,128)(2,1)S(1)}, u32[]{:S(2)}, u32[]{:S(2)}) collective-permute-start(bf16[2,2,256,128]{3,2,1,0:T(8,128)(2,1)S(1)} %get-tuple-element.69.rest_0_), channel_id=1, source_target_pairs={{0,1},{1,0},{2,3},{3,2},{4,5},{5,4},{6,7},{7,6},{8,9},{9,8},{10,11... | collective-permute-start | bytes 786440 | tf_op jit(solution)/shard_map/ppermute | solution.py:356
  136.0 63.3 %collective-permute-start.78 = (bf16[4,2,256,128]{3,2,1,0:T(8,128)(2,1)S(1)}, bf16[4,2,256,128]{3,2,1,0:T(8,128)(2,1)S(1)}, u32[]{:S(2)}, u32[]{:S(2)}) collective-permute-start(bf16[4,2,256,128]{3,2,1,0:T(8,128)(2,1)S(1)} %copy-done.125), channel_id=1, source_target_pairs={{0,8},{2,10},{4,12},{6,14},{8,0},{10,2},{12,4},{14,6},{1,9},{3,11}... | collective-permute-start | bytes 1572872 | tf_op jit(solution)/shard_map/ppermute | solution.py:351
  143.6 67.6 %collective-permute-start.79 = (bf16[4,2,256,128]{3,2,1,0:T(8,128)(2,1)S(1)}, bf16[4,2,256,128]{3,2,1,0:T(8,128)(2,1)S(1)}, u32[]{:S(2)}, u32[]{:S(2)}) collective-permute-start(bf16[4,2,256,128]{3,2,1,0:T(8,128)(2,1)S(1)} %copy-done.123), channel_id=1, source_target_pairs={{0,10},{2,8},{4,14},{6,12},{8,2},{10,0},{12,6},{14,4},{1,11},{3,9}... | collective-permute-start | bytes 1572872 | tf_op jit(solution)/shard_map/ppermute | solution.py:351
  149.7 61.4 %collective-permute-start.80 = (bf16[4,2,256,128]{3,2,1,0:T(8,128)(2,1)}, bf16[4,2,256,128]{3,2,1,0:T(8,128)(2,1)S(1)}, u32[]{:S(2)}, u32[]{:S(2)}) collective-permute-start(bf16[4,2,256,128]{3,2,1,0:T(8,128)(2,1)} %get-tuple-element.99), channel_id=1, source_target_pairs={{0,12},{2,14},{4,8},{6,10},{8,4},{10,6},{12,0},{14,2},{1,13},{3,15... | collective-permute-start | bytes 1572872 | tf_op jit(solution)/shard_map/ppermute | solution.py:351
  153.6 57.7 %collective-permute-start.81 = (bf16[4,2,256,128]{3,2,1,0:T(8,128)(2,1)}, bf16[4,2,256,128]{3,2,1,0:T(8,128)(2,1)S(1)}, u32[]{:S(2)}, u32[]{:S(2)}) collective-permute-start(bf16[4,2,256,128]{3,2,1,0:T(8,128)(2,1)} %get-tuple-element.100), channel_id=1, source_target_pairs={{0,14},{2,12},{4,10},{6,8},{8,6},{10,4},{12,2},{14,0},{1,15},{3,13... | collective-permute-start | bytes 1572872 | tf_op jit(solution)/shard_map/ppermute | solution.py:351
  154.8 81.3 %collective-permute-start.75 = (bf16[4,2,256,128]{3,2,1,0:T(8,128)(2,1)}, bf16[4,2,256,128]{3,2,1,0:T(8,128)(2,1)S(1)}, u32[]{:S(2)}, u32[]{:S(2)}) collective-permute-start(bf16[4,2,256,128]{3,2,1,0:T(8,128)(2,1)} %copy-done.126), channel_id=1, source_target_pairs={{0,2},{2,0},{4,6},{6,4},{8,10},{10,8},{12,14},{14,12},{1,3},{3,1},... | collective-permute-start | bytes 1572872 | tf_op jit(solution)/shard_map/ppermute | solution.py:351
  199.3 37.5 %collective-permute-start.76 = (bf16[4,2,256,128]{3,2,1,0:T(8,128)(2,1)S(1)}, bf16[4,2,256,128]{3,2,1,0:T(8,128)(2,1)S(1)}, u32[]{:S(2)}, u32[]{:S(2)}) collective-permute-start(bf16[4,2,256,128]{3,2,1,0:T(8,128)(2,1)S(1)} %get-tuple-element.95), channel_id=1, source_target_pairs={{0,4},{2,6},{4,0},{6,2},{8,12},{10,14},{12,8},{14,10},{1,5},{3,7},... | collective-permute-start | bytes 1572872 | tf_op jit(solution)/shard_map/ppermute | solution.py:351
  211.2 28.7 %collective-permute-start.77 = (bf16[4,2,256,128]{3,2,1,0:T(8,128)(2,1)S(1)}, bf16[4,2,256,128]{3,2,1,0:T(8,128)(2,1)}, u32[]{:S(2)}, u32[]{:S(2)}) collective-permute-start(bf16[4,2,256,128]{3,2,1,0:T(8,128)(2,1)S(1)} %get-tuple-element.96), channel_id=1, source_target_pairs={{0,6},{2,4},{4,2},{6,0},{8,14},{10,12},{12,10},{14,8},{1,7},{3,5},... | collective-permute-start | bytes 1572872 | tf_op jit(solution)/shard_map/ppermute | solution.py:351
  211.2 29.8 %collective-permute-start.82 = (bf16[4,2,256,128]{3,2,1,0:T(8,128)(2,1)S(1)}, bf16[4,2,256,128]{3,2,1,0:T(8,128)(2,1)S(1)}, u32[]{:S(2)}, u32[]{:S(2)}) collective-permute-start(bf16[4,2,256,128]{3,2,1,0:T(8,128)(2,1)S(1)} %get-tuple-element.93.rest_0_), channel_id=1, source_target_pairs={{0,1},{1,0},{2,3},{3,2},{4,5},{5,4},{6,7},{7,6},{8,9},{9,8},{10,11... | collective-permute-start | bytes 1572872 | tf_op jit(solution)/shard_map/ppermute | solution.py:356
  211.3 82.5 %collective-permute-start.63 = (bf16[4,2,256,128]{3,2,1,0:T(8,128)(2,1)S(1)}, bf16[4,2,256,128]{3,2,1,0:T(8,128)(2,1)S(1)}, u32[]{:S(2)}, u32[]{:S(2)}) collective-permute-start(bf16[4,2,256,128]{3,2,1,0:T(8,128)(2,1)S(1)} %copy-done.117), channel_id=1, source_target_pairs={{0,8},{2,10},{4,12},{6,14},{8,0},{10,2},{12,4},{14,6},{1,9},{3,11}... | collective-permute-start | bytes 1572872 | tf_op jit(solution)/shard_map/ppermute | solution.py:351
  236.1 69.6 %collective-permute-start.64 = (bf16[4,2,256,128]{3,2,1,0:T(8,128)(2,1)S(1)}, bf16[4,2,256,128]{3,2,1,0:T(8,128)(2,1)S(1)}, u32[]{:S(2)}, u32[]{:S(2)}) collective-permute-start(bf16[4,2,256,128]{3,2,1,0:T(8,128)(2,1)S(1)} %copy-done.115), channel_id=1, source_target_pairs={{0,10},{2,8},{4,14},{6,12},{8,2},{10,0},{12,6},{14,4},{1,11},{3,9}... | collective-permute-start | bytes 1572872 | tf_op jit(solution)/shard_map/ppermute | solution.py:351
  236.8 68.9 %collective-permute-start.65 = (bf16[4,2,256,128]{3,2,1,0:T(8,128)(2,1)}, bf16[4,2,256,128]{3,2,1,0:T(8,128)(2,1)S(1)}, u32[]{:S(2)}, u32[]{:S(2)}) collective-permute-start(bf16[4,2,256,128]{3,2,1,0:T(8,128)(2,1)} %copy-done.120), channel_id=1, source_target_pairs={{0,12},{2,14},{4,8},{6,10},{8,4},{10,6},{12,0},{14,2},{1,13},{3,15... | collective-permute-start | bytes 1572872 | tf_op jit(solution)/shard_map/ppermute | solution.py:351
  239.9 65.8 %collective-permute-start.66 = (bf16[4,2,256,128]{3,2,1,0:T(8,128)(2,1)S(1)}, bf16[4,2,256,128]{3,2,1,0:T(8,128)(2,1)}, u32[]{:S(2)}, u32[]{:S(2)}) collective-permute-start(bf16[4,2,256,128]{3,2,1,0:T(8,128)(2,1)S(1)} %copy-done.119), channel_id=1, source_target_pairs={{0,14},{2,12},{4,10},{6,8},{8,6},{10,4},{12,2},{14,0},{1,15},{3,13... | collective-permute-start | bytes 1572872 | tf_op jit(solution)/shard_map/ppermute | solution.py:351
  241.8 90.5 %collective-permute-start.60 = (bf16[4,2,256,128]{3,2,1,0:T(8,128)(2,1)}, bf16[4,2,256,128]{3,2,1,0:T(8,128)(2,1)S(1)}, u32[]{:S(2)}, u32[]{:S(2)}) collective-permute-start(bf16[4,2,256,128]{3,2,1,0:T(8,128)(2,1)} %copy-done.121), channel_id=1, source_target_pairs={{0,2},{2,0},{4,6},{6,4},{8,10},{10,8},{12,14},{14,12},{1,3},{3,1},... | collective-permute-start | bytes 1572872 | tf_op jit(solution)/shard_map/ppermute | solution.py:351
  293.8 39.9 %collective-permute-start.61 = (bf16[4,2,256,128]{3,2,1,0:T(8,128)(2,1)S(1)}, bf16[4,2,256,128]{3,2,1,0:T(8,128)(2,1)S(1)}, u32[]{:S(2)}, u32[]{:S(2)}) collective-permute-start(bf16[4,2,256,128]{3,2,1,0:T(8,128)(2,1)S(1)} %get-tuple-element.87), channel_id=1, source_target_pairs={{0,4},{2,6},{4,0},{6,2},{8,12},{10,14},{12,8},{14,10},{1,5},{3,7},... | collective-permute-start | bytes 1572872 | tf_op jit(solution)/shard_map/ppermute | solution.py:351
  305.7 29.5 %collective-permute-start.62 = (bf16[4,2,256,128]{3,2,1,0:T(8,128)(2,1)S(1)}, bf16[4,2,256,128]{3,2,1,0:T(8,128)(2,1)S(1)}, u32[]{:S(2)}, u32[]{:S(2)}) collective-permute-start(bf16[4,2,256,128]{3,2,1,0:T(8,128)(2,1)S(1)} %get-tuple-element.88), channel_id=1, source_target_pairs={{0,6},{2,4},{4,2},{6,0},{8,14},{10,12},{12,10},{14,8},{1,7},{3,5},... | collective-permute-start | bytes 1572872 | tf_op jit(solution)/shard_map/ppermute | solution.py:351
  305.7 33.8 %collective-permute-start.67 = (bf16[4,2,256,128]{3,2,1,0:T(8,128)(2,1)S(1)}, bf16[4,2,256,128]{3,2,1,0:T(8,128)(2,1)S(1)}, u32[]{:S(2)}, u32[]{:S(2)}) collective-permute-start(bf16[4,2,256,128]{3,2,1,0:T(8,128)(2,1)S(1)} %get-tuple-element.85.rest_0_), channel_id=1, source_target_pairs={{0,1},{1,0},{2,3},{3,2},{4,5},{5,4},{6,7},{7,6},{8,9},{9,8},{10,11... | collective-permute-start | bytes 1572872 | tf_op jit(solution)/shard_map/ppermute | solution.py:356
  305.8 83.4 %collective-permute-start.48 = (bf16[4,2,256,128]{3,2,1,0:T(8,128)(2,1)S(1)}, bf16[4,2,256,128]{3,2,1,0:T(8,128)(2,1)S(1)}, u32[]{:S(2)}, u32[]{:S(2)}) collective-permute-start(bf16[4,2,256,128]{3,2,1,0:T(8,128)(2,1)S(1)} %copy-done.111), channel_id=1, source_target_pairs={{0,8},{2,10},{4,12},{6,14},{8,0},{10,2},{12,4},{14,6},{1,9},{3,11}... | collective-permute-start | bytes 1572872 | tf_op jit(solution)/shard_map/ppermute | solution.py:351
  333.1 67.6 %collective-permute-start.49 = (bf16[4,2,256,128]{3,2,1,0:T(8,128)(2,1)S(1)}, bf16[4,2,256,128]{3,2,1,0:T(8,128)(2,1)S(1)}, u32[]{:S(2)}, u32[]{:S(2)}) collective-permute-start(bf16[4,2,256,128]{3,2,1,0:T(8,128)(2,1)S(1)} %copy-done.107), channel_id=1, source_target_pairs={{0,10},{2,8},{4,14},{6,12},{8,2},{10,0},{12,6},{14,4},{1,11},{3,9}... | collective-permute-start | bytes 1572872 | tf_op jit(solution)/shard_map/ppermute | solution.py:351
  334.5 66.2 %collective-permute-start.50 = (bf16[4,2,256,128]{3,2,1,0:T(8,128)(2,1)S(1)}, bf16[4,2,256,128]{3,2,1,0:T(8,128)(2,1)S(1)}, u32[]{:S(2)}, u32[]{:S(2)}) collective-permute-start(bf16[4,2,256,128]{3,2,1,0:T(8,128)(2,1)S(1)} %copy-done.113), channel_id=1, source_target_pairs={{0,12},{2,14},{4,8},{6,10},{8,4},{10,6},{12,0},{14,2},{1,13},{3,15... | collective-permute-start | bytes 1572872 | tf_op jit(solution)/shard_map/ppermute | solution.py:351
  336.1 64.8 %collective-permute-start.51 = (bf16[4,2,256,128]{3,2,1,0:T(8,128)(2,1)S(1)}, bf16[4,2,256,128]{3,2,1,0:T(8,128)(2,1)S(1)}, u32[]{:S(2)}, u32[]{:S(2)}) collective-permute-start(bf16[4,2,256,128]{3,2,1,0:T(8,128)(2,1)S(1)} %copy-done.109), channel_id=1, source_target_pairs={{0,14},{2,12},{4,10},{6,8},{8,6},{10,4},{12,2},{14,0},{1,15},{3,13... | collective-permute-start | bytes 1572872 | tf_op jit(solution)/shard_map/ppermute | solution.py:351
  340.3 61.8 %collective-permute-start.45 = (bf16[4,2,256,128]{3,2,1,0:T(8,128)(2,1)S(1)}, bf16[4,2,256,128]{3,2,1,0:T(8,128)(2,1)S(1)}, u32[]{:S(2)}, u32[]{:S(2)}) collective-permute-start(bf16[4,2,256,128]{3,2,1,0:T(8,128)(2,1)S(1)} %get-tuple-element.78), channel_id=1, source_target_pairs={{0,2},{2,0},{4,6},{6,4},{8,10},{10,8},{12,14},{14,12},{1,3},{3,1},... | collective-permute-start | bytes 1572872 | tf_op jit(solution)/shard_map/ppermute | solution.py:351
  389.1 22.5 %collective-permute-start.46 = (bf16[4,2,256,128]{3,2,1,0:T(8,128)(2,1)S(1)}, bf16[4,2,256,128]{3,2,1,0:T(8,128)(2,1)S(1)}, u32[]{:S(2)}, u32[]{:S(2)}) collective-permute-start(bf16[4,2,256,128]{3,2,1,0:T(8,128)(2,1)S(1)} %get-tuple-element.79), channel_id=1, source_target_pairs={{0,4},{2,6},{4,0},{6,2},{8,12},{10,14},{12,8},{14,10},{1,5},{3,7},... | collective-permute-start | bytes 1572872 | tf_op jit(solution)/shard_map/ppermute | solution.py:351
  400.8 22.4 %collective-permute-start.47 = (bf16[4,2,256,128]{3,2,1,0:T(8,128)(2,1)S(1)}, bf16[4,2,256,128]{3,2,1,0:T(8,128)(2,1)S(1)}, u32[]{:S(2)}, u32[]{:S(2)}) collective-permute-start(bf16[4,2,256,128]{3,2,1,0:T(8,128)(2,1)S(1)} %get-tuple-element.80), channel_id=1, source_target_pairs={{0,6},{2,4},{4,2},{6,0},{8,14},{10,12},{12,10},{14,8},{1,7},{3,5},... | collective-permute-start | bytes 1572872 | tf_op jit(solution)/shard_map/ppermute | solution.py:351
  400.8 23.2 %collective-permute-start.52 = (bf16[4,2,256,128]{3,2,1,0:T(8,128)(2,1)S(1)}, bf16[4,2,256,128]{3,2,1,0:T(8,128)(2,1)S(1)}, u32[]{:S(2)}, u32[]{:S(2)}) collective-permute-start(bf16[4,2,256,128]{3,2,1,0:T(8,128)(2,1)S(1)} %get-tuple-element.77.rest_0_), channel_id=1, source_target_pairs={{0,1},{1,0},{2,3},{3,2},{4,5},{5,4},{6,7},{7,6},{8,9},{9,8},{10,11... | collective-permute-start | bytes 1572872 | tf_op jit(solution)/shard_map/ppermute | solution.py:356
  400.9 28.7 %collective-permute-start.86 = (bf16[4,2,256,128]{3,2,1,0:T(8,128)(2,1)S(1)}, bf16[4,2,256,128]{3,2,1,0:T(8,128)(2,1)S(1)}, u32[]{:S(2)}, u32[]{:S(2)}) collective-permute-start(bf16[4,2,256,128]{3,2,1,0:T(8,128)(2,1)S(1)} %collective-permute-done.78.rest_4_), channel_id=1, source_target_pairs={{0,1},{1,0},{2,3},{3,2},{4,5},{5,4},{6,7},{7,6},{8,9},{9,8},{10,11... | collective-permute-start | bytes 1572872 | tf_op jit(solution)/shard_map/ppermute | solution.py:356
  402.2 23.9 %collective-permute-start.41 = (bf16[2,2,256,128]{3,2,1,0:T(8,128)(2,1)S(1)}, bf16[2,2,256,128]{3,2,1,0:T(8,128)(2,1)S(1)}, u32[]{:S(2)}, u32[]{:S(2)}) collective-permute-start(bf16[2,2,256,128]{3,2,1,0:T(8,128)(2,1)S(1)} %collective-permute-done.33.rest_4_), channel_id=1, source_target_pairs={{0,1},{1,0},{2,3},{3,2},{4,5},{5,4},{6,7},{7,6},{8,9},{9,8},{10,11... | collective-permute-start | bytes 786440 | tf_op jit(solution)/shard_map/ppermute | solution.py:356
  411.6 16.0 %collective-permute-start.42 = (bf16[2,2,256,128]{3,2,1,0:T(8,128)(2,1)S(1)}, bf16[2,2,256,128]{3,2,1,0:T(8,128)(2,1)S(1)}, u32[]{:S(2)}, u32[]{:S(2)}) collective-permute-start(bf16[2,2,256,128]{3,2,1,0:T(8,128)(2,1)S(1)} %collective-permute-done.34.rest_5_), channel_id=1, source_target_pairs={{0,1},{1,0},{2,3},{3,2},{4,5},{5,4},{6,7},{7,6},{8,9},{9,8},{10,11... | collective-permute-start | bytes 786440 | tf_op jit(solution)/shard_map/ppermute | solution.py:356
  433.8 32.9 %collective-permute-start.68 = (bf16[4,2,256,128]{3,2,1,0:T(8,128)(2,1)}, bf16[4,2,256,128]{3,2,1,0:T(8,128)(2,1)S(1)}, u32[]{:S(2)}, u32[]{:S(2)}) collective-permute-start(bf16[4,2,256,128]{3,2,1,0:T(8,128)(2,1)} %copy-done.6), channel_id=1, source_target_pairs={{0,1},{1,0},{2,3},{3,2},{4,5},{5,4},{6,7},{7,6},{8,9},{9,8},{10,11... | collective-permute-start | bytes 1572872 | tf_op jit(solution)/shard_map/ppermute | solution.py:356
  434.0 33.0 %collective-permute-start.69 = (bf16[4,2,256,128]{3,2,1,0:T(8,128)(2,1)}, bf16[4,2,256,128]{3,2,1,0:T(8,128)(2,1)S(1)}, u32[]{:S(2)}, u32[]{:S(2)}) collective-permute-start(bf16[4,2,256,128]{3,2,1,0:T(8,128)(2,1)} %copy-done.10), channel_id=1, source_target_pairs={{0,1},{1,0},{2,3},{3,2},{4,5},{5,4},{6,7},{7,6},{8,9},{9,8},{10,11... | collective-permute-start | bytes 1572872 | tf_op jit(solution)/shard_map/ppermute | solution.py:356
  434.4 32.9 %collective-permute-start.70 = (bf16[4,2,256,128]{3,2,1,0:T(8,128)(2,1)}, bf16[4,2,256,128]{3,2,1,0:T(8,128)(2,1)}, u32[]{:S(2)}, u32[]{:S(2)}) collective-permute-start(bf16[4,2,256,128]{3,2,1,0:T(8,128)(2,1)} %copy-done.14), channel_id=1, source_target_pairs={{0,1},{1,0},{2,3},{3,2},{4,5},{5,4},{6,7},{7,6},{8,9},{9,8},{10,11... | collective-permute-start | bytes 1572872 | tf_op jit(solution)/shard_map/ppermute | solution.py:356
  434.8 32.7 %collective-permute-start.56 = (bf16[4,2,256,128]{3,2,1,0:T(8,128)(2,1)S(1)}, bf16[4,2,256,128]{3,2,1,0:T(8,128)(2,1)S(1)}, u32[]{:S(2)}, u32[]{:S(2)}) collective-permute-start(bf16[4,2,256,128]{3,2,1,0:T(8,128)(2,1)S(1)} %collective-permute-done.48.rest_4_), channel_id=1, source_target_pairs={{0,1},{1,0},{2,3},{3,2},{4,5},{5,4},{6,7},{7,6},{8,9},{9,8},{10,11... | collective-permute-start | bytes 1572872 | tf_op jit(solution)/shard_map/ppermute | solution.py:356
  435.8 32.1 %collective-permute-start.57 = (bf16[4,2,256,128]{3,2,1,0:T(8,128)(2,1)}, bf16[4,2,256,128]{3,2,1,0:T(8,128)(2,1)}, u32[]{:S(2)}, u32[]{:S(2)}) collective-permute-start(bf16[4,2,256,128]{3,2,1,0:T(8,128)(2,1)} %copy-done.2), channel_id=1, source_target_pairs={{0,1},{1,0},{2,3},{3,2},{4,5},{5,4},{6,7},{7,6},{8,9},{9,8},{10,11... | collective-permute-start | bytes 1572872 | tf_op jit(solution)/shard_map/ppermute | solution.py:356
  466.7 22.0 %collective-permute-start.58 = (bf16[4,2,256,128]{3,2,1,0:T(8,128)(2,1)S(1)}, bf16[4,2,256,128]{3,2,1,0:T(8,128)(2,1)S(1)}, u32[]{:S(2)}, u32[]{:S(2)}) collective-permute-start(bf16[4,2,256,128]{3,2,1,0:T(8,128)(2,1)S(1)} %copy-done.5), channel_id=1, source_target_pairs={{0,1},{1,0},{2,3},{3,2},{4,5},{5,4},{6,7},{7,6},{8,9},{9,8},{10,11... | collective-permute-start | bytes 1572872 | tf_op jit(solution)/shard_map/ppermute | solution.py:356
  467.0 22.2 %collective-permute-start.59 = (bf16[4,2,256,128]{3,2,1,0:T(8,128)(2,1)S(1)}, bf16[4,2,256,128]{3,2,1,0:T(8,128)(2,1)S(1)}, u32[]{:S(2)}, u32[]{:S(2)}) collective-permute-start(bf16[4,2,256,128]{3,2,1,0:T(8,128)(2,1)S(1)} %copy-done.9), channel_id=1, source_target_pairs={{0,1},{1,0},{2,3},{3,2},{4,5},{5,4},{6,7},{7,6},{8,9},{9,8},{10,11... | collective-permute-start | bytes 1572872 | tf_op jit(solution)/shard_map/ppermute | solution.py:356
  467.3 22.1 %collective-permute-start.53 = (bf16[4,2,256,128]{3,2,1,0:T(8,128)(2,1)S(1)}, bf16[4,2,256,128]{3,2,1,0:T(8,128)(2,1)S(1)}, u32[]{:S(2)}, u32[]{:S(2)}) collective-permute-start(bf16[4,2,256,128]{3,2,1,0:T(8,128)(2,1)S(1)} %copy-done.13), channel_id=1, source_target_pairs={{0,1},{1,0},{2,3},{3,2},{4,5},{5,4},{6,7},{7,6},{8,9},{9,8},{10,11... | collective-permute-start | bytes 1572872 | tf_op jit(solution)/shard_map/ppermute | solution.py:356
  467.5 22.2 %collective-permute-start.54 = (bf16[4,2,256,128]{3,2,1,0:T(8,128)(2,1)S(1)}, bf16[4,2,256,128]{3,2,1,0:T(8,128)(2,1)S(1)}, u32[]{:S(2)}, u32[]{:S(2)}) collective-permute-start(bf16[4,2,256,128]{3,2,1,0:T(8,128)(2,1)S(1)} %copy-done.17), channel_id=1, source_target_pairs={{0,1},{1,0},{2,3},{3,2},{4,5},{5,4},{6,7},{7,6},{8,9},{9,8},{10,11... | collective-permute-start | bytes 1572872 | tf_op jit(solution)/shard_map/ppermute | solution.py:356
  467.9 22.1 %collective-permute-start.55 = (bf16[4,2,256,128]{3,2,1,0:T(8,128)(2,1)S(1)}, bf16[4,2,256,128]{3,2,1,0:T(8,128)(2,1)S(1)}, u32[]{:S(2)}, u32[]{:S(2)}) collective-permute-start(bf16[4,2,256,128]{3,2,1,0:T(8,128)(2,1)S(1)} %copy-done.21), channel_id=1, source_target_pairs={{0,1},{1,0},{2,3},{3,2},{4,5},{5,4},{6,7},{7,6},{8,9},{9,8},{10,11... | collective-permute-start | bytes 1572872 | tf_op jit(solution)/shard_map/ppermute | solution.py:356
  488.8 22.2 %collective-permute-start.43 = (bf16[2,2,256,128]{3,2,1,0:T(8,128)(2,1)S(1)}, bf16[2,2,256,128]{3,2,1,0:T(8,128)(2,1)S(1)}, u32[]{:S(2)}, u32[]{:S(2)}) collective-permute-start(bf16[2,2,256,128]{3,2,1,0:T(8,128)(2,1)S(1)} %copy-done.49), channel_id=1, source_target_pairs={{0,1},{1,0},{2,3},{3,2},{4,5},{5,4},{6,7},{7,6},{8,9},{9,8},{10,11... | collective-permute-start | bytes 786440 | tf_op jit(solution)/shard_map/ppermute | solution.py:356
  489.1 22.2 %collective-permute-start.44 = (bf16[2,2,256,128]{3,2,1,0:T(8,128)(2,1)S(1)}, bf16[2,2,256,128]{3,2,1,0:T(8,128)(2,1)S(1)}, u32[]{:S(2)}, u32[]{:S(2)}) collective-permute-start(bf16[2,2,256,128]{3,2,1,0:T(8,128)(2,1)S(1)} %copy-done.51), channel_id=1, source_target_pairs={{0,1},{1,0},{2,3},{3,2},{4,5},{5,4},{6,7},{7,6},{8,9},{9,8},{10,11... | collective-permute-start | bytes 786440 | tf_op jit(solution)/shard_map/ppermute | solution.py:356
  489.4 22.1 %collective-permute-start.38 = (bf16[2,2,256,128]{3,2,1,0:T(8,128)(2,1)S(1)}, bf16[2,2,256,128]{3,2,1,0:T(8,128)(2,1)S(1)}, u32[]{:S(2)}, u32[]{:S(2)}) collective-permute-start(bf16[2,2,256,128]{3,2,1,0:T(8,128)(2,1)S(1)} %copy-done.53), channel_id=1, source_target_pairs={{0,1},{1,0},{2,3},{3,2},{4,5},{5,4},{6,7},{7,6},{8,9},{9,8},{10,11... | collective-permute-start | bytes 786440 | tf_op jit(solution)/shard_map/ppermute | solution.py:356
  489.7 22.1 %collective-permute-start.39 = (bf16[2,2,256,128]{3,2,1,0:T(8,128)(2,1)S(1)}, bf16[2,2,256,128]{3,2,1,0:T(8,128)(2,1)S(1)}, u32[]{:S(2)}, u32[]{:S(2)}) collective-permute-start(bf16[2,2,256,128]{3,2,1,0:T(8,128)(2,1)S(1)} %copy-done.55), channel_id=1, source_target_pairs={{0,1},{1,0},{2,3},{3,2},{4,5},{5,4},{6,7},{7,6},{8,9},{9,8},{10,11... | collective-permute-start | bytes 786440 | tf_op jit(solution)/shard_map/ppermute | solution.py:356
  489.9 22.1 %collective-permute-start.40 = (bf16[2,2,256,128]{3,2,1,0:T(8,128)(2,1)S(1)}, bf16[2,2,256,128]{3,2,1,0:T(8,128)(2,1)S(1)}, u32[]{:S(2)}, u32[]{:S(2)}) collective-permute-start(bf16[2,2,256,128]{3,2,1,0:T(8,128)(2,1)S(1)} %copy-done.57), channel_id=1, source_target_pairs={{0,1},{1,0},{2,3},{3,2},{4,5},{5,4},{6,7},{7,6},{8,9},{9,8},{10,11... | collective-permute-start | bytes 786440 | tf_op jit(solution)/shard_map/ppermute | solution.py:356
  511.5 11.6 %collective-permute-start.25 = (bf16[1,2,256,128]{3,2,1,0:T(8,128)(2,1)S(1)}, bf16[1,2,256,128]{3,2,1,0:T(8,128)(2,1)S(1)}, u32[]{:S(2)}, u32[]{:S(2)}) collective-permute-start(bf16[1,2,256,128]{3,2,1,0:T(8,128)(2,1)S(1)} %copy-done.83), channel_id=1, source_target_pairs={{0,1},{1,0},{2,3},{3,2},{4,5},{5,4},{6,7},{7,6},{8,9},{9,8},{10,11... | collective-permute-start | bytes 393224 | tf_op jit(solution)/shard_map/ppermute | solution.py:356
  512.1 11.6 %collective-permute-start.12 = (bf16[1,2,256,128]{3,2,1,0:T(8,128)(2,1)S(1)}, bf16[1,2,256,128]{3,2,1,0:T(8,128)(2,1)S(1)}, u32[]{:S(2)}, u32[]{:S(2)}) collective-permute-start(bf16[1,2,256,128]{3,2,1,0:T(8,128)(2,1)S(1)} %copy-done.81), channel_id=1, source_target_pairs={{0,1},{1,0},{2,3},{3,2},{4,5},{5,4},{6,7},{7,6},{8,9},{9,8},{10,11... | collective-permute-start | bytes 393224 | tf_op jit(solution)/shard_map/ppermute | solution.py:356
  (177 other events, 4458.2 us)

commit v2 on v1

--- a/solution.py
+++ b/solution.py
@@ -14,7 +14,8 @@
 TAPS = 4
 LANES = 128
 GROUP = 8
-VMEM = 48 * 1024 * 1024
+VMEM = 64 * 1024 * 1024 - 64 * 1024
+PARTS = (2, 10, 15, 16)
 
 
 def prototype(tap_count, fine_count):
@@ -94,7 +95,7 @@
     return summed.astype(jnp.bfloat16)
 
 
-def filter_rows(halves):
+def filter_rows(halves, kept):
     length = TAPS * FINE
     run = -(-(GROUP * FINE + length - FINE) // LANES) * LANES
     offsets = np.arange(length)
@@ -111,17 +112,18 @@
         table[:, 0, frame, 1, at] = hsin
         table[:, 1, frame, 0, at] = -hsin
         table[:, 1, frame, 1, at] = hcos
-    return table.reshape(halves, -1, 2 * run).astype(ml_dtypes.bfloat16)
-
-
-def filter_kernel(halves, chunks, where_ref, now_ref, next_ref, gain_ref, *rest):
-    table_refs = rest[:halves]
-    outs = rest[halves:-2]
+    table = table.reshape(halves, FINE // halves, -1, 2 * run)[:, kept]
+    return table.reshape(-1, 2 * run).astype(ml_dtypes.bfloat16)
+
+
+def filter_kernel(halves, kept, chunks, now_ref, next_ref, gain_ref, table_ref, *rest):
+    outs = rest[:-2]
     turned_ref, wide_ref = rest[-2:]
-    step = pl.program_id(0)
+    step = pl.program_id(1)
     inputs, samples = now_ref.shape[2], now_ref.shape[3]
     per_half = FINE // halves
-    run = table_refs[0].shape[2] // 2
+    count = sum(chunks)
+    run = table_ref.shape[1] // 2
     pair = 2 * GROUP
 
     @pl.when(step == 0)
@@ -129,14 +131,13 @@
         for part in range(2):
             turned_ref[part] = gain_ref[part, 0].T
             for half in range(halves):
-                start = pl.multiple_of(where_ref[1 + half] * per_half, per_half)
-                rows = turned_ref[part, pl.ds(start, per_half), :]
-                wide_ref[part, half] = jnp.broadcast_to(rows[:, None, :], (per_half, pair, inputs))
-
-    last = step == pl.num_programs(0) - 1
+                start = half * per_half + kept.start
+                rows = turned_ref[part, start : start + count, :]
+                wide_ref[part, half] = jnp.broadcast_to(rows[:, None, :], (count, pair, inputs))
+
+    last = step == pl.num_programs(1) - 1
     following = next_ref[:, 0]
     following = jnp.where(last, jnp.zeros_like(following), following)
-    table = jnp.concatenate([table_refs[half][0] for half in range(halves)], axis=0)
     for block in range(samples // (pair * FINE)):
         sets = []
         for group in range(2):
@@ -150,9 +151,9 @@
             sets.append(jnp.concatenate(columns, axis=1))
         lines = jnp.concatenate(sets, axis=0)
         sums = lax.dot_general(
-            table, lines, (((1,), (1,)), ((), ())), preferred_element_type=jnp.float32
+            table_ref[...], lines, (((1,), (1,)), ((), ())), preferred_element_type=jnp.float32
         )
-        sums = sums.reshape(halves, per_half, 2, GROUP, 2 * inputs)
+        sums = sums.reshape(halves, count, 2, GROUP, 2 * inputs)
         sums = jnp.concatenate([sums[..., :inputs], sums[..., inputs:]], axis=3)
         frames = slice(block * pair, (block + 1) * pair)
         for half in range(halves):
@@ -161,76 +162,80 @@
             real = (raw_real * gain_real - raw_imag * gain_imag).astype(jnp.bfloat16)
             imag = (raw_real * gain_imag + raw_imag * gain_real).astype(jnp.bfloat16)
             start = 0
-            for index, count in enumerate(chunks):
-                out = outs[half * len(chunks) + index]
-                out[:, 0, frames, :] = real[start : start + count]
-                out[:, 1, frames, :] = imag[start : start + count]
-                start += count
-
-
-def filter_bank(voltages, gains, tables, where, halves, chunks, samples_step):
-    _, _, inputs, samples = voltages.shape
+            for out, size in zip(outs, chunks):
+                out[half, :, 0, frames, :] = real[start : start + size]
+                out[half, :, 1, frames, :] = imag[start : start + size]
+                start += size
+
+
+def filter_bank(voltages, gains, halves, first, chunks, samples_step):
+    _, coarse, inputs, samples = voltages.shape
     frames = samples // FINE
     steps = samples // samples_step
     ratio = samples_step // LANES
     frames_step = samples_step // FINE
-    _, table_rows, table_columns = tables.shape
-    spec = pltpu.PrefetchScalarGridSpec(
-        num_scalar_prefetch=1,
-        grid=(steps,),
+    kept = slice(first, first + sum(chunks))
+    table = filter_rows(halves, kept)
+    return pl.pallas_call(
+        functools.partial(filter_kernel, halves, kept, chunks),
+        out_shape=[
+            jax.ShapeDtypeStruct((coarse * halves, count, 2, frames, inputs), jnp.bfloat16)
+            for count in chunks
+        ],
+        grid=(coarse, steps),
         in_specs=[
-            pl.BlockSpec((2, 1, inputs, samples_step), lambda t, w: (0, w[0], 0, t)),
+            pl.BlockSpec((2, 1, inputs, samples_step), lambda c, t: (0, c, 0, t)),
             pl.BlockSpec(
                 (2, 1, inputs, LANES),
-                lambda t, w: (0, w[0], 0, jnp.minimum((t + 1) * ratio, steps * ratio - 1)),
+                lambda c, t: (0, c, 0, jnp.minimum((t + 1) * ratio, steps * ratio - 1)),
             ),
-            pl.BlockSpec((2, 1, inputs, FINE), lambda t, w: (0, w[0], 0, 0)),
-        ]
-        + [
-            pl.BlockSpec((1, table_rows, table_columns), lambda t, w, half=half: (w[1 + half], 0, 0))
-            for half in range(halves)
+            pl.BlockSpec((2, 1, inputs, FINE), lambda c, t: (0, c, 0, 0)),
+            pl.BlockSpec(table.shape, lambda c, t: (0, 0)),
         ],
         out_specs=[
-            pl.BlockSpec((count, 2, frames_step, inputs), lambda t, w: (0, 0, t, 0))
-            for _ in range(halves)
+            pl.BlockSpec((halves, count, 2, frames_step, inputs), lambda c, t: (c, 0, 0, t, 0))
             for count in chunks
         ],
         scratch_shapes=[
             pltpu.VMEM((2, FINE, inputs), jnp.float32),
-            pltpu.VMEM((2, halves, FINE // halves, 2 * GROUP, inputs), jnp.float32),
+            pltpu.VMEM((2, halves, sum(chunks), 2 * GROUP, inputs), jnp.float32),
         ],
-    )
-    flops = 2 * 2 * FINE * GROUP * table_columns * inputs * (frames // GROUP)
-    outs = pl.pallas_call(
-        functools.partial(filter_kernel, halves, chunks),
-        out_shape=[
-            jax.ShapeDtypeStruct((count, 2, frames, inputs), jnp.bfloat16)
-            for _ in range(halves)
-            for count in chunks
-        ],
-        grid_spec=spec,
         compiler_params=pltpu.CompilerParams(vmem_limit_bytes=VMEM),
-        cost_estimate=pl.CostEstimate(
-            flops=flops, bytes_accessed=16 * inputs * samples, transcendentals=0
-        ),
+        cost_estimate=pl.CostEstimate(flops=4 * table.size * inputs * frames // GROUP * coarse, bytes_accessed=16 * coarse * inputs * samples, transcendentals=0),
         name="filter_bank",
-    )(where, voltages, voltages, gains, *([tables] * halves))
-    return [outs[half * len(chunks) : (half + 1) * len(chunks)] for half in range(halves)]
-
-
-def correlate_kernel(count, spans, tile, scale, where_ref, *rest):
-    blocks = rest[: count * spans]
+    )(voltages, voltages, gains, jnp.asarray(table))
+
+
+def gate(released, waits):
+    def nothing(*_):
+        pass
+
+    anywhere = pl.BlockSpec(memory_space=pl.ANY)
+    return pl.pallas_call(
+        nothing,
+        out_shape=[jax.ShapeDtypeStruct(array.shape, array.dtype) for array in released],
+        in_specs=[anywhere] * (len(released) + len(waits)),
+        out_specs=[anywhere] * len(released),
+        input_output_aliases={index: index for index in range(len(released))},
+        compiler_params=pltpu.CompilerParams(vmem_limit_bytes=VMEM),
+        cost_estimate=pl.CostEstimate(flops=0, bytes_accessed=0, transcendentals=0),
+        name="gate",
+    )(*released, *waits)
+
+
+def correlate_kernel(spans, tile, scale, where_ref, *rest):
+    blocks = rest[:spans]
     out_ref, all_ref, rows_ref = rest[-3:]
-    _, _, frames, inputs = blocks[0].shape
+    count, _, _, frames, inputs = blocks[0].shape
     total = all_ref.shape[2]
     row_count = out_ref.shape[1]
     depth = spans * 2 * frames
     for span in range(spans):
         for index in range(count):
-            start = pl.multiple_of(where_ref[index] * inputs, inputs)
+            columns = slice(index * inputs, (index + 1) * inputs)
             for part in range(2):
-                all_ref[2 * span + part, :, pl.ds(start, inputs)] = blocks[span * count + index][0, part]
-    first_row = pl.multiple_of(where_ref[count] * row_count, row_count)
+                all_ref[2 * span + part, :, columns] = blocks[span][index, 0, part]
+    first_row = pl.multiple_of(where_ref[0] * row_count, row_count)
     for start in range(0, row_count, LANES):
         for span in range(spans):
             for part in range(2):
@@ -247,7 +252,7 @@
         row, column = position // column_tiles, position % column_tiles
         row_at = pl.multiple_of(row * tile, tile)
         column_at = pl.multiple_of(column * tile, tile)
-        row_global = where_ref[count] * row_tiles + row
+        row_global = where_ref[0] * row_tiles + row
         columns = all_ref[:, :, pl.ds(column_at, tile)].reshape(depth, tile)
 
         def product(kind):
@@ -274,18 +279,18 @@
 
 
 def correlate(pieces, where, held, first, channels, row_count, total, tile, scale):
-    spans, count = len(pieces), len(pieces[0])
-    chunk, _, frames, inputs = pieces[0][0].shape
+    spans = len(pieces)
+    count, chunk, _, frames, inputs = pieces[0].shape
     depth = spans * 2 * frames
-    operands = [piece for row in pieces for piece in row]
-    in_specs = [pl.BlockSpec((1, 2, frames, inputs), lambda q, w: (q, 0, 0, 0)) for _ in operands]
+    operands = list(pieces)
+    in_specs = [pl.BlockSpec((count, 1, 2, frames, inputs), lambda q, w: (0, q, 0, 0, 0)) for _ in operands]
     aliases = {}
     if held is not None:
         aliases = {1 + len(operands): 0}
         operands.append(held)
         in_specs.append(pl.BlockSpec(memory_space=pl.ANY))
     return pl.pallas_call(
-        functools.partial(correlate_kernel, count, spans, tile, scale),
+        functools.partial(correlate_kernel, spans, tile, scale),
         out_shape=jax.ShapeDtypeStruct((channels, row_count, total), jnp.bfloat16),
         grid_spec=pltpu.PrefetchScalarGridSpec(
             num_scalar_prefetch=1,
@@ -309,12 +314,8 @@
 
 
 def chunk_sizes(channels):
-    sizes, left = [], channels
-    while left > 0:
-        size = max(1, min(channels // 4, left // 2))
-        sizes.append(size)
-        left -= size
-    return sizes
+    cuts = sorted({0} | {max(1, channels * part // 16) for part in PARTS})
+    return [stop - start for start, stop in zip(cuts, cuts[1:])]
 
 
 def local_kernels(count, spans, voltages, gains):
@@ -326,37 +327,22 @@
     total = count * inputs
     row_count = total // spans
     tile = min(2 * LANES, row_count)
-    here = lax.axis_index("inp")
-    span_here = lax.axis_index("span")
-    tables = jnp.asarray(filter_rows(halves))
     pair = 2 * GROUP * FINE
-    samples_step = 2 * pair if samples % (2 * pair) == 0 else pair
-    order = sorted(range(coarse), key=lambda m: -m)
-    own = here % halves
-    spectra = {}
-    for step in order:
-        where = jnp.stack([(here // halves) ^ step] + [own ^ half for half in range(halves)])
-        banks = filter_bank(
-            voltages, gains, tables, where.astype(jnp.int32), halves, chunks, samples_step
-        )
-        for half in range(halves):
-            spectra[step * halves + half] = banks[half]
-    places = jnp.stack([here ^ step for step in range(count)] + [span_here]).astype(jnp.int32)
+    samples_step = max(size for size in (pair, 2 * pair, 4 * pair) if samples % size == 0)
+    where = jnp.stack([lax.axis_index("span")]).astype(jnp.int32)
+    outgoing = list(filter_bank(voltages, gains, halves, 0, chunks[:1], samples_step))
+    if len(chunks) > 1:
+        outgoing += list(filter_bank(voltages, gains, halves, chunks[0], chunks[1:], samples_step))
     held, first = None, 0
     for index, size in enumerate(chunks):
-        mine = []
-        for step in range(count):
-            piece = spectra[step][index]
-            if step:
-                piece = lax.ppermute(piece, "inp", [(i, i ^ step) for i in range(count)])
-            mine.append(piece)
-        pieces = [mine]
+        turned = lax.all_to_all(outgoing[index], "inp", split_axis=0, concat_axis=0, tiled=True)
+        if index > 0:
+            turned, held = gate([turned, held], [])
+        pieces = [turned]
         for other in range(1, spans):
-            pieces.append(
-                [lax.ppermute(piece, "span", [(i, i ^ other) for i in range(spans)]) for piece in mine]
-            )
+            pieces.append(lax.ppermute(turned, "span", [(i, i ^ other) for i in range(spans)]))
         held = correlate(
-            pieces, places, held, first, channels, row_count, total, tile, 1.0 / (spans * frames)
+            pieces, where, held, first, channels, row_count, total, tile, 1.0 / (spans * frames)
         )
         first += size
     return held

time: 541 us -> 427 us (0.79)
  starting transfers between devices: 142 us -> 21.5 us
  waiting for transfers between devices: 224 us -> 284 us
  local copies, waits for them, and re-layouts: 49.8 us -> 1.9 us
    all_to_all x0 -> x4, waiting for transfers between devices: none -> 263 us  [local_kernels(): lax.all_to_all(outgoing[index], 'inp', split_axis=0, concat_axis=0, tiled...]
    ppermute x90 -> x4, waiting for transfers between devices: 224 us -> 20.9 us  [local_kernels(): lax.ppermute(turned, 'span', [(i, i ^ other) for i in range(spans)])]
    ppermute x90 -> x4, starting transfers between devices: 142 us -> 0.24 us  [local_kernels(): lax.ppermute(turned, 'span', [(i, i ^ other) for i in range(spans)])]
    unnamed x303 -> x1, local copies, waits for them, and re-layouts: 49.7 us -> 1.9 us
    all_to_all x0 -> x4, starting transfers between devices: none -> 21.2 us  [local_kernels(): lax.all_to_all(outgoing[index], 'inp', split_axis=0, concat_axis=0, tiled...]
    pallas_call x10 -> x9, Pallas kernels: 119 us -> 119 us  [the longest x4 79 us: correlate(): pl.pallas_call(functools.partial(correlate_kernel, spans, tile, scale), o...]
  transfers between devices with their start and end apart: 90 -> 8, of which waited for: 14 -> 7; matrix products, arithmetic and copies ran while one was open for 0% -> 0% of each run, Pallas kernels for 19% -> 22%
where the time goes in v2:
time: 427 us; the launch traced here: 426 us
  waiting for transfers between devices  284 us (67%)
  Pallas kernels  119 us (28%)
  starting transfers between devices  21.5 us (5%)
    all_to_all x4, waiting for transfers between devices, local_kernels(): lax.all_to_all(outgoing[index], 'inp', split_axis=0, concat_axis=0, tiled...  263 us
    pallas_call x4, Pallas kernels, correlate(): pl.pallas_call(functools.partial(correlate_kernel, spans, tile, scale), o...  79 us
    pallas_call x2, Pallas kernels, filter_bank(): pl.pallas_call(functools.partial(filter_kernel, halves, kept, chunks), ou...  40 us
    all_to_all x4, starting transfers between devices, local_kernels(): lax.all_to_all(outgoing[index], 'inp', split_axis=0, concat_axis=0, tiled...  21.2 us
    ppermute x4, waiting for transfers between devices, local_kernels(): lax.ppermute(turned, 'span', [(i, i ^ other) for i in range(spans)])  20.9 us
  transfers between devices with their start and end apart: 8, of which 7 were waited for; matrix products, arithmetic and copies ran while one was open for 0% of the time, Pallas kernels for 22%

profile of v2, /device:TPU:0, one launch (start us, length us, event | category | flops | bytes accessed | tf_op | source)
XLA Modules:
  0.0 426.1 jit_solution(12866145440306162943)
XLA Ops:
  0.0 1.9 copy.14.gain_ref
  1.9 17.2 %filter_bank.3 = bf16[8,2,2,256,128]{4,3,2,1,0:T(8,128)(2,1)} custom-call(bf16[2,4,128,8192]{3,2,1,0:T(8,128)(2,1)} %next_ref.3, bf16[2,4,128,8192]{3,2,1,0:T(8,128)(2,1)} %next_ref.3, f32[2,4,128,32]{3,2,1,0:T(8,128)} %copy.14.gain_ref, bf16[64,768]{1,0:T(8,128)(2,1)} %constant.8.clone.table_ref), custom_call_target="tpu_custom_call" | custom-call | flops 3221225472 | bytes 67108864 | tf_op jit(solution)/shard_map/filter_bank/pallas_call | solution.py:179
  19.1 7.3 %all-to-all-start.3 = ((bf16[8,2,2,256,128]{4,3,2,1,0:T(8,128)(2,1)}), bf16[8,2,2,256,128]{4,3,2,1,0:T(8,128)(2,1)}, u32[]{:S(2)}, u32[]{:S(2)}) async-start(bf16[8,2,2,256,128]{4,3,2,1,0:T(8,128)(2,1)} %filter_bank.3), calls=%async_computation.3 | async-start | bytes 4194304 | tf_op jit(solution)/shard_map/all_to_all | solution.py:338
  26.4 22.7 %filter_bank.2 = (bf16[8,8,2,256,128]{4,3,2,1,0:T(8,128)(2,1)}, bf16[8,5,2,256,128]{4,3,2,1,0:T(8,128)(2,1)}, bf16[8,1,2,256,128]{4,3,2,1,0:T(8,128)(2,1)}) custom-call(bf16[2,4,128,8192]{3,2,1,0:T(8,128)(2,1)} %next_ref.3, bf16[2,4,128,8192]{3,2,1,0:T(8,128)(2,1)} %next_ref.3, f32[2,4,128,32]{3,2,1,0:T(8,128)} %copy.14.gain_ref, ...), custom_call_target="tpu_custom_call" | custom-call | flops 22548578304 | bytes 67108864 | tf_op jit(solution)/shard_map/filter_bank/pallas_call | solution.py:179
  49.1 25.6 %all-to-all-done.3.rest_0_ = bf16[8,2,2,256,128]{4,3,2,1,0:T(8,128)(2,1)} async-done(((bf16[8,2,2,256,128]{4,3,2,1,0:T(8,128)(2,1)}), bf16[8,2,2,256,128]{4,3,2,1,0:T(8,128)(2,1)}, u32[]{:S(2)}, u32[]{:S(2)}) %all-to-all-start.3) | async-done | bytes 2097184 | tf_op jit(solution)/shard_map/all_to_all | solution.py:338
  74.7 5.0 %all-to-all-start.2 = ((bf16[8,8,2,256,128]{4,3,2,1,0:T(8,128)(2,1)}), bf16[8,8,2,256,128]{4,3,2,1,0:T(8,128)(2,1)}, u32[]{:S(2)}, u32[]{:S(2)}) async-start(bf16[8,8,2,256,128]{4,3,2,1,0:T(8,128)(2,1)} %get-tuple-element.16), calls=%async_computation.2 | async-start | bytes 16777216 | tf_op jit(solution)/shard_map/all_to_all | solution.py:338
  79.8 0.1 collective-permute-start
  79.9 4.5 %collective-permute-done.rest_1_ = bf16[8,2,2,256,128]{4,3,2,1,0:T(8,128)(2,1)} collective-permute-done((bf16[8,2,2,256,128]{4,3,2,1,0:T(8,128)(2,1)}, bf16[8,2,2,256,128]{4,3,2,1,0:T(8,128)(2,1)}, u32[]{:S(2)}, u32[]{:S(2)}) %collective-permute-start) | collective-permute-done | bytes 2097184 | tf_op jit(solution)/shard_map/ppermute | solution.py:343
  84.3 11.1 %correlate.4.__1_ = bf16[16,512,1024]{2,1,0:T(8,128)(2,1)} custom-call(s32[1]{0:T(128)} %bitcast.where_ref, bf16[8,2,2,256,128]{4,3,2,1,0:T(8,128)(2,1)} %all-to-all-done.3.rest_0_, bf16[8,2,2,256,128]{4,3,2,1,0:T(8,128)(2,1)} %collective-permute-done.rest_1_), custom_call_target="tpu_custom_call" | custom-call | flops 3221225472 | bytes 6291456 | tf_op jit(solution)/shard_map/correlate/pallas_call | solution.py:292
  95.4 166.5 %all-to-all-done.2.__0_ = bf16[8,8,2,256,128]{4,3,2,1,0:T(8,128)(2,1)} async-done(((bf16[8,8,2,256,128]{4,3,2,1,0:T(8,128)(2,1)}), bf16[8,8,2,256,128]{4,3,2,1,0:T(8,128)(2,1)}, u32[]{:S(2)}, u32[]{:S(2)}) %all-to-all-start.2) | async-done | bytes 8388640 | tf_op jit(solution)/shard_map/all_to_all | solution.py:338
  262.0 0.0 collective-permute-start.1
  262.0 4.7 %all-to-all-start.1 = ((bf16[8,5,2,256,128]{4,3,2,1,0:T(8,128)(2,1)}), bf16[8,5,2,256,128]{4,3,2,1,0:T(8,128)(2,1)}, u32[]{:S(2)}, u32[]{:S(2)}) async-start(bf16[8,5,2,256,128]{4,3,2,1,0:T(8,128)(2,1)} %get-tuple-element.15), calls=%async_computation.1 | async-start | bytes 10485760 | tf_op jit(solution)/shard_map/all_to_all | solution.py:338
  266.7 8.8 %collective-permute-done.1.rest_1_ = bf16[8,8,2,256,128]{4,3,2,1,0:T(8,128)(2,1)} collective-permute-done((bf16[8,8,2,256,128]{4,3,2,1,0:T(8,128)(2,1)}, bf16[8,8,2,256,128]{4,3,2,1,0:T(8,128)(2,1)}, u32[]{:S(2)}, u32[]{:S(2)}) %collective-permute-start.1) | collective-permute-done | bytes 8388640 | tf_op jit(solution)/shard_map/ppermute | solution.py:343
  275.5 37.0 %correlate.5.__1_ = bf16[16,512,1024]{2,1,0:T(8,128)(2,1)} custom-call(s32[1]{0:T(128)} %bitcast.where_ref, bf16[8,8,2,256,128]{4,3,2,1,0:T(8,128)(2,1)} %get-tuple-element.17.rest_0_, bf16[8,8,2,256,128]{4,3,2,1,0:T(8,128)(2,1)} %collective-permute-done.1.rest_1_, bf16[16,512,1024]{2,1,0:T(8,128)(2,1)} %get-tuple-element.18.rest_2_), custom_call_target="tpu_custom_call", output_to_operand_aliasing={{}: (3, {})} | custom-call | flops 12884901888 | bytes 25165824 | tf_op jit(solution)/shard_map/correlate/pallas_call | solution.py:292
  312.5 70.8 %all-to-all-done.1.__0_ = bf16[8,5,2,256,128]{4,3,2,1,0:T(8,128)(2,1)} async-done(((bf16[8,5,2,256,128]{4,3,2,1,0:T(8,128)(2,1)}), bf16[8,5,2,256,128]{4,3,2,1,0:T(8,128)(2,1)}, u32[]{:S(2)}, u32[]{:S(2)}) %all-to-all-start.1) | async-done | bytes 5242912 | tf_op jit(solution)/shard_map/all_to_all | solution.py:338
  383.3 0.0 collective-permute-start.2
  383.3 4.3 all-to-all-start
  387.5 4.7 %collective-permute-done.2.rest_1_ = bf16[8,5,2,256,128]{4,3,2,1,0:T(8,128)(2,1)} collective-permute-done((bf16[8,5,2,256,128]{4,3,2,1,0:T(8,128)(2,1)}, bf16[8,5,2,256,128]{4,3,2,1,0:T(8,128)(2,1)}, u32[]{:S(2)}, u32[]{:S(2)}) %collective-permute-start.2) | collective-permute-done | bytes 5242912 | tf_op jit(solution)/shard_map/ppermute | solution.py:343
  392.3 24.1 %correlate.6.__1_ = bf16[16,512,1024]{2,1,0:T(8,128)(2,1)} custom-call(s32[1]{0:T(128)} %bitcast.where_ref, bf16[8,5,2,256,128]{4,3,2,1,0:T(8,128)(2,1)} %get-tuple-element.19.rest_0_, bf16[8,5,2,256,128]{4,3,2,1,0:T(8,128)(2,1)} %collective-permute-done.2.rest_1_, bf16[16,512,1024]{2,1,0:T(8,128)(2,1)} %get-tuple-element.20.rest_2_), custom_call_target="tpu_custom_call", output_to_operand_aliasing={{}: (3, {})} | custom-call | flops 8053063680 | bytes 15728640 | tf_op jit(solution)/shard_map/correlate/pallas_call | solution.py:292
  416.3 0.0 all-to-all-done.__0_
  416.3 0.2 collective-permute-start.3
  416.5 2.8 collective-permute-done.3.rest_1_
  419.3 6.8 %correlate.7 = bf16[16,512,1024]{2,1,0:T(8,128)(2,1)} custom-call(s32[1]{0:T(128)} %bitcast.where_ref, bf16[8,1,2,256,128]{4,3,2,1,0:T(8,128)(2,1)} %get-tuple-element.21.rest_0_, bf16[8,1,2,256,128]{4,3,2,1,0:T(8,128)(2,1)} %collective-permute-done.3.rest_1_, bf16[16,512,1024]{2,1,0:T(8,128)(2,1)} %get-tuple-element.22.rest_2_), custom_call_target="tpu_custom_call", output_to_operand_aliasing={{}: (3, {})} | custom-call | flops 1610612736 | bytes 3145728 | tf_op jit(solution)/shard_map/correlate/pallas_call | solution.py:292
  (3 shorter events, 0.0 us)
Async XLA Ops:
  19.1 55.6 %all-to-all-start.3 = ((bf16[8,2,2,256,128]{4,3,2,1,0:T(8,128)(2,1)}), bf16[8,2,2,256,128]{4,3,2,1,0:T(8,128)(2,1)}, u32[]{:S(2)}, u32[]{:S(2)}) async-start(bf16[8,2,2,256,128]{4,3,2,1,0:T(8,128)(2,1)} %filter_bank.3), calls=%async_computation.3 | async-start | bytes 4194304 | tf_op jit(solution)/shard_map/all_to_all | solution.py:338
  74.7 187.2 %all-to-all-start.2 = ((bf16[8,8,2,256,128]{4,3,2,1,0:T(8,128)(2,1)}), bf16[8,8,2,256,128]{4,3,2,1,0:T(8,128)(2,1)}, u32[]{:S(2)}, u32[]{:S(2)}) async-start(bf16[8,8,2,256,128]{4,3,2,1,0:T(8,128)(2,1)} %get-tuple-element.16), calls=%async_computation.2 | async-start | bytes 16777216 | tf_op jit(solution)/shard_map/all_to_all | solution.py:338
  79.8 4.6 %collective-permute-start = (bf16[8,2,2,256,128]{4,3,2,1,0:T(8,128)(2,1)}, bf16[8,2,2,256,128]{4,3,2,1,0:T(8,128)(2,1)}, u32[]{:S(2)}, u32[]{:S(2)}) collective-permute-start(bf16[8,2,2,256,128]{4,3,2,1,0:T(8,128)(2,1)} %all-to-all-done.3.rest_0_), channel_id=1, source_target_pairs={{0,1},{1,0},{2,3},{3,2},{4,5},{5,4},{6,7},{7,6},{8,9},{9,8},{10,11... | collective-permute-start | bytes 6291464 | tf_op jit(solution)/shard_map/ppermute | solution.py:343
  262.0 13.5 %collective-permute-start.1 = (bf16[8,8,2,256,128]{4,3,2,1,0:T(8,128)(2,1)}, bf16[8,8,2,256,128]{4,3,2,1,0:T(8,128)(2,1)}, u32[]{:S(2)}, u32[]{:S(2)}) collective-permute-start(bf16[8,8,2,256,128]{4,3,2,1,0:T(8,128)(2,1)} %get-tuple-element.17.rest_0_), channel_id=1, source_target_pairs={{0,1},{1,0},{2,3},{3,2},{4,5},{5,4},{6,7},{7,6},{8,9},{9,8},{10,11... | collective-permute-start | bytes 25165832 | tf_op jit(solution)/shard_map/ppermute | solution.py:343
  262.0 121.3 %all-to-all-start.1 = ((bf16[8,5,2,256,128]{4,3,2,1,0:T(8,128)(2,1)}), bf16[8,5,2,256,128]{4,3,2,1,0:T(8,128)(2,1)}, u32[]{:S(2)}, u32[]{:S(2)}) async-start(bf16[8,5,2,256,128]{4,3,2,1,0:T(8,128)(2,1)} %get-tuple-element.15), calls=%async_computation.1 | async-start | bytes 10485760 | tf_op jit(solution)/shard_map/all_to_all | solution.py:338
  383.3 9.0 %collective-permute-start.2 = (bf16[8,5,2,256,128]{4,3,2,1,0:T(8,128)(2,1)}, bf16[8,5,2,256,128]{4,3,2,1,0:T(8,128)(2,1)}, u32[]{:S(2)}, u32[]{:S(2)}) collective-permute-start(bf16[8,5,2,256,128]{4,3,2,1,0:T(8,128)(2,1)} %get-tuple-element.19.rest_0_), channel_id=1, source_target_pairs={{0,1},{1,0},{2,3},{3,2},{4,5},{5,4},{6,7},{7,6},{8,9},{9,8},{10,11... | collective-permute-start | bytes 15728648 | tf_op jit(solution)/shard_map/ppermute | solution.py:343
  383.3 33.1 %all-to-all-start = ((bf16[8,1,2,256,128]{4,3,2,1,0:T(8,128)(2,1)}), bf16[8,1,2,256,128]{4,3,2,1,0:T(8,128)(2,1)}, u32[]{:S(2)}, u32[]{:S(2)}) async-start(bf16[8,1,2,256,128]{4,3,2,1,0:T(8,128)(2,1)} %get-tuple-element.14), calls=%async_computation | async-start | bytes 2097152 | tf_op jit(solution)/shard_map/all_to_all | solution.py:338
  416.3 3.0 collective-permute-start.3

commit v3 on v0

--- a/solution.py
+++ b/solution.py
@@ -1,12 +1,22 @@
+import functools
 import math
 
 import jax
 import jax.numpy as jnp
+import ml_dtypes
+import numpy as np
 from jax import lax
+from jax.experimental import pallas as pl
+from jax.experimental.pallas import tpu as pltpu
 from jax.sharding import PartitionSpec as P
 
 FINE = 32
 TAPS = 4
+LANES = 128
+GROUP = 8
+VMEM = 64 * 1024 * 1024 - 64 * 1024
+EARLY = 2
+PARTS = (10, 15, 16)
 
 
 def prototype(tap_count, fine_count):
@@ -43,7 +53,7 @@
     return jnp.where(upper[None], real_sums, imag_sums)
 
 
-def local(voltages, gains):
+def local_plain(voltages, gains):
     coarse = voltages.shape[1]
     local_inputs = voltages.shape[2]
     samples = voltages.shape[3]
@@ -86,7 +96,298 @@
     return summed.astype(jnp.bfloat16)
 
 
+def filter_rows():
+    length = TAPS * FINE
+    run = -(-(GROUP * FINE + length - FINE) // LANES) * LANES
+    offsets = np.arange(length)
+    window = np.sinc((offsets - length / 2 + 0.5) / FINE)
+    window = window * (0.5 - 0.5 * np.cos(2.0 * np.pi * (offsets + 0.5) / length))
+    window = window / np.sqrt(np.sum(window * window))
+    angles = 2.0 * np.pi * (offsets[None, :] * np.arange(FINE)[:, None] % FINE) / FINE
+    hcos = window * np.cos(angles)
+    hsin = window * np.sin(angles)
+    table = np.zeros((FINE, 2, GROUP, 2, run))
+    for frame in range(GROUP):
+        at = slice(frame * FINE, frame * FINE + length)
+        table[:, 0, frame, 0, at] = hcos
+        table[:, 0, frame, 1, at] = hsin
+        table[:, 1, frame, 0, at] = -hsin
+        table[:, 1, frame, 1, at] = hcos
+    return table.reshape(-1, 2 * run).astype(ml_dtypes.bfloat16)
+
+
+def filter_kernel(halves, chunks, lead, pairs, volt_ref, gain_ref, table_ref, *rest):
+    outs, wide_ref = rest[-1 - len(chunks) : -1], rest[-1]
+    inputs, samples = volt_ref.shape[2], volt_ref.shape[3]
+    per_half = FINE // halves
+    run = table_ref.shape[1] // 2
+    hop = GROUP * FINE
+    wide_ref[...] = jnp.broadcast_to(gain_ref[:, 0][:, :, None, :], wide_ref.shape)
+
+    def one(pair, inside):
+        sets = []
+        for group in range(2):
+            start = lead + (2 * pair + group) * hop
+            columns = []
+            for part in range(2):
+                if inside:
+                    columns.append(volt_ref[part, 0, :, pl.ds(pl.multiple_of(start, LANES), run)])
+                else:
+                    stop = min(start + run, samples)
+                    columns.append(volt_ref[part, 0, :, start:stop])
+                    if start + run > stop:
+                        columns.append(jnp.zeros((inputs, start + run - stop), volt_ref.dtype))
+            sets.append(jnp.concatenate(columns, axis=1))
+        lines = jnp.concatenate(sets, axis=0)
+        sums = lax.dot_general(
+            table_ref[...], lines, (((1,), (1,)), ((), ())), preferred_element_type=jnp.float32
+        )
+        sums = sums.reshape(FINE, 2, GROUP, 2 * inputs)
+        raw_real = jnp.concatenate([sums[:, 0, :, :inputs], sums[:, 0, :, inputs:]], axis=1)
+        raw_imag = jnp.concatenate([sums[:, 1, :, :inputs], sums[:, 1, :, inputs:]], axis=1)
+        gain_real, gain_imag = wide_ref[0], wide_ref[1]
+        real = (raw_real * gain_real - raw_imag * gain_imag).astype(jnp.bfloat16)
+        imag = (raw_real * gain_imag + raw_imag * gain_real).astype(jnp.bfloat16)
+        frames = pl.ds(pl.multiple_of(2 * GROUP * pair, 2 * GROUP), 2 * GROUP) if inside else pl.ds(
+            2 * GROUP * pair, 2 * GROUP
+        )
+        for half in range(halves):
+            start = half * per_half
+            for out, size in zip(outs, chunks):
+                out[half, :, 0, frames, :] = real[start : start + size]
+                out[half, :, 1, frames, :] = imag[start : start + size]
+                start += size
+
+    whole = min(pairs, (samples - lead - run + hop) // (2 * hop))
+
+    def loop(pair, _):
+        one(pair, True)
+        return 0
+
+    lax.fori_loop(0, whole, loop, 0)
+    for pair in range(whole, pairs):
+        one(pair, False)
+
+
+def filter_bank(voltages, gains, halves, chunks, first_frame, last_frame, waits=()):
+    _, coarse, inputs, samples = voltages.shape
+    table = filter_rows()
+    run = table.shape[1] // 2
+    frames = last_frame - first_frame
+    ahead = run - GROUP * FINE
+    block = min(samples, last_frame * FINE + ahead)
+    return pl.pallas_call(
+        functools.partial(
+            filter_kernel, halves, chunks, first_frame * FINE, frames // (2 * GROUP)
+        ),
+        out_shape=[
+            jax.ShapeDtypeStruct((coarse * halves, count, 2, frames, inputs), jnp.bfloat16)
+            for count in chunks
+        ],
+        grid=(coarse,),
+        in_specs=[
+            pl.BlockSpec((2, 1, inputs, block), lambda c: (0, c, 0, 0)),
+            pl.BlockSpec((2, 1, FINE, inputs), lambda c: (0, c, 0, 0)),
+            pl.BlockSpec(table.shape, lambda c: (0, 0)),
+        ]
+        + [pl.BlockSpec(memory_space=pl.ANY)] * len(waits),
+        out_specs=[
+            pl.BlockSpec((halves, count, 2, frames, inputs), lambda c: (c, 0, 0, 0, 0))
+            for count in chunks
+        ],
+        scratch_shapes=[pltpu.VMEM((2, FINE, 2 * GROUP, inputs), jnp.float32)],
+        compiler_params=pltpu.CompilerParams(vmem_limit_bytes=VMEM),
+        cost_estimate=pl.CostEstimate(
+            flops=4 * table.size * inputs * frames // GROUP * coarse,
+            bytes_accessed=16 * coarse * inputs * frames * FINE,
+            transcendentals=0,
+        ),
+        name="filter_bank",
+    )(voltages, gains, jnp.asarray(table), *waits)
+
+
+def gate(released, waits):
+    def nothing(*_):
+        pass
+
+    anywhere = pl.BlockSpec(memory_space=pl.ANY)
+    return pl.pallas_call(
+        nothing,
+        out_shape=[jax.ShapeDtypeStruct(array.shape, array.dtype) for array in released],
+        in_specs=[anywhere] * (len(released) + len(waits)),
+        out_specs=[anywhere] * len(released),
+        input_output_aliases={index: index for index in range(len(released))},
+        compiler_params=pltpu.CompilerParams(vmem_limit_bytes=VMEM),
+        cost_estimate=pl.CostEstimate(flops=0, bytes_accessed=0, transcendentals=0),
+        name="gate",
+    )(*released, *waits)
+
+
+def correlate_kernel(pieces, tile, scale, where_ref, *rest):
+    blocks = rest[:pieces]
+    out_ref, rows_ref = rest[-2:]
+    inputs = blocks[0].shape[4]
+    row_count, total = out_ref.shape[1:]
+    depth = rows_ref.shape[2]
+    per_tile = tile // inputs
+    row_tiles, column_tiles = row_count // tile, total // tile
+
+    def columns_of(position):
+        sources = [position * per_tile + index for index in range(per_tile)]
+        parts = [
+            jnp.concatenate([block[source, 0, part] for source in sources], axis=1)
+            for part in range(2)
+            for block in blocks
+        ]
+        return jnp.concatenate(parts, axis=0)
+
+    first_tile = where_ref[0] * row_tiles
+    unit = (
+        lax.broadcasted_iota(jnp.int32, (tile, tile), 0)
+        == lax.broadcasted_iota(jnp.int32, (tile, tile), 1)
+    )
+    unit = jnp.where(unit, 1.0, 0.0).astype(jnp.bfloat16)
+    for row in range(row_tiles):
+        at = slice(row * tile, (row + 1) * tile)
+        turned = lax.dot_general(
+            unit, columns_of(first_tile + row), (((1,), (1,)), ((), ())), preferred_element_type=jnp.float32
+        ).astype(jnp.bfloat16)
+        rows_ref[0, at, :] = turned
+        rows_ref[1, at, : depth // 2] = turned[:, depth // 2 :]
+        rows_ref[1, at, depth // 2 :] = -turned[:, : depth // 2]
+
+    def one(column, _):
+        right = columns_of(column)
+        column_at = pl.ds(pl.multiple_of(column * tile, tile), tile)
+        for row in range(row_tiles):
+            at = slice(row * tile, (row + 1) * tile)
+            global_row = first_tile + row
+
+            @pl.when(global_row != column)
+            def _():
+                kind = jnp.where(column > global_row, 0, 1)
+                sums = jnp.dot(rows_ref[kind, at, :], right, preferred_element_type=jnp.float32) * scale
+                out_ref[0, at, column_at] = sums.astype(out_ref.dtype)
+
+            @pl.when(global_row == column)
+            def _():
+                upper = lax.broadcasted_iota(jnp.int32, (tile, tile), 0) <= lax.broadcasted_iota(
+                    jnp.int32, (tile, tile), 1
+                )
+                real = jnp.dot(rows_ref[0, at, :], right, preferred_element_type=jnp.float32)
+                imag = jnp.dot(rows_ref[1, at, :], right, preferred_element_type=jnp.float32)
+                out_ref[0, at, column_at] = (jnp.where(upper, real, imag) * scale).astype(out_ref.dtype)
+
+        return 0
+
+    lax.fori_loop(0, column_tiles, one, 0)
+
+
+def correlate(pieces, where, held, first, count, channels, row_count, total, tile, scale):
+    sources, _, _, _, inputs = pieces[0][0].shape
+    depth = 2 * sum(array.shape[3] for array, _ in pieces)
+    operands = [array for array, _ in pieces]
+    in_specs = [
+        pl.BlockSpec((sources, 1, 2, array.shape[3], inputs), lambda q, w, start=start: (0, start + q, 0, 0, 0))
+        for array, start in pieces
+    ]
+    aliases = {}
+    if held is not None:
+        aliases = {1 + len(operands): 0}
+        operands.append(held)
+        in_specs.append(pl.BlockSpec(memory_space=pl.ANY))
+    return pl.pallas_call(
+        functools.partial(correlate_kernel, len(pieces), tile, scale),
+        out_shape=jax.ShapeDtypeStruct((channels, row_count, total), jnp.bfloat16),
+        grid_spec=pltpu.PrefetchScalarGridSpec(
+            num_scalar_prefetch=1,
+            grid=(count,),
+            in_specs=in_specs,
+            out_specs=pl.BlockSpec((1, row_count, total), lambda q, w: (first + q, 0, 0)),
+            scratch_shapes=[pltpu.VMEM((2, row_count, depth), jnp.bfloat16)],
+        ),
+        input_output_aliases=aliases,
+        compiler_params=pltpu.CompilerParams(vmem_limit_bytes=VMEM),
+        cost_estimate=pl.CostEstimate(
+            flops=count * 8 * row_count * total * depth,
+            bytes_accessed=count * 16 * total * depth,
+            transcendentals=0,
+        ),
+        name="correlate",
+    )(where, *operands)
+
+
+def chunk_sizes(channels):
+    cuts = sorted({0} | {max(1, channels * part // 16) for part in PARTS})
+    return [stop - start for start, stop in zip(cuts, cuts[1:])]
+
+
+def local_kernels(count, spans, voltages, gains):
+    coarse, inputs, samples = voltages.shape[1:]
+    frames = samples // FINE
+    halves = count // coarse
+    channels = FINE // halves
+    chunks = chunk_sizes(channels)
+    total = count * inputs
+    row_count = total // spans
+    early = max(2 * GROUP, frames * EARLY // 16 // (2 * GROUP) * (2 * GROUP))
+    scale = 1.0 / (spans * frames)
+    where = jnp.stack([lax.axis_index("span")]).astype(jnp.int32)
+    gains = jnp.swapaxes(gains, 2, 3)
+
+    def across(array):
+        return lax.all_to_all(array, "inp", split_axis=0, concat_axis=0, tiled=True)
+
+    def other_spans(array):
+        return [
+            lax.ppermute(array, "span", [(i, i ^ other) for i in range(spans)]) for other in range(1, spans)
+        ]
+
+    outgoing = filter_bank(voltages, gains, halves, [channels], 0, early)
+    outgoing = list(outgoing)
+    outgoing += list(filter_bank(voltages, gains, halves, chunks, early, frames, outgoing))
+    turned = across(outgoing[0])
+    outgoing[1] = gate([outgoing[1]], [turned])[0]
+    first_frames = [turned] + other_spans(turned)
+    held, first = None, 0
+    for index, size in enumerate(chunks):
+        turned = across(outgoing[1 + index])
+        if held is not None:
+            turned, held = gate([turned, held], [])
+        pieces = [(array, first) for array in first_frames]
+        pieces += [(array, 0) for array in [turned] + other_spans(turned)]
+        held = correlate(
+            pieces, where, held, first, size, channels, row_count, total, 2 * LANES, scale
+        )
+        first += size
+    return held
+
+
+def power_of_two(number):
+    return number > 0 and number & (number - 1) == 0
+
+
 def solution(mesh):
+    count, spans = mesh.shape["inp"], mesh.shape["span"]
+
+    def local(voltages, gains):
+        coarse, inputs, samples = voltages.shape[1:]
+        fits = (
+            power_of_two(count)
+            and power_of_two(spans)
+            and count % coarse == 0
+            and power_of_two(count // coarse)
+            and FINE % (count // coarse) == 0
+            and (FINE // (count // coarse)) % 8 == 0
+            and inputs == LANES
+            and samples % (2 * GROUP * FINE) == 0
+            and samples >= 8 * GROUP * FINE
+            and (count * inputs // spans) % (2 * LANES) == 0
+        )
+        if fits:
+            return local_kernels(count, spans, voltages, gains)
+        return local_plain(voltages, gains)
+
     placed = (P(None, "beam", "inp", "span"), P(None, "beam", "inp", None))
     return jax.shard_map(
         local,

time: 868 us -> 412 us (0.47)
  local copies, waits for them, and re-layouts: 238 us -> 0 us
  blocking collectives: 370 us -> 205 us
  matrix products: 155 us -> 0 us
  Pallas kernels: 0 us -> 94.6 us
  waiting for transfers between devices: 50 us -> 94.5 us
  other arithmetic: 37.4 us -> 0 us
  starting transfers between devices: 0.01 us -> 16.7 us
  between operations: 14.2 us -> 0.03 us
    all_to_all x1, blocking collectives: 370 us -> 205 us  [across(): return lax.all_to_all(array, 'inp', split_axis=0, concat_axis=0, tiled=True)]
    dot_general x4 -> x0, matrix products: 155 us -> none  [the longest x1 44.4 us: local(): jnp.einsum('atcnmp,atpbk->bcknm', stacked, filter_high, preferred_element...]
    another operation x7 -> x0, local copies, waits for them, and re-layouts: 148 us -> none  [the longest x4 123 us: local(): jnp.stack([padded[..., tap_index * FINE:tap_index * FINE + samples] for t...]
    pallas_call x0 -> x8, Pallas kernels: none -> 94.6 us  [the longest x3 60.9 us: correlate(): pl.pallas_call(functools.partial(correlate_kernel, len(pieces), tile, sca...]
    all_to_all x0 -> x3, waiting for transfers between devices: none -> 75.4 us  [across(): return lax.all_to_all(array, 'inp', split_axis=0, concat_axis=0, tiled=True)]
    all_gather x1 -> x0, waiting for transfers between devices: 50 us -> none  [local(): frame_piece = lax.all_gather(turned, 'span', axis=3, tiled=True)]
    slice x2 -> x0, local copies, waits for them, and re-layouts: 32.5 us -> none  [the longest x1 32.5 us: local(): padded[..., tap_index * FINE:tap_index * FINE + samples]]
    squeeze x2 -> x0, local copies, waits for them, and re-layouts: 29.9 us -> none  [the longest x1 22.5 us: local(): left_all = jnp.concatenate([frame_piece[0], frame_piece[1]], axis=-1)]
  transfers between devices with their start and end apart: 1 -> 7, of which waited for: 1 -> 6; matrix products, arithmetic and copies ran while one was open for 0% -> 0% of each run, Pallas kernels for 0% -> 20%
where the time goes in v3:
time: 412 us; the launch traced here: 411 us
  blocking collectives  205 us (50%)
  Pallas kernels  94.6 us (23%)
  waiting for transfers between devices  94.5 us (23%)
  starting transfers between devices  16.7 us (4%)
    all_to_all x1, blocking collectives, across(): return lax.all_to_all(array, 'inp', split_axis=0, concat_axis=0, tiled=True)  205 us
    all_to_all x3, waiting for transfers between devices, across(): return lax.all_to_all(array, 'inp', split_axis=0, concat_axis=0, tiled=True)  75.4 us
    pallas_call x3, Pallas kernels, correlate(): pl.pallas_call(functools.partial(correlate_kernel, len(pieces), tile, sca...  60.9 us
    pallas_call x2, Pallas kernels, filter_bank(): pl.pallas_call(functools.partial(filter_kernel, halves, chunks, first_fra...  33.6 us
    ppermute x4, waiting for transfers between devices, other_spans(): lax.ppermute(array, 'span', [(i, i ^ other) for i in range(spans)])  19.1 us
    all_to_all x3, starting transfers between devices, across(): return lax.all_to_all(array, 'inp', split_axis=0, concat_axis=0, tiled=True)  16.1 us
  transfers between devices with their start and end apart: 7, of which 6 were waited for; matrix products, arithmetic and copies ran while one was open for 0% of the time, Pallas kernels for 20%

profile of v3, /device:TPU:0, one launch (start us, length us, event | category | flops | bytes accessed | tf_op | source)
XLA Modules:
  0.0 411.1 jit_solution(8626604228434161375)
XLA Ops:
  0.0 6.1 %filter_bank.2.rest_0_ = bf16[8,16,2,32,128]{4,3,2,1,0:T(8,128)(2,1)} custom-call(bf16[2,4,128,8192]{3,2,1,0:T(8,128)(2,1)} %volt_ref.3, f32[2,4,32,128]{3,2,1,0:T(8,128)} %bitcast.2, bf16[512,768]{1,0:T(8,128)(2,1)} %constant.6.clone.table_ref), custom_call_target="tpu_custom_call" | custom-call | flops 3221225472 | bytes 8388608 | tf_op jit(solution)/shard_map/filter_bank/pallas_call | solution.py:179
  6.1 7.2 %all-to-all-start = ((bf16[8,16,2,32,128]{4,3,2,1,0:T(8,128)(2,1)}), bf16[8,16,2,32,128]{4,3,2,1,0:T(8,128)(2,1)}, u32[]{:S(2)}, u32[]{:S(2)}) async-start(bf16[8,16,2,32,128]{4,3,2,1,0:T(8,128)(2,1)} %filter_bank.2.rest_0_), calls=%async_computation | async-start | bytes 4194304 | tf_op jit(solution)/shard_map/all_to_all | solution.py:339
  13.4 27.5 %filter_bank.3 = (bf16[8,10,2,224,128]{4,3,2,1,0:T(8,128)(2,1)}, bf16[8,5,2,224,128]{4,3,2,1,0:T(8,128)(2,1)}, bf16[8,1,2,224,128]{4,3,2,1,0:T(8,128)(2,1)}) custom-call(bf16[2,4,128,8192]{3,2,1,0:T(8,128)(2,1)} %volt_ref.3, f32[2,4,32,128]{3,2,1,0:T(8,128)} %bitcast.3, bf16[512,768]{1,0:T(8,128)(2,1)} %constant.6.clone.table_ref, ...), custom_call_target="tpu_custom_call" | custom-call | flops 22548578304 | bytes 58720256 | tf_op jit(solution)/shard_map/filter_bank/pallas_call | solution.py:179
  40.9 20.8 %all-to-all-done.__1_.rest_0_ = bf16[8,16,2,32,128]{4,3,2,1,0:T(8,128)(2,1)} async-done(((bf16[8,16,2,32,128]{4,3,2,1,0:T(8,128)(2,1)}), bf16[8,16,2,32,128]{4,3,2,1,0:T(8,128)(2,1)}, u32[]{:S(2)}, u32[]{:S(2)}) %all-to-all-start) | async-done | bytes 2097184 | tf_op jit(solution)/shard_map/all_to_all | solution.py:339
  61.7 205.5 %all_to_all.20.rest_2_ = bf16[8,10,2,224,128]{4,3,2,1,0:T(8,128)(2,1)} all-to-all(bf16[8,10,2,224,128]{4,3,2,1,0:T(8,128)(2,1)} %gate.3), channel_id=1, replica_groups=mesh['beam'=2,'inp'=8,'span'=2] {'inp'}, dimensions={0} | all-to-all | bytes 18350080 | tf_op jit(solution)/shard_map/all_to_all | solution.py:339
  267.2 0.0 collective-permute-start.1
  267.2 4.6 %all-to-all-start.2 = ((bf16[8,5,2,224,128]{4,3,2,1,0:T(8,128)(2,1)}), bf16[8,5,2,224,128]{4,3,2,1,0:T(8,128)(2,1)}, u32[]{:S(2)}, u32[]{:S(2)}) async-start(bf16[8,5,2,224,128]{4,3,2,1,0:T(8,128)(2,1)} %get-tuple-element.13), calls=%async_computation.2 | async-start | bytes 9175040 | tf_op jit(solution)/shard_map/all_to_all | solution.py:339
  271.8 0.6 collective-permute-start
  272.4 12.4 %collective-permute-done.rest_1_ = bf16[8,16,2,32,128]{4,3,2,1,0:T(8,128)(2,1)} collective-permute-done((bf16[8,16,2,32,128]{4,3,2,1,0:T(8,128)(2,1)}, bf16[8,16,2,32,128]{4,3,2,1,0:T(8,128)(2,1)}, u32[]{:S(2)}, u32[]{:S(2)}) %collective-permute-start) | collective-permute-done | bytes 2097184 | tf_op jit(solution)/shard_map/ppermute | solution.py:343
  284.8 0.0 collective-permute-done.1.rest_3_
  284.8 35.9 %correlate.3.__1_ = bf16[16,512,1024]{2,1,0:T(8,128)(2,1)} custom-call(s32[1]{0:T(128)} %bitcast.where_ref, bf16[8,16,2,32,128]{4,3,2,1,0:T(8,128)(2,1)} %all-to-all-done.__1_.rest_0_, bf16[8,16,2,32,128]{4,3,2,1,0:T(8,128)(2,1)} %collective-permute-done.rest_1_, bf16[8,10,2,224,128]{4,3,2,1,0:T(8,128)(2,1)} %all_to_all.20.rest_2_, ...), custom_call_target="tpu_custom_call" | custom-call | flops 42949672960 | bytes 167772160 | tf_op jit(solution)/shard_map/correlate/pallas_call | solution.py:299
  320.6 53.7 %all-to-all-done.2.__0_ = bf16[8,5,2,224,128]{4,3,2,1,0:T(8,128)(2,1)} async-done(((bf16[8,5,2,224,128]{4,3,2,1,0:T(8,128)(2,1)}), bf16[8,5,2,224,128]{4,3,2,1,0:T(8,128)(2,1)}, u32[]{:S(2)}, u32[]{:S(2)}) %all-to-all-start.2) | async-done | bytes 4587552 | tf_op jit(solution)/shard_map/all_to_all | solution.py:339
  374.3 0.0 collective-permute-start.2
  374.3 4.2 %all-to-all-start.1 = ((bf16[8,1,2,224,128]{4,3,2,1,0:T(8,128)(2,1)}), bf16[8,1,2,224,128]{4,3,2,1,0:T(8,128)(2,1)}, u32[]{:S(2)}, u32[]{:S(2)}) async-start(bf16[8,1,2,224,128]{4,3,2,1,0:T(8,128)(2,1)} %get-tuple-element.12), calls=%async_computation.1 | async-start | bytes 1835008 | tf_op jit(solution)/shard_map/all_to_all | solution.py:339
  378.6 3.8 collective-permute-done.2.rest_3_
  382.4 19.2 %correlate.4.__1_ = bf16[16,512,1024]{2,1,0:T(8,128)(2,1)} custom-call(s32[1]{0:T(128)} %bitcast.where_ref, bf16[8,16,2,32,128]{4,3,2,1,0:T(8,128)(2,1)} %all-to-all-done.__1_.rest_0_, bf16[8,16,2,32,128]{4,3,2,1,0:T(8,128)(2,1)} %collective-permute-done.rest_1_, ...), custom_call_target="tpu_custom_call", output_to_operand_aliasing={{}: (5, {})} | custom-call | flops 21474836480 | bytes 83886080 | tf_op jit(solution)/shard_map/correlate/pallas_call | solution.py:299
  401.6 0.9 all-to-all-done.1.__0_
  402.5 0.0 collective-permute-start.3
  402.5 2.8 collective-permute-done.3.rest_3_
  405.3 5.9 %correlate.5 = bf16[16,512,1024]{2,1,0:T(8,128)(2,1)} custom-call(s32[1]{0:T(128)} %bitcast.where_ref, bf16[8,16,2,32,128]{4,3,2,1,0:T(8,128)(2,1)} %all-to-all-done.__1_.rest_0_, bf16[8,16,2,32,128]{4,3,2,1,0:T(8,128)(2,1)} %collective-permute-done.rest_1_, bf16[8,1,2,224,128]{4,3,2,1,0:T(8,128)(2,1)} %get-tuple-element.17.rest_2_, ...), custom_call_target="tpu_custom_call", output_to_operand_aliasing={{}: (5, {})} | custom-call | flops 4294967296 | bytes 16777216 | tf_op jit(solution)/shard_map/correlate/pallas_call | solution.py:299
  (3 shorter events, 0.0 us)
Async XLA Ops:
  6.1 55.6 %all-to-all-start = ((bf16[8,16,2,32,128]{4,3,2,1,0:T(8,128)(2,1)}), bf16[8,16,2,32,128]{4,3,2,1,0:T(8,128)(2,1)}, u32[]{:S(2)}, u32[]{:S(2)}) async-start(bf16[8,16,2,32,128]{4,3,2,1,0:T(8,128)(2,1)} %filter_bank.2.rest_0_), calls=%async_computation | async-start | bytes 4194304 | tf_op jit(solution)/shard_map/all_to_all | solution.py:339
  267.2 17.6 %collective-permute-start.1 = (bf16[8,10,2,224,128]{4,3,2,1,0:T(8,128)(2,1)}, bf16[8,10,2,224,128]{4,3,2,1,0:T(8,128)(2,1)}, u32[]{:S(2)}, u32[]{:S(2)}) collective-permute-start(bf16[8,10,2,224,128]{4,3,2,1,0:T(8,128)(2,1)} %all_to_all.20.rest_2_), channel_id=1, source_target_pairs={{0,1},{1,0},{2,3},{3,2},{4,5},{5,4},{6,7},{7,6},{8,9},{9,8},{10,11... | collective-permute-start | bytes 27525128 | tf_op jit(solution)/shard_map/ppermute | solution.py:343
  267.2 107.2 %all-to-all-start.2 = ((bf16[8,5,2,224,128]{4,3,2,1,0:T(8,128)(2,1)}), bf16[8,5,2,224,128]{4,3,2,1,0:T(8,128)(2,1)}, u32[]{:S(2)}, u32[]{:S(2)}) async-start(bf16[8,5,2,224,128]{4,3,2,1,0:T(8,128)(2,1)} %get-tuple-element.13), calls=%async_computation.2 | async-start | bytes 9175040 | tf_op jit(solution)/shard_map/all_to_all | solution.py:339
  271.8 13.0 %collective-permute-start = (bf16[8,16,2,32,128]{4,3,2,1,0:T(8,128)(2,1)}, bf16[8,16,2,32,128]{4,3,2,1,0:T(8,128)(2,1)}, u32[]{:S(2)}, u32[]{:S(2)}) collective-permute-start(bf16[8,16,2,32,128]{4,3,2,1,0:T(8,128)(2,1)} %all-to-all-done.__1_.rest_0_), channel_id=1, source_target_pairs={{0,1},{1,0},{2,3},{3,2},{4,5},{5,4},{6,7},{7,6},{8,9},{9,8},{10,11... | collective-permute-start | bytes 6291464 | tf_op jit(solution)/shard_map/ppermute | solution.py:343
  374.3 8.1 %collective-permute-start.2 = (bf16[8,5,2,224,128]{4,3,2,1,0:T(8,128)(2,1)}, bf16[8,5,2,224,128]{4,3,2,1,0:T(8,128)(2,1)}, u32[]{:S(2)}, u32[]{:S(2)}) collective-permute-start(bf16[8,5,2,224,128]{4,3,2,1,0:T(8,128)(2,1)} %get-tuple-element.15.rest_2_), channel_id=1, source_target_pairs={{0,1},{1,0},{2,3},{3,2},{4,5},{5,4},{6,7},{7,6},{8,9},{9,8},{10,11... | collective-permute-start | bytes 13762568 | tf_op jit(solution)/shard_map/ppermute | solution.py:343
  374.3 28.1 %all-to-all-start.1 = ((bf16[8,1,2,224,128]{4,3,2,1,0:T(8,128)(2,1)}), bf16[8,1,2,224,128]{4,3,2,1,0:T(8,128)(2,1)}, u32[]{:S(2)}, u32[]{:S(2)}) async-start(bf16[8,1,2,224,128]{4,3,2,1,0:T(8,128)(2,1)} %get-tuple-element.12), calls=%async_computation.1 | async-start | bytes 1835008 | tf_op jit(solution)/shard_map/all_to_all | solution.py:339
  402.5 2.8 collective-permute-start.3

commit v4 on v3

--- a/solution.py
+++ b/solution.py
@@ -15,8 +15,9 @@
 LANES = 128
 GROUP = 8
 VMEM = 64 * 1024 * 1024 - 64 * 1024
-EARLY = 2
-PARTS = (10, 15, 16)
+UNROLL = 4
+EARLY = 1
+PARTS = (13, 16)
 
 
 def prototype(tap_count, fine_count):
@@ -164,7 +165,7 @@
         one(pair, True)
         return 0
 
-    lax.fori_loop(0, whole, loop, 0)
+    lax.fori_loop(0, whole, loop, 0, unroll=UNROLL)
     for pair in range(whole, pairs):
         one(pair, False)
 
@@ -228,7 +229,7 @@
     out_ref, rows_ref = rest[-2:]
     inputs = blocks[0].shape[4]
     row_count, total = out_ref.shape[1:]
-    depth = rows_ref.shape[2]
+    depth = rows_ref.shape[1]
     per_tile = tile // inputs
     row_tiles, column_tiles = row_count // tile, total // tile
 
@@ -248,39 +249,36 @@
     )
     unit = jnp.where(unit, 1.0, 0.0).astype(jnp.bfloat16)
     for row in range(row_tiles):
-        at = slice(row * tile, (row + 1) * tile)
         turned = lax.dot_general(
             unit, columns_of(first_tile + row), (((1,), (1,)), ((), ())), preferred_element_type=jnp.float32
         ).astype(jnp.bfloat16)
-        rows_ref[0, at, :] = turned
-        rows_ref[1, at, : depth // 2] = turned[:, depth // 2 :]
-        rows_ref[1, at, depth // 2 :] = -turned[:, : depth // 2]
-
-    def one(column, _):
-        right = columns_of(column)
+        imag_at = slice(row * tile, (row + 1) * tile)
+        real_at = slice(row_count + row * tile, row_count + (row + 1) * tile)
+        rows_ref[real_at, :] = turned
+        rows_ref[imag_at, : depth // 2] = turned[:, depth // 2 :]
+        rows_ref[imag_at, depth // 2 :] = -turned[:, : depth // 2]
+
+    def product(start, size, column):
+        left = rows_ref[pl.ds(pl.multiple_of(start, tile), size), :]
+        return jnp.dot(left, columns_of(column), preferred_element_type=jnp.float32) * scale
+
+    def outside(index, _):
+        column = jnp.where(index < first_tile, index, index + row_tiles)
         column_at = pl.ds(pl.multiple_of(column * tile, tile), tile)
-        for row in range(row_tiles):
-            at = slice(row * tile, (row + 1) * tile)
-            global_row = first_tile + row
-
-            @pl.when(global_row != column)
-            def _():
-                kind = jnp.where(column > global_row, 0, 1)
-                sums = jnp.dot(rows_ref[kind, at, :], right, preferred_element_type=jnp.float32) * scale
-                out_ref[0, at, column_at] = sums.astype(out_ref.dtype)
-
-            @pl.when(global_row == column)
-            def _():
-                upper = lax.broadcasted_iota(jnp.int32, (tile, tile), 0) <= lax.broadcasted_iota(
-                    jnp.int32, (tile, tile), 1
-                )
-                real = jnp.dot(rows_ref[0, at, :], right, preferred_element_type=jnp.float32)
-                imag = jnp.dot(rows_ref[1, at, :], right, preferred_element_type=jnp.float32)
-                out_ref[0, at, column_at] = (jnp.where(upper, real, imag) * scale).astype(out_ref.dtype)
-
+        start = jnp.where(index < first_tile, 0, row_count)
+        out_ref[0, :, column_at] = product(start, row_count, column).astype(out_ref.dtype)
         return 0
 
-    lax.fori_loop(0, column_tiles, one, 0)
+    lax.fori_loop(0, column_tiles - row_tiles, outside, 0, unroll=True)
+    upper = lax.broadcasted_iota(jnp.int32, (tile, tile), 0) <= lax.broadcasted_iota(jnp.int32, (tile, tile), 1)
+    column_at = pl.ds(pl.multiple_of(first_tile * tile, tile), tile)
+    sums = product(0, 3 * tile, first_tile)
+    out_ref[0, :tile, column_at] = jnp.where(upper, sums[2 * tile :], sums[:tile]).astype(out_ref.dtype)
+    out_ref[0, tile:, column_at] = sums[tile : 2 * tile].astype(out_ref.dtype)
+    column_at = pl.ds(pl.multiple_of((first_tile + 1) * tile, tile), tile)
+    sums = product(tile, 3 * tile, first_tile + 1)
+    out_ref[0, :tile, column_at] = sums[tile : 2 * tile].astype(out_ref.dtype)
+    out_ref[0, tile:, column_at] = jnp.where(upper, sums[2 * tile :], sums[:tile]).astype(out_ref.dtype)
 
 
 def correlate(pieces, where, held, first, count, channels, row_count, total, tile, scale):
@@ -304,7 +302,7 @@
             grid=(count,),
             in_specs=in_specs,
             out_specs=pl.BlockSpec((1, row_count, total), lambda q, w: (first + q, 0, 0)),
-            scratch_shapes=[pltpu.VMEM((2, row_count, depth), jnp.bfloat16)],
+            scratch_shapes=[pltpu.VMEM((2 * row_count, depth), jnp.bfloat16)],
         ),
         input_output_aliases=aliases,
         compiler_params=pltpu.CompilerParams(vmem_limit_bytes=VMEM),
@@ -382,7 +380,7 @@
             and inputs == LANES
             and samples % (2 * GROUP * FINE) == 0
             and samples >= 8 * GROUP * FINE
-            and (count * inputs // spans) % (2 * LANES) == 0
+            and count * inputs // spans == 4 * LANES
         )
         if fits:
             return local_kernels(count, spans, voltages, gains)

time: 412 us -> 407 us (0.988)
  blocking collectives: 205 us -> 283 us
  waiting for transfers between devices: 94.5 us -> 47.4 us
  Pallas kernels: 94.6 us -> 64.3 us
  starting transfers between devices: 16.7 us -> 12.2 us
    all_to_all x1, blocking collectives: 205 us -> 283 us  [across(): return lax.all_to_all(array, 'inp', split_axis=0, concat_axis=0, tiled=True)]
    all_to_all x3 -> x2, waiting for transfers between devices: 75.4 us -> 25.3 us  [across(): return lax.all_to_all(array, 'inp', split_axis=0, concat_axis=0, tiled=True)]
    pallas_call x3 -> x2, Pallas kernels: 60.9 us -> 37.8 us  [correlate(): pl.pallas_call(functools.partial(correlate_kernel, len(pieces), tile, sca...]
    pallas_call x2, Pallas kernels: 33.6 us -> 26.6 us  [filter_bank(): pl.pallas_call(functools.partial(filter_kernel, halves, chunks, first_fra...]
    all_to_all x3 -> x2, starting transfers between devices: 16.1 us -> 11.7 us  [across(): return lax.all_to_all(array, 'inp', split_axis=0, concat_axis=0, tiled=True)]
    ppermute x4 -> x3, waiting for transfers between devices: 19.1 us -> 22 us  [other_spans(): lax.ppermute(array, 'span', [(i, i ^ other) for i in range(spans)])]
  transfers between devices with their start and end apart: 7 -> 5, of which waited for: 6 -> 4; matrix products, arithmetic and copies ran while one was open for 0% -> 0% of each run, Pallas kernels for 20% -> 13%
where the time goes in v4:
time: 407 us
  blocking collectives  283 us (70%)
  Pallas kernels  64.3 us (16%)
  waiting for transfers between devices  47.4 us (12%)
  starting transfers between devices  12.2 us (3%)
    all_to_all x1, blocking collectives, across(): return lax.all_to_all(array, 'inp', split_axis=0, concat_axis=0, tiled=True)  283 us
    pallas_call x2, Pallas kernels, correlate(): pl.pallas_call(functools.partial(correlate_kernel, len(pieces), tile, sca...  37.8 us
    pallas_call x2, Pallas kernels, filter_bank(): pl.pallas_call(functools.partial(filter_kernel, halves, chunks, first_fra...  26.6 us
    all_to_all x2, waiting for transfers between devices, across(): return lax.all_to_all(array, 'inp', split_axis=0, concat_axis=0, tiled=True)  25.3 us
    ppermute x3, waiting for transfers between devices, other_spans(): lax.ppermute(array, 'span', [(i, i ^ other) for i in range(spans)])  22 us
    all_to_all x2, starting transfers between devices, across(): return lax.all_to_all(array, 'inp', split_axis=0, concat_axis=0, tiled=True)  11.7 us
  transfers between devices with their start and end apart: 5, of which 4 were waited for; matrix products, arithmetic and copies ran while one was open for 0% of the time, Pallas kernels for 13%

profile of v4, /device:TPU:0, one launch (start us, length us, event | category | flops | bytes accessed | tf_op | source)
XLA Modules:
  0.0 406.7 jit_solution(5695880460793017565)
XLA Ops:
  0.0 4.5 %filter_bank.2.rest_0_ = bf16[8,16,2,16,128]{4,3,2,1,0:T(8,128)(2,1)} custom-call(bf16[2,4,128,8192]{3,2,1,0:T(8,128)(2,1)} %volt_ref.3, f32[2,4,32,128]{3,2,1,0:T(8,128)} %bitcast.2, bf16[512,768]{1,0:T(8,128)(2,1)} %constant.6.clone.table_ref), custom_call_target="tpu_custom_call" | custom-call | flops 1610612736 | bytes 4194304 | tf_op jit(solution)/shard_map/filter_bank/pallas_call | solution.py:180
  4.5 7.3 %all-to-all-start = ((bf16[8,16,2,16,128]{4,3,2,1,0:T(8,128)(2,1)}), bf16[8,16,2,16,128]{4,3,2,1,0:T(8,128)(2,1)}, u32[]{:S(2)}, u32[]{:S(2)}) async-start(bf16[8,16,2,16,128]{4,3,2,1,0:T(8,128)(2,1)} %filter_bank.2.rest_0_), calls=%async_computation | async-start | bytes 2097152 | tf_op jit(solution)/shard_map/all_to_all | solution.py:337
  11.8 22.1 %filter_bank.3 = (bf16[8,13,2,240,128]{4,3,2,1,0:T(8,128)(2,1)}, bf16[8,3,2,240,128]{4,3,2,1,0:T(8,128)(2,1)}) custom-call(bf16[2,4,128,8192]{3,2,1,0:T(8,128)(2,1)} %volt_ref.3, f32[2,4,32,128]{3,2,1,0:T(8,128)} %bitcast.3, bf16[512,768]{1,0:T(8,128)(2,1)} %constant.6.clone.table_ref, bf16[8,16,2,16,128]{4,3,2,1,0:T(8,128)(2,1)} %filter_bank.2.rest_0_), custom_call_target="tpu_custom_call" | custom-call | flops 24159191040 | bytes 62914560 | tf_op jit(solution)/shard_map/filter_bank/pallas_call | solution.py:180
  33.8 3.8 all-to-all-done.__1_.rest_0_
  37.6 282.8 %all_to_all.15.rest_2_ = bf16[8,13,2,240,128]{4,3,2,1,0:T(8,128)(2,1)} all-to-all(bf16[8,13,2,240,128]{4,3,2,1,0:T(8,128)(2,1)} %gate.2), channel_id=1, replica_groups=mesh['beam'=2,'inp'=8,'span'=2] {'inp'}, dimensions={0} | all-to-all | bytes 25559040 | tf_op jit(solution)/shard_map/all_to_all | solution.py:337
  320.5 0.0 collective-permute-start.1
  320.5 0.5 collective-permute-start
  321.0 4.4 %all-to-all-start.1 = ((bf16[8,3,2,240,128]{4,3,2,1,0:T(8,128)(2,1)}), bf16[8,3,2,240,128]{4,3,2,1,0:T(8,128)(2,1)}, u32[]{:S(2)}, u32[]{:S(2)}) async-start(bf16[8,3,2,240,128]{4,3,2,1,0:T(8,128)(2,1)} %get-tuple-element.9), calls=%async_computation.1 | async-start | bytes 5898240 | tf_op jit(solution)/shard_map/all_to_all | solution.py:337
  325.4 16.3 %collective-permute-done.rest_1_ = bf16[8,16,2,16,128]{4,3,2,1,0:T(8,128)(2,1)} collective-permute-done((bf16[8,16,2,16,128]{4,3,2,1,0:T(8,128)(2,1)}, bf16[8,16,2,16,128]{4,3,2,1,0:T(8,128)(2,1)}, u32[]{:S(2)}, u32[]{:S(2)}) %collective-permute-start) | collective-permute-done | bytes 1048608 | tf_op jit(solution)/shard_map/ppermute | solution.py:341
  341.8 0.0 collective-permute-done.1.rest_3_
  341.8 29.1 %correlate.2.__1_ = bf16[16,512,1024]{2,1,0:T(8,128)(2,1)} custom-call(s32[1]{0:T(128)} %bitcast.where_ref, bf16[8,16,2,16,128]{4,3,2,1,0:T(8,128)(2,1)} %all-to-all-done.__1_.rest_0_, bf16[8,16,2,16,128]{4,3,2,1,0:T(8,128)(2,1)} %collective-permute-done.rest_1_, bf16[8,13,2,240,128]{4,3,2,1,0:T(8,128)(2,1)} %all_to_all.15.rest_2_, ...), custom_call_target="tpu_custom_call" | custom-call | flops 55834574848 | bytes 218103808 | tf_op jit(solution)/shard_map/correlate/pallas_call | solution.py:297
  370.9 21.5 %all-to-all-done.1.__0_ = bf16[8,3,2,240,128]{4,3,2,1,0:T(8,128)(2,1)} async-done(((bf16[8,3,2,240,128]{4,3,2,1,0:T(8,128)(2,1)}), bf16[8,3,2,240,128]{4,3,2,1,0:T(8,128)(2,1)}, u32[]{:S(2)}, u32[]{:S(2)}) %all-to-all-start.1) | async-done | bytes 2949152 | tf_op jit(solution)/shard_map/all_to_all | solution.py:337
  392.4 0.0 collective-permute-start.2
  392.4 5.7 %collective-permute-done.2.rest_3_ = bf16[8,3,2,240,128]{4,3,2,1,0:T(8,128)(2,1)} collective-permute-done((bf16[8,3,2,240,128]{4,3,2,1,0:T(8,128)(2,1)}, bf16[8,3,2,240,128]{4,3,2,1,0:T(8,128)(2,1)}, u32[]{:S(2)}, u32[]{:S(2)}) %collective-permute-start.2) | collective-permute-done | bytes 2949152 | tf_op jit(solution)/shard_map/ppermute | solution.py:341
  398.1 8.6 %correlate.3 = bf16[16,512,1024]{2,1,0:T(8,128)(2,1)} custom-call(s32[1]{0:T(128)} %bitcast.where_ref, bf16[8,16,2,16,128]{4,3,2,1,0:T(8,128)(2,1)} %all-to-all-done.__1_.rest_0_, bf16[8,16,2,16,128]{4,3,2,1,0:T(8,128)(2,1)} %collective-permute-done.rest_1_, bf16[8,3,2,240,128]{4,3,2,1,0:T(8,128)(2,1)} %get-tuple-element.11.rest_2_, ...), custom_call_target="tpu_custom_call", output_to_operand_aliasing={{}: (5, {})} | custom-call | flops 12884901888 | bytes 50331648 | tf_op jit(solution)/shard_map/correlate/pallas_call | solution.py:297
  (2 shorter events, 0.0 us)
Async XLA Ops:
  4.5 33.1 %all-to-all-start = ((bf16[8,16,2,16,128]{4,3,2,1,0:T(8,128)(2,1)}), bf16[8,16,2,16,128]{4,3,2,1,0:T(8,128)(2,1)}, u32[]{:S(2)}, u32[]{:S(2)}) async-start(bf16[8,16,2,16,128]{4,3,2,1,0:T(8,128)(2,1)} %filter_bank.2.rest_0_), calls=%async_computation | async-start | bytes 2097152 | tf_op jit(solution)/shard_map/all_to_all | solution.py:337
  320.5 21.3 %collective-permute-start.1 = (bf16[8,13,2,240,128]{4,3,2,1,0:T(8,128)(2,1)}, bf16[8,13,2,240,128]{4,3,2,1,0:T(8,128)(2,1)}, u32[]{:S(2)}, u32[]{:S(2)}) collective-permute-start(bf16[8,13,2,240,128]{4,3,2,1,0:T(8,128)(2,1)} %all_to_all.15.rest_2_), channel_id=1, source_target_pairs={{0,1},{1,0},{2,3},{3,2},{4,5},{5,4},{6,7},{7,6},{8,9},{9,8},{10,11... | collective-permute-start | bytes 38338568 | tf_op jit(solution)/shard_map/ppermute | solution.py:341
  320.5 21.3 %collective-permute-start = (bf16[8,16,2,16,128]{4,3,2,1,0:T(8,128)(2,1)}, bf16[8,16,2,16,128]{4,3,2,1,0:T(8,128)(2,1)}, u32[]{:S(2)}, u32[]{:S(2)}) collective-permute-start(bf16[8,16,2,16,128]{4,3,2,1,0:T(8,128)(2,1)} %all-to-all-done.__1_.rest_0_), channel_id=1, source_target_pairs={{0,1},{1,0},{2,3},{3,2},{4,5},{5,4},{6,7},{7,6},{8,9},{9,8},{10,11... | collective-permute-start | bytes 3145736 | tf_op jit(solution)/shard_map/ppermute | solution.py:341
  321.0 71.4 %all-to-all-start.1 = ((bf16[8,3,2,240,128]{4,3,2,1,0:T(8,128)(2,1)}), bf16[8,3,2,240,128]{4,3,2,1,0:T(8,128)(2,1)}, u32[]{:S(2)}, u32[]{:S(2)}) async-start(bf16[8,3,2,240,128]{4,3,2,1,0:T(8,128)(2,1)} %get-tuple-element.9), calls=%async_computation.1 | async-start | bytes 5898240 | tf_op jit(solution)/shard_map/all_to_all | solution.py:337
  392.4 5.7 %collective-permute-start.2 = (bf16[8,3,2,240,128]{4,3,2,1,0:T(8,128)(2,1)}, bf16[8,3,2,240,128]{4,3,2,1,0:T(8,128)(2,1)}, u32[]{:S(2)}, u32[]{:S(2)}) collective-permute-start(bf16[8,3,2,240,128]{4,3,2,1,0:T(8,128)(2,1)} %get-tuple-element.11.rest_2_), channel_id=1, source_target_pairs={{0,1},{1,0},{2,3},{3,2},{4,5},{5,4},{6,7},{7,6},{8,9},{9,8},{10,11... | collective-permute-start | bytes 8847368 | tf_op jit(solution)/shard_map/ppermute | solution.py:341

commit v5 on v4

--- a/solution.py
+++ b/solution.py
@@ -17,7 +17,7 @@
 VMEM = 64 * 1024 * 1024 - 64 * 1024
 UNROLL = 4
 EARLY = 1
-PARTS = (13, 16)
+PARTS = (14, 16)
 
 
 def prototype(tap_count, fine_count):
@@ -249,9 +249,7 @@
     )
     unit = jnp.where(unit, 1.0, 0.0).astype(jnp.bfloat16)
     for row in range(row_tiles):
-        turned = lax.dot_general(
-            unit, columns_of(first_tile + row), (((1,), (1,)), ((), ())), preferred_element_type=jnp.float32
-        ).astype(jnp.bfloat16)
+        turned = columns_of(first_tile + row).T
         imag_at = slice(row * tile, (row + 1) * tile)
         real_at = slice(row_count + row * tile, row_count + (row + 1) * tile)
         rows_ref[real_at, :] = turned
@@ -262,14 +260,15 @@
         left = rows_ref[pl.ds(pl.multiple_of(start, tile), size), :]
         return jnp.dot(left, columns_of(column), preferred_element_type=jnp.float32) * scale
 
-    def outside(index, _):
-        column = jnp.where(index < first_tile, index, index + row_tiles)
-        column_at = pl.ds(pl.multiple_of(column * tile, tile), tile)
-        start = jnp.where(index < first_tile, 0, row_count)
-        out_ref[0, :, column_at] = product(start, row_count, column).astype(out_ref.dtype)
-        return 0
-
-    lax.fori_loop(0, column_tiles - row_tiles, outside, 0, unroll=True)
+    before = first_tile > 0
+    start = jnp.where(before, 0, row_count)
+    first_column = jnp.where(before, 0, row_tiles)
+    width = total - row_count
+    right = jnp.concatenate([columns_of(first_column + index) for index in range(width // tile)], axis=1)
+    column_at = pl.ds(pl.multiple_of(first_column * tile, tile), width)
+    left = rows_ref[pl.ds(pl.multiple_of(start, tile), row_count), :]
+    sums = jnp.dot(left, right, preferred_element_type=jnp.float32) * scale
+    out_ref[0, :, column_at] = sums.astype(out_ref.dtype)
     upper = lax.broadcasted_iota(jnp.int32, (tile, tile), 0) <= lax.broadcasted_iota(jnp.int32, (tile, tile), 1)
     column_at = pl.ds(pl.multiple_of(first_tile * tile, tile), tile)
     sums = product(0, 3 * tile, first_tile)

time: 407 us -> 405 us (level)
  waiting for transfers between devices: 47.4 us -> 25.6 us
  blocking collectives: 283 us -> 304 us
    all_to_all x2, waiting for transfers between devices: 25.3 us -> 3.77 us  [across(): return lax.all_to_all(array, 'inp', split_axis=0, concat_axis=0, tiled=True)]
    all_to_all x1, blocking collectives: 283 us -> 304 us  [across(): return lax.all_to_all(array, 'inp', split_axis=0, concat_axis=0, tiled=True)]
  transfers between devices with their start and end apart: 5 -> 5, of which waited for: 4 -> 3; matrix products, arithmetic and copies ran while one was open for 0% -> 0% of each run, Pallas kernels for 13% -> 13%
where the time goes in v5:
time: 405 us; the launch traced here: 404 us
  blocking collectives  304 us (75%)
  Pallas kernels  61.2 us (15%)
  waiting for transfers between devices  25.6 us (6%)
  starting transfers between devices  12.4 us (3%)
    all_to_all x1, blocking collectives, across(): return lax.all_to_all(array, 'inp', split_axis=0, concat_axis=0, tiled=True)  304 us
    pallas_call x2, Pallas kernels, correlate(): pl.pallas_call(functools.partial(correlate_kernel, len(pieces), tile, sca...  34.5 us
    pallas_call x2, Pallas kernels, filter_bank(): pl.pallas_call(functools.partial(filter_kernel, halves, chunks, first_fra...  26.6 us
    ppermute x3, waiting for transfers between devices, other_spans(): lax.ppermute(array, 'span', [(i, i ^ other) for i in range(spans)])  21.9 us
    all_to_all x2, starting transfers between devices, across(): return lax.all_to_all(array, 'inp', split_axis=0, concat_axis=0, tiled=True)  11.6 us
  transfers between devices with their start and end apart: 5, of which 3 were waited for; matrix products, arithmetic and copies ran while one was open for 0% of the time, Pallas kernels for 13%

profile of v5, /device:TPU:0, one launch (start us, length us, event | category | flops | bytes accessed | tf_op | source)
XLA Modules:
  0.0 403.5 jit_solution(4634416011503827811)
XLA Ops:
  0.0 4.5 %filter_bank.2.rest_0_ = bf16[8,16,2,16,128]{4,3,2,1,0:T(8,128)(2,1)} custom-call(bf16[2,4,128,8192]{3,2,1,0:T(8,128)(2,1)} %volt_ref.3, f32[2,4,32,128]{3,2,1,0:T(8,128)} %bitcast.2, bf16[512,768]{1,0:T(8,128)(2,1)} %constant.6.clone.table_ref), custom_call_target="tpu_custom_call" | custom-call | flops 1610612736 | bytes 4194304 | tf_op jit(solution)/shard_map/filter_bank/pallas_call | solution.py:180
  4.5 7.2 %all-to-all-start = ((bf16[8,16,2,16,128]{4,3,2,1,0:T(8,128)(2,1)}), bf16[8,16,2,16,128]{4,3,2,1,0:T(8,128)(2,1)}, u32[]{:S(2)}, u32[]{:S(2)}) async-start(bf16[8,16,2,16,128]{4,3,2,1,0:T(8,128)(2,1)} %filter_bank.2.rest_0_), calls=%async_computation | async-start | bytes 2097152 | tf_op jit(solution)/shard_map/all_to_all | solution.py:336
  11.8 22.1 %filter_bank.3 = (bf16[8,14,2,240,128]{4,3,2,1,0:T(8,128)(2,1)}, bf16[8,2,2,240,128]{4,3,2,1,0:T(8,128)(2,1)}) custom-call(bf16[2,4,128,8192]{3,2,1,0:T(8,128)(2,1)} %volt_ref.3, f32[2,4,32,128]{3,2,1,0:T(8,128)} %bitcast.3, bf16[512,768]{1,0:T(8,128)(2,1)} %constant.6.clone.table_ref, bf16[8,16,2,16,128]{4,3,2,1,0:T(8,128)(2,1)} %filter_bank.2.rest_0_), custom_call_target="tpu_custom_call" | custom-call | flops 24159191040 | bytes 62914560 | tf_op jit(solution)/shard_map/filter_bank/pallas_call | solution.py:180
  33.9 3.8 all-to-all-done.__1_.rest_0_
  37.6 304.3 %all_to_all.15.rest_2_ = bf16[8,14,2,240,128]{4,3,2,1,0:T(8,128)(2,1)} all-to-all(bf16[8,14,2,240,128]{4,3,2,1,0:T(8,128)(2,1)} %gate.2), channel_id=1, replica_groups=mesh['beam'=2,'inp'=8,'span'=2] {'inp'}, dimensions={0} | all-to-all | bytes 27525120 | tf_op jit(solution)/shard_map/all_to_all | solution.py:336
  341.9 0.0 collective-permute-start.1
  341.9 0.5 collective-permute-start
  342.4 4.3 %all-to-all-start.1 = ((bf16[8,2,2,240,128]{4,3,2,1,0:T(8,128)(2,1)}), bf16[8,2,2,240,128]{4,3,2,1,0:T(8,128)(2,1)}, u32[]{:S(2)}, u32[]{:S(2)}) async-start(bf16[8,2,2,240,128]{4,3,2,1,0:T(8,128)(2,1)} %get-tuple-element.9), calls=%async_computation.1 | async-start | bytes 3932160 | tf_op jit(solution)/shard_map/all_to_all | solution.py:336
  346.8 17.8 %collective-permute-done.rest_1_ = bf16[8,16,2,16,128]{4,3,2,1,0:T(8,128)(2,1)} collective-permute-done((bf16[8,16,2,16,128]{4,3,2,1,0:T(8,128)(2,1)}, bf16[8,16,2,16,128]{4,3,2,1,0:T(8,128)(2,1)}, u32[]{:S(2)}, u32[]{:S(2)}) %collective-permute-start) | collective-permute-done | bytes 1048608 | tf_op jit(solution)/shard_map/ppermute | solution.py:340
  364.6 0.0 collective-permute-done.1.rest_3_
  364.6 28.4 %correlate.2.__1_ = bf16[16,512,1024]{2,1,0:T(8,128)(2,1)} custom-call(s32[1]{0:T(128)} %bitcast.where_ref, bf16[8,16,2,16,128]{4,3,2,1,0:T(8,128)(2,1)} %all-to-all-done.__1_.rest_0_, bf16[8,16,2,16,128]{4,3,2,1,0:T(8,128)(2,1)} %collective-permute-done.rest_1_, bf16[8,14,2,240,128]{4,3,2,1,0:T(8,128)(2,1)} %all_to_all.15.rest_2_, ...), custom_call_target="tpu_custom_call" | custom-call | flops 60129542144 | bytes 234881024 | tf_op jit(solution)/shard_map/correlate/pallas_call | solution.py:296
  393.0 0.0 all-to-all-done.1.__0_
  393.0 0.3 collective-permute-start.2
  393.4 4.0 %collective-permute-done.2.rest_3_ = bf16[8,2,2,240,128]{4,3,2,1,0:T(8,128)(2,1)} collective-permute-done((bf16[8,2,2,240,128]{4,3,2,1,0:T(8,128)(2,1)}, bf16[8,2,2,240,128]{4,3,2,1,0:T(8,128)(2,1)}, u32[]{:S(2)}, u32[]{:S(2)}) %collective-permute-start.2) | collective-permute-done | bytes 1966112 | tf_op jit(solution)/shard_map/ppermute | solution.py:340
  397.4 6.1 %correlate.3 = bf16[16,512,1024]{2,1,0:T(8,128)(2,1)} custom-call(s32[1]{0:T(128)} %bitcast.where_ref, bf16[8,16,2,16,128]{4,3,2,1,0:T(8,128)(2,1)} %all-to-all-done.__1_.rest_0_, bf16[8,16,2,16,128]{4,3,2,1,0:T(8,128)(2,1)} %collective-permute-done.rest_1_, bf16[8,2,2,240,128]{4,3,2,1,0:T(8,128)(2,1)} %get-tuple-element.11.rest_2_, ...), custom_call_target="tpu_custom_call", output_to_operand_aliasing={{}: (5, {})} | custom-call | flops 8589934592 | bytes 33554432 | tf_op jit(solution)/shard_map/correlate/pallas_call | solution.py:296
  (2 shorter events, 0.0 us)
Async XLA Ops:
  4.5 33.1 %all-to-all-start = ((bf16[8,16,2,16,128]{4,3,2,1,0:T(8,128)(2,1)}), bf16[8,16,2,16,128]{4,3,2,1,0:T(8,128)(2,1)}, u32[]{:S(2)}, u32[]{:S(2)}) async-start(bf16[8,16,2,16,128]{4,3,2,1,0:T(8,128)(2,1)} %filter_bank.2.rest_0_), calls=%async_computation | async-start | bytes 2097152 | tf_op jit(solution)/shard_map/all_to_all | solution.py:336
  341.9 22.7 %collective-permute-start.1 = (bf16[8,14,2,240,128]{4,3,2,1,0:T(8,128)(2,1)}, bf16[8,14,2,240,128]{4,3,2,1,0:T(8,128)(2,1)}, u32[]{:S(2)}, u32[]{:S(2)}) collective-permute-start(bf16[8,14,2,240,128]{4,3,2,1,0:T(8,128)(2,1)} %all_to_all.15.rest_2_), channel_id=1, source_target_pairs={{0,1},{1,0},{2,3},{3,2},{4,5},{5,4},{6,7},{7,6},{8,9},{9,8},{10,11... | collective-permute-start | bytes 41287688 | tf_op jit(solution)/shard_map/ppermute | solution.py:340
  341.9 22.7 %collective-permute-start = (bf16[8,16,2,16,128]{4,3,2,1,0:T(8,128)(2,1)}, bf16[8,16,2,16,128]{4,3,2,1,0:T(8,128)(2,1)}, u32[]{:S(2)}, u32[]{:S(2)}) collective-permute-start(bf16[8,16,2,16,128]{4,3,2,1,0:T(8,128)(2,1)} %all-to-all-done.__1_.rest_0_), channel_id=1, source_target_pairs={{0,1},{1,0},{2,3},{3,2},{4,5},{5,4},{6,7},{7,6},{8,9},{9,8},{10,11... | collective-permute-start | bytes 3145736 | tf_op jit(solution)/shard_map/ppermute | solution.py:340
  342.4 50.6 %all-to-all-start.1 = ((bf16[8,2,2,240,128]{4,3,2,1,0:T(8,128)(2,1)}), bf16[8,2,2,240,128]{4,3,2,1,0:T(8,128)(2,1)}, u32[]{:S(2)}, u32[]{:S(2)}) async-start(bf16[8,2,2,240,128]{4,3,2,1,0:T(8,128)(2,1)} %get-tuple-element.9), calls=%async_computation.1 | async-start | bytes 3932160 | tf_op jit(solution)/shard_map/all_to_all | solution.py:336
  393.0 4.4 %collective-permute-start.2 = (bf16[8,2,2,240,128]{4,3,2,1,0:T(8,128)(2,1)}, bf16[8,2,2,240,128]{4,3,2,1,0:T(8,128)(2,1)}, u32[]{:S(2)}, u32[]{:S(2)}) collective-permute-start(bf16[8,2,2,240,128]{4,3,2,1,0:T(8,128)(2,1)} %get-tuple-element.11.rest_2_), channel_id=1, source_target_pairs={{0,1},{1,0},{2,3},{3,2},{4,5},{5,4},{6,7},{7,6},{8,9},{9,8},{10,11... | collective-permute-start | bytes 5898248 | tf_op jit(solution)/shard_map/ppermute | solution.py:340

commit v6 on v5

--- a/solution.py
+++ b/solution.py
@@ -15,7 +15,8 @@
 LANES = 128
 GROUP = 8
 VMEM = 64 * 1024 * 1024 - 64 * 1024
-UNROLL = 4
+UNROLL = 7
+TOGETHER = 2
 EARLY = 1
 PARTS = (14, 16)
 
@@ -117,25 +118,25 @@
     return table.reshape(-1, 2 * run).astype(ml_dtypes.bfloat16)
 
 
-def filter_kernel(halves, chunks, lead, pairs, volt_ref, gain_ref, table_ref, *rest):
+def filter_kernel(halves, chunks, lead, pairs, coarse, volt_ref, gain_ref, table_ref, *rest):
     outs, wide_ref = rest[-1 - len(chunks) : -1], rest[-1]
     inputs, samples = volt_ref.shape[2], volt_ref.shape[3]
     per_half = FINE // halves
     run = table_ref.shape[1] // 2
     hop = GROUP * FINE
-    wide_ref[...] = jnp.broadcast_to(gain_ref[:, 0][:, :, None, :], wide_ref.shape)
-
-    def one(pair, inside):
+    wide_ref[...] = jnp.broadcast_to(gain_ref[...][:, :, :, None, :], wide_ref.shape)
+
+    def one(channel, pair, inside):
         sets = []
         for group in range(2):
             start = lead + (2 * pair + group) * hop
             columns = []
             for part in range(2):
                 if inside:
-                    columns.append(volt_ref[part, 0, :, pl.ds(pl.multiple_of(start, LANES), run)])
+                    columns.append(volt_ref[part, channel, :, pl.ds(pl.multiple_of(start, LANES), run)])
                 else:
                     stop = min(start + run, samples)
-                    columns.append(volt_ref[part, 0, :, start:stop])
+                    columns.append(volt_ref[part, channel, :, start:stop])
                     if start + run > stop:
                         columns.append(jnp.zeros((inputs, start + run - stop), volt_ref.dtype))
             sets.append(jnp.concatenate(columns, axis=1))
@@ -146,7 +147,7 @@
         sums = sums.reshape(FINE, 2, GROUP, 2 * inputs)
         raw_real = jnp.concatenate([sums[:, 0, :, :inputs], sums[:, 0, :, inputs:]], axis=1)
         raw_imag = jnp.concatenate([sums[:, 1, :, :inputs], sums[:, 1, :, inputs:]], axis=1)
-        gain_real, gain_imag = wide_ref[0], wide_ref[1]
+        gain_real, gain_imag = wide_ref[0, channel], wide_ref[1, channel]
         real = (raw_real * gain_real - raw_imag * gain_imag).astype(jnp.bfloat16)
         imag = (raw_real * gain_imag + raw_imag * gain_real).astype(jnp.bfloat16)
         frames = pl.ds(pl.multiple_of(2 * GROUP * pair, 2 * GROUP), 2 * GROUP) if inside else pl.ds(
@@ -155,22 +156,24 @@
         for half in range(halves):
             start = half * per_half
             for out, size in zip(outs, chunks):
-                out[half, :, 0, frames, :] = real[start : start + size]
-                out[half, :, 1, frames, :] = imag[start : start + size]
+                out[channel * halves + half, :, 0, frames, :] = real[start : start + size]
+                out[channel * halves + half, :, 1, frames, :] = imag[start : start + size]
                 start += size
 
     whole = min(pairs, (samples - lead - run + hop) // (2 * hop))
 
-    def loop(pair, _):
-        one(pair, True)
-        return 0
-
-    lax.fori_loop(0, whole, loop, 0, unroll=UNROLL)
-    for pair in range(whole, pairs):
-        one(pair, False)
-
-
-def filter_bank(voltages, gains, halves, chunks, first_frame, last_frame, waits=()):
+    for channel in range(coarse):
+
+        def loop(pair, _, channel=channel):
+            one(channel, pair, True)
+            return 0
+
+        lax.fori_loop(0, whole, loop, 0, unroll=UNROLL)
+        for pair in range(whole, pairs):
+            one(channel, pair, False)
+
+
+def filter_bank(voltages, gains, halves, chunks, first_frame, last_frame, together, waits=()):
     _, coarse, inputs, samples = voltages.shape
     table = filter_rows()
     run = table.shape[1] // 2
@@ -179,24 +182,24 @@
     block = min(samples, last_frame * FINE + ahead)
     return pl.pallas_call(
         functools.partial(
-            filter_kernel, halves, chunks, first_frame * FINE, frames // (2 * GROUP)
+            filter_kernel, halves, chunks, first_frame * FINE, frames // (2 * GROUP), together
         ),
         out_shape=[
             jax.ShapeDtypeStruct((coarse * halves, count, 2, frames, inputs), jnp.bfloat16)
             for count in chunks
         ],
-        grid=(coarse,),
+        grid=(coarse // together,),
         in_specs=[
-            pl.BlockSpec((2, 1, inputs, block), lambda c: (0, c, 0, 0)),
-            pl.BlockSpec((2, 1, FINE, inputs), lambda c: (0, c, 0, 0)),
+            pl.BlockSpec((2, together, inputs, block), lambda c: (0, c, 0, 0)),
+            pl.BlockSpec((2, together, FINE, inputs), lambda c: (0, c, 0, 0)),
             pl.BlockSpec(table.shape, lambda c: (0, 0)),
         ]
         + [pl.BlockSpec(memory_space=pl.ANY)] * len(waits),
         out_specs=[
-            pl.BlockSpec((halves, count, 2, frames, inputs), lambda c: (c, 0, 0, 0, 0))
+            pl.BlockSpec((together * halves, count, 2, frames, inputs), lambda c: (c, 0, 0, 0, 0))
             for count in chunks
         ],
-        scratch_shapes=[pltpu.VMEM((2, FINE, 2 * GROUP, inputs), jnp.float32)],
+        scratch_shapes=[pltpu.VMEM((2, together, FINE, 2 * GROUP, inputs), jnp.float32)],
         compiler_params=pltpu.CompilerParams(vmem_limit_bytes=VMEM),
         cost_estimate=pl.CostEstimate(
             flops=4 * table.size * inputs * frames // GROUP * coarse,
@@ -340,9 +343,9 @@
             lax.ppermute(array, "span", [(i, i ^ other) for i in range(spans)]) for other in range(1, spans)
         ]
 
-    outgoing = filter_bank(voltages, gains, halves, [channels], 0, early)
+    outgoing = filter_bank(voltages, gains, halves, [channels], 0, early, TOGETHER if coarse % TOGETHER == 0 else 1)
     outgoing = list(outgoing)
-    outgoing += list(filter_bank(voltages, gains, halves, chunks, early, frames, outgoing))
+    outgoing += list(filter_bank(voltages, gains, halves, chunks, early, frames, 1, outgoing))
     turned = across(outgoing[0])
     outgoing[1] = gate([outgoing[1]], [turned])[0]
     first_frames = [turned] + other_spans(turned)

time: 405 us -> 403 us (level)
  transfers between devices with their start and end apart: 5 -> 5, of which waited for: 3 -> 3; matrix products, arithmetic and copies ran while one was open for 0% -> 0% of each run, Pallas kernels for 13% -> 12%
where the time goes in v6:
time: 403 us; the launch traced here: 402 us
  blocking collectives  304 us (75%)
  Pallas kernels  57.7 us (14%)
  waiting for transfers between devices  28 us (7%)
  starting transfers between devices  12.4 us (3%)
    all_to_all x1, blocking collectives, across(): return lax.all_to_all(array, 'inp', split_axis=0, concat_axis=0, tiled=True)  304 us
    pallas_call x2, Pallas kernels, correlate(): pl.pallas_call(functools.partial(correlate_kernel, len(pieces), tile, sca...  34.5 us
    pallas_call x2, Pallas kernels, filter_bank(): pl.pallas_call(functools.partial(filter_kernel, halves, chunks, first_fra...  23.2 us
    ppermute x3, waiting for transfers between devices, other_spans(): lax.ppermute(array, 'span', [(i, i ^ other) for i in range(spans)])  21.9 us
    all_to_all x2, starting transfers between devices, across(): return lax.all_to_all(array, 'inp', split_axis=0, concat_axis=0, tiled=True)  11.6 us
  transfers between devices with their start and end apart: 5, of which 3 were waited for; matrix products, arithmetic and copies ran while one was open for 0% of the time, Pallas kernels for 12%

profile of v6, /device:TPU:0, one launch (start us, length us, event | category | flops | bytes accessed | tf_op | source)
XLA Modules:
  0.0 402.4 jit_solution(7368519663861129180)
XLA Ops:
  0.0 3.4 filter_bank.2.rest_0_
  3.4 7.3 %all-to-all-start = ((bf16[8,16,2,16,128]{4,3,2,1,0:T(8,128)(2,1)}), bf16[8,16,2,16,128]{4,3,2,1,0:T(8,128)(2,1)}, u32[]{:S(2)}, u32[]{:S(2)}) async-start(bf16[8,16,2,16,128]{4,3,2,1,0:T(8,128)(2,1)} %filter_bank.2.rest_0_), calls=%async_computation | async-start | bytes 2097152 | tf_op jit(solution)/shard_map/all_to_all | solution.py:339
  10.7 19.8 %filter_bank.3 = (bf16[8,14,2,240,128]{4,3,2,1,0:T(8,128)(2,1)}, bf16[8,2,2,240,128]{4,3,2,1,0:T(8,128)(2,1)}) custom-call(bf16[2,4,128,8192]{3,2,1,0:T(8,128)(2,1)} %volt_ref.3, f32[2,4,32,128]{3,2,1,0:T(8,128)} %bitcast.3, bf16[512,768]{1,0:T(8,128)(2,1)} %constant.6.clone.table_ref, bf16[8,16,2,16,128]{4,3,2,1,0:T(8,128)(2,1)} %filter_bank.2.rest_0_), custom_call_target="tpu_custom_call" | custom-call | flops 24159191040 | bytes 62914560 | tf_op jit(solution)/shard_map/filter_bank/pallas_call | solution.py:183
  30.5 6.1 %all-to-all-done.__1_.rest_0_ = bf16[8,16,2,16,128]{4,3,2,1,0:T(8,128)(2,1)} async-done(((bf16[8,16,2,16,128]{4,3,2,1,0:T(8,128)(2,1)}), bf16[8,16,2,16,128]{4,3,2,1,0:T(8,128)(2,1)}, u32[]{:S(2)}, u32[]{:S(2)}) %all-to-all-start) | async-done | bytes 1048608 | tf_op jit(solution)/shard_map/all_to_all | solution.py:339
  36.5 304.3 %all_to_all.15.rest_2_ = bf16[8,14,2,240,128]{4,3,2,1,0:T(8,128)(2,1)} all-to-all(bf16[8,14,2,240,128]{4,3,2,1,0:T(8,128)(2,1)} %gate.2), channel_id=1, replica_groups=mesh['beam'=2,'inp'=8,'span'=2] {'inp'}, dimensions={0} | all-to-all | bytes 27525120 | tf_op jit(solution)/shard_map/all_to_all | solution.py:339
  340.8 0.0 collective-permute-start.1
  340.8 0.5 collective-permute-start
  341.3 4.3 %all-to-all-start.1 = ((bf16[8,2,2,240,128]{4,3,2,1,0:T(8,128)(2,1)}), bf16[8,2,2,240,128]{4,3,2,1,0:T(8,128)(2,1)}, u32[]{:S(2)}, u32[]{:S(2)}) async-start(bf16[8,2,2,240,128]{4,3,2,1,0:T(8,128)(2,1)} %get-tuple-element.9), calls=%async_computation.1 | async-start | bytes 3932160 | tf_op jit(solution)/shard_map/all_to_all | solution.py:339
  345.7 17.8 %collective-permute-done.rest_1_ = bf16[8,16,2,16,128]{4,3,2,1,0:T(8,128)(2,1)} collective-permute-done((bf16[8,16,2,16,128]{4,3,2,1,0:T(8,128)(2,1)}, bf16[8,16,2,16,128]{4,3,2,1,0:T(8,128)(2,1)}, u32[]{:S(2)}, u32[]{:S(2)}) %collective-permute-start) | collective-permute-done | bytes 1048608 | tf_op jit(solution)/shard_map/ppermute | solution.py:343
  363.5 0.0 collective-permute-done.1.rest_3_
  363.5 28.4 %correlate.2.__1_ = bf16[16,512,1024]{2,1,0:T(8,128)(2,1)} custom-call(s32[1]{0:T(128)} %bitcast.where_ref, bf16[8,16,2,16,128]{4,3,2,1,0:T(8,128)(2,1)} %all-to-all-done.__1_.rest_0_, bf16[8,16,2,16,128]{4,3,2,1,0:T(8,128)(2,1)} %collective-permute-done.rest_1_, bf16[8,14,2,240,128]{4,3,2,1,0:T(8,128)(2,1)} %all_to_all.15.rest_2_, ...), custom_call_target="tpu_custom_call" | custom-call | flops 60129542144 | bytes 234881024 | tf_op jit(solution)/shard_map/correlate/pallas_call | solution.py:299
  391.9 0.0 all-to-all-done.1.__0_
  391.9 0.3 collective-permute-start.2
  392.3 4.0 %collective-permute-done.2.rest_3_ = bf16[8,2,2,240,128]{4,3,2,1,0:T(8,128)(2,1)} collective-permute-done((bf16[8,2,2,240,128]{4,3,2,1,0:T(8,128)(2,1)}, bf16[8,2,2,240,128]{4,3,2,1,0:T(8,128)(2,1)}, u32[]{:S(2)}, u32[]{:S(2)}) %collective-permute-start.2) | collective-permute-done | bytes 1966112 | tf_op jit(solution)/shard_map/ppermute | solution.py:343
  396.3 6.1 %correlate.3 = bf16[16,512,1024]{2,1,0:T(8,128)(2,1)} custom-call(s32[1]{0:T(128)} %bitcast.where_ref, bf16[8,16,2,16,128]{4,3,2,1,0:T(8,128)(2,1)} %all-to-all-done.__1_.rest_0_, bf16[8,16,2,16,128]{4,3,2,1,0:T(8,128)(2,1)} %collective-permute-done.rest_1_, bf16[8,2,2,240,128]{4,3,2,1,0:T(8,128)(2,1)} %get-tuple-element.11.rest_2_, ...), custom_call_target="tpu_custom_call", output_to_operand_aliasing={{}: (5, {})} | custom-call | flops 8589934592 | bytes 33554432 | tf_op jit(solution)/shard_map/correlate/pallas_call | solution.py:299
  (2 shorter events, 0.0 us)
Async XLA Ops:
  3.4 33.1 %all-to-all-start = ((bf16[8,16,2,16,128]{4,3,2,1,0:T(8,128)(2,1)}), bf16[8,16,2,16,128]{4,3,2,1,0:T(8,128)(2,1)}, u32[]{:S(2)}, u32[]{:S(2)}) async-start(bf16[8,16,2,16,128]{4,3,2,1,0:T(8,128)(2,1)} %filter_bank.2.rest_0_), calls=%async_computation | async-start | bytes 2097152 | tf_op jit(solution)/shard_map/all_to_all | solution.py:339
  340.8 22.7 %collective-permute-start.1 = (bf16[8,14,2,240,128]{4,3,2,1,0:T(8,128)(2,1)}, bf16[8,14,2,240,128]{4,3,2,1,0:T(8,128)(2,1)}, u32[]{:S(2)}, u32[]{:S(2)}) collective-permute-start(bf16[8,14,2,240,128]{4,3,2,1,0:T(8,128)(2,1)} %all_to_all.15.rest_2_), channel_id=1, source_target_pairs={{0,1},{1,0},{2,3},{3,2},{4,5},{5,4},{6,7},{7,6},{8,9},{9,8},{10,11... | collective-permute-start | bytes 41287688 | tf_op jit(solution)/shard_map/ppermute | solution.py:343
  340.8 22.7 %collective-permute-start = (bf16[8,16,2,16,128]{4,3,2,1,0:T(8,128)(2,1)}, bf16[8,16,2,16,128]{4,3,2,1,0:T(8,128)(2,1)}, u32[]{:S(2)}, u32[]{:S(2)}) collective-permute-start(bf16[8,16,2,16,128]{4,3,2,1,0:T(8,128)(2,1)} %all-to-all-done.__1_.rest_0_), channel_id=1, source_target_pairs={{0,1},{1,0},{2,3},{3,2},{4,5},{5,4},{6,7},{7,6},{8,9},{9,8},{10,11... | collective-permute-start | bytes 3145736 | tf_op jit(solution)/shard_map/ppermute | solution.py:343
  341.3 50.6 %all-to-all-start.1 = ((bf16[8,2,2,240,128]{4,3,2,1,0:T(8,128)(2,1)}), bf16[8,2,2,240,128]{4,3,2,1,0:T(8,128)(2,1)}, u32[]{:S(2)}, u32[]{:S(2)}) async-start(bf16[8,2,2,240,128]{4,3,2,1,0:T(8,128)(2,1)} %get-tuple-element.9), calls=%async_computation.1 | async-start | bytes 3932160 | tf_op jit(solution)/shard_map/all_to_all | solution.py:339
  391.9 4.4 %collective-permute-start.2 = (bf16[8,2,2,240,128]{4,3,2,1,0:T(8,128)(2,1)}, bf16[8,2,2,240,128]{4,3,2,1,0:T(8,128)(2,1)}, u32[]{:S(2)}, u32[]{:S(2)}) collective-permute-start(bf16[8,2,2,240,128]{4,3,2,1,0:T(8,128)(2,1)} %get-tuple-element.11.rest_2_), channel_id=1, source_target_pairs={{0,1},{1,0},{2,3},{3,2},{4,5},{5,4},{6,7},{7,6},{8,9},{9,8},{10,11... | collective-permute-start | bytes 5898248 | tf_op jit(solution)/shard_map/ppermute | solution.py:343

commit v7 on v6

--- a/solution.py
+++ b/solution.py
@@ -118,7 +118,7 @@
     return table.reshape(-1, 2 * run).astype(ml_dtypes.bfloat16)
 
 
-def filter_kernel(halves, chunks, lead, pairs, coarse, volt_ref, gain_ref, table_ref, *rest):
+def filter_kernel(halves, chunks, firsts, pairs, coarse, volt_ref, gain_ref, table_ref, *rest):
     outs, wide_ref = rest[-1 - len(chunks) : -1], rest[-1]
     inputs, samples = volt_ref.shape[2], volt_ref.shape[3]
     per_half = FINE // halves
@@ -129,7 +129,7 @@
     def one(channel, pair, inside):
         sets = []
         for group in range(2):
-            start = lead + (2 * pair + group) * hop
+            start = (2 * pair + group) * hop
             columns = []
             for part in range(2):
                 if inside:
@@ -150,17 +150,20 @@
         gain_real, gain_imag = wide_ref[0, channel], wide_ref[1, channel]
         real = (raw_real * gain_real - raw_imag * gain_imag).astype(jnp.bfloat16)
         imag = (raw_real * gain_imag + raw_imag * gain_real).astype(jnp.bfloat16)
-        frames = pl.ds(pl.multiple_of(2 * GROUP * pair, 2 * GROUP), 2 * GROUP) if inside else pl.ds(
-            2 * GROUP * pair, 2 * GROUP
-        )
         for half in range(halves):
             start = half * per_half
-            for out, size in zip(outs, chunks):
+            for out, size, first in zip(outs, chunks, firsts):
+                if not inside and pair < first:
+                    start += size
+                    continue
+                at = 2 * GROUP * (pair - first)
+                frames = pl.ds(pl.multiple_of(at, 2 * GROUP) if inside else at, 2 * GROUP)
                 out[channel * halves + half, :, 0, frames, :] = real[start : start + size]
                 out[channel * halves + half, :, 1, frames, :] = imag[start : start + size]
                 start += size
 
-    whole = min(pairs, (samples - lead - run + hop) // (2 * hop))
+    whole = min(pairs, (samples - run + hop) // (2 * hop))
+    common = max(firsts)
 
     for channel in range(coarse):
 
@@ -168,25 +171,31 @@
             one(channel, pair, True)
             return 0
 
-        lax.fori_loop(0, whole, loop, 0, unroll=UNROLL)
+        for pair in range(min(firsts), common):
+            one(channel, pair, False)
+        lax.fori_loop(common, whole, loop, 0, unroll=UNROLL)
         for pair in range(whole, pairs):
             one(channel, pair, False)
 
 
-def filter_bank(voltages, gains, halves, chunks, first_frame, last_frame, together, waits=()):
+def filter_bank(voltages, gains, halves, chunks, first_frames, last_frame, together, waits=()):
     _, coarse, inputs, samples = voltages.shape
     table = filter_rows()
     run = table.shape[1] // 2
-    frames = last_frame - first_frame
     ahead = run - GROUP * FINE
     block = min(samples, last_frame * FINE + ahead)
     return pl.pallas_call(
         functools.partial(
-            filter_kernel, halves, chunks, first_frame * FINE, frames // (2 * GROUP), together
+            filter_kernel,
+            halves,
+            chunks,
+            [first // (2 * GROUP) for first in first_frames],
+            last_frame // (2 * GROUP),
+            together,
         ),
         out_shape=[
-            jax.ShapeDtypeStruct((coarse * halves, count, 2, frames, inputs), jnp.bfloat16)
-            for count in chunks
+            jax.ShapeDtypeStruct((coarse * halves, count, 2, last_frame - first, inputs), jnp.bfloat16)
+            for count, first in zip(chunks, first_frames)
         ],
         grid=(coarse // together,),
         in_specs=[
@@ -196,14 +205,14 @@
         ]
         + [pl.BlockSpec(memory_space=pl.ANY)] * len(waits),
         out_specs=[
-            pl.BlockSpec((together * halves, count, 2, frames, inputs), lambda c: (c, 0, 0, 0, 0))
-            for count in chunks
+            pl.BlockSpec((together * halves, count, 2, last_frame - first, inputs), lambda c: (c, 0, 0, 0, 0))
+            for count, first in zip(chunks, first_frames)
         ],
         scratch_shapes=[pltpu.VMEM((2, together, FINE, 2 * GROUP, inputs), jnp.float32)],
         compiler_params=pltpu.CompilerParams(vmem_limit_bytes=VMEM),
         cost_estimate=pl.CostEstimate(
-            flops=4 * table.size * inputs * frames // GROUP * coarse,
-            bytes_accessed=16 * coarse * inputs * frames * FINE,
+            flops=4 * table.size * inputs * last_frame // GROUP * coarse,
+            bytes_accessed=16 * coarse * inputs * last_frame * FINE,
             transcendentals=0,
         ),
         name="filter_bank",
@@ -227,8 +236,9 @@
     )(*released, *waits)
 
 
-def correlate_kernel(pieces, tile, scale, where_ref, *rest):
+def correlate_kernel(pieces, tile, scale, added, where_ref, *rest):
     blocks = rest[:pieces]
+    added_ref = rest[pieces] if added else None
     out_ref, rows_ref = rest[-2:]
     inputs = blocks[0].shape[4]
     row_count, total = out_ref.shape[1:]
@@ -261,7 +271,12 @@
 
     def product(start, size, column):
         left = rows_ref[pl.ds(pl.multiple_of(start, tile), size), :]
-        return jnp.dot(left, columns_of(column), preferred_element_type=jnp.float32) * scale
+        return jnp.dot(left, columns_of(column), preferred_element_type=jnp.float32)
+
+    def store(at, column_at, sums):
+        if added:
+            sums = sums + added_ref[0, at, column_at]
+        out_ref[0, at, column_at] = (sums * scale if scale != 1.0 else sums).astype(out_ref.dtype)
 
     before = first_tile > 0
     start = jnp.where(before, 0, row_count)
@@ -270,20 +285,19 @@
     right = jnp.concatenate([columns_of(first_column + index) for index in range(width // tile)], axis=1)
     column_at = pl.ds(pl.multiple_of(first_column * tile, tile), width)
     left = rows_ref[pl.ds(pl.multiple_of(start, tile), row_count), :]
-    sums = jnp.dot(left, right, preferred_element_type=jnp.float32) * scale
-    out_ref[0, :, column_at] = sums.astype(out_ref.dtype)
+    store(slice(0, row_count), column_at, jnp.dot(left, right, preferred_element_type=jnp.float32))
     upper = lax.broadcasted_iota(jnp.int32, (tile, tile), 0) <= lax.broadcasted_iota(jnp.int32, (tile, tile), 1)
     column_at = pl.ds(pl.multiple_of(first_tile * tile, tile), tile)
     sums = product(0, 3 * tile, first_tile)
-    out_ref[0, :tile, column_at] = jnp.where(upper, sums[2 * tile :], sums[:tile]).astype(out_ref.dtype)
-    out_ref[0, tile:, column_at] = sums[tile : 2 * tile].astype(out_ref.dtype)
+    store(slice(0, tile), column_at, jnp.where(upper, sums[2 * tile :], sums[:tile]))
+    store(slice(tile, row_count), column_at, sums[tile : 2 * tile])
     column_at = pl.ds(pl.multiple_of((first_tile + 1) * tile, tile), tile)
     sums = product(tile, 3 * tile, first_tile + 1)
-    out_ref[0, :tile, column_at] = sums[tile : 2 * tile].astype(out_ref.dtype)
-    out_ref[0, tile:, column_at] = jnp.where(upper, sums[2 * tile :], sums[:tile]).astype(out_ref.dtype)
-
-
-def correlate(pieces, where, held, first, count, channels, row_count, total, tile, scale):
+    store(slice(0, tile), column_at, sums[tile : 2 * tile])
+    store(slice(tile, row_count), column_at, jnp.where(upper, sums[2 * tile :], sums[:tile]))
+
+
+def correlate(pieces, where, held, first, count, channels, row_count, total, tile, scale, added=None, dtype=jnp.bfloat16):
     sources, _, _, _, inputs = pieces[0][0].shape
     depth = 2 * sum(array.shape[3] for array, _ in pieces)
     operands = [array for array, _ in pieces]
@@ -291,14 +305,17 @@
         pl.BlockSpec((sources, 1, 2, array.shape[3], inputs), lambda q, w, start=start: (0, start + q, 0, 0, 0))
         for array, start in pieces
     ]
+    if added is not None:
+        operands.append(added)
+        in_specs.append(pl.BlockSpec((1, row_count, total), lambda q, w: (q, 0, 0)))
     aliases = {}
     if held is not None:
         aliases = {1 + len(operands): 0}
         operands.append(held)
         in_specs.append(pl.BlockSpec(memory_space=pl.ANY))
     return pl.pallas_call(
-        functools.partial(correlate_kernel, len(pieces), tile, scale),
-        out_shape=jax.ShapeDtypeStruct((channels, row_count, total), jnp.bfloat16),
+        functools.partial(correlate_kernel, len(pieces), tile, scale, added is not None),
+        out_shape=jax.ShapeDtypeStruct((channels, row_count, total), dtype),
         grid_spec=pltpu.PrefetchScalarGridSpec(
             num_scalar_prefetch=1,
             grid=(count,),
@@ -343,9 +360,11 @@
             lax.ppermute(array, "span", [(i, i ^ other) for i in range(spans)]) for other in range(1, spans)
         ]
 
-    outgoing = filter_bank(voltages, gains, halves, [channels], 0, early, TOGETHER if coarse % TOGETHER == 0 else 1)
+    ahead = chunks[:-1] if len(chunks) > 1 else chunks
+    begins = [early] * len(ahead) + [0] * (len(chunks) - len(ahead))
+    outgoing = filter_bank(voltages, gains, halves, [sum(ahead)], [0], early, TOGETHER if coarse % TOGETHER == 0 else 1)
     outgoing = list(outgoing)
-    outgoing += list(filter_bank(voltages, gains, halves, chunks, early, frames, 1, outgoing))
+    outgoing += list(filter_bank(voltages, gains, halves, chunks, begins, frames, 1, outgoing))
     turned = across(outgoing[0])
     outgoing[1] = gate([outgoing[1]], [turned])[0]
     first_frames = [turned] + other_spans(turned)
@@ -354,10 +373,18 @@
         turned = across(outgoing[1 + index])
         if held is not None:
             turned, held = gate([turned, held], [])
-        pieces = [(array, first) for array in first_frames]
-        pieces += [(array, 0) for array in [turned] + other_spans(turned)]
+        others = other_spans(turned)
+        pieces = [(array, first) for array in first_frames] if begins[index] else []
+        added = None
+        if pieces:
+            pieces += [(turned, 0)] + [(array, 0) for array in others]
+        else:
+            added = correlate(
+                [(turned, 0)], where, None, 0, size, size, row_count, total, 2 * LANES, 1.0, None, jnp.float32
+            )
+            pieces = [(array, 0) for array in others]
         held = correlate(
-            pieces, where, held, first, size, channels, row_count, total, 2 * LANES, scale
+            pieces, where, held, first, size, channels, row_count, total, 2 * LANES, scale, added
         )
         first += size
     return held
@@ -380,6 +407,7 @@
             and FINE % (count // coarse) == 0
             and (FINE // (count // coarse)) % 8 == 0
             and inputs == LANES
+            and spans > 1
             and samples % (2 * GROUP * FINE) == 0
             and samples >= 8 * GROUP * FINE
             and count * inputs // spans == 4 * LANES

time: 403 us -> 402 us (level)
  waiting for transfers between devices: 28 us -> 22 us
  Pallas kernels: 57.7 us -> 62.7 us
    ppermute x3, waiting for transfers between devices: 21.9 us -> 17.6 us  [other_spans(): lax.ppermute(array, 'span', [(i, i ^ other) for i in range(spans)])]
    pallas_call x2 -> x3, Pallas kernels: 34.5 us -> 37.9 us  [correlate(): pl.pallas_call(functools.partial(correlate_kernel, len(pieces), tile, sca...]
  transfers between devices with their start and end apart: 5 -> 5, of which waited for: 3 -> 3; matrix products, arithmetic and copies ran while one was open for 0% -> 0% of each run, Pallas kernels for 12% -> 14%
where the time goes in v7:
time: 402 us; the launch traced here: 401 us
  blocking collectives  304 us (76%)
  Pallas kernels  62.7 us (16%)
  waiting for transfers between devices  22 us (5%)
  starting transfers between devices  12.1 us (3%)
    all_to_all x1, blocking collectives, across(): return lax.all_to_all(array, 'inp', split_axis=0, concat_axis=0, tiled=True)  304 us
    pallas_call x3, Pallas kernels, correlate(): pl.pallas_call(functools.partial(correlate_kernel, len(pieces), tile, sca...  37.9 us
    pallas_call x2, Pallas kernels, filter_bank(): pl.pallas_call(functools.partial(filter_kernel, halves, chunks, [first //...  24.8 us
    ppermute x3, waiting for transfers between devices, other_spans(): lax.ppermute(array, 'span', [(i, i ^ other) for i in range(spans)])  17.6 us
    all_to_all x2, starting transfers between devices, across(): return lax.all_to_all(array, 'inp', split_axis=0, concat_axis=0, tiled=True)  11.6 us
  transfers between devices with their start and end apart: 5, of which 3 were waited for; matrix products, arithmetic and copies ran while one was open for 0% of the time, Pallas kernels for 14%

profile of v7, /device:TPU:0, one launch (start us, length us, event | category | flops | bytes accessed | tf_op | source)
XLA Modules:
  0.0 401.2 jit_solution(7327160084071107108)
XLA Ops:
  0.0 3.4 filter_bank.2.rest_0_
  3.4 7.3 %all-to-all-start.1 = ((bf16[8,14,2,16,128]{4,3,2,1,0:T(8,128)(2,1)}), bf16[8,14,2,16,128]{4,3,2,1,0:T(8,128)(2,1)}, u32[]{:S(2)}, u32[]{:S(2)}) async-start(bf16[8,14,2,16,128]{4,3,2,1,0:T(8,128)(2,1)} %filter_bank.2.rest_0_), calls=%async_computation.1 | async-start | bytes 1835008 | tf_op jit(solution)/shard_map/all_to_all | solution.py:356
  10.6 21.4 %filter_bank.3 = (bf16[8,14,2,240,128]{4,3,2,1,0:T(8,128)(2,1)}, bf16[8,2,2,256,128]{4,3,2,1,0:T(8,128)(2,1)}) custom-call(bf16[2,4,128,8192]{3,2,1,0:T(8,128)(2,1)} %volt_ref.3, f32[2,4,32,128]{3,2,1,0:T(8,128)} %bitcast.3, bf16[512,768]{1,0:T(8,128)(2,1)} %constant.6.clone.table_ref, bf16[8,14,2,16,128]{4,3,2,1,0:T(8,128)(2,1)} %filter_bank.2.rest_0_), custom_call_target="tpu_custom_call" | custom-call | flops 25769803776 | bytes 67108864 | tf_op jit(solution)/shard_map/filter_bank/pallas_call | solution.py:187
  32.0 1.7 all-to-all-done.1.__1_.rest_0_
  33.8 304.3 %all_to_all.15.rest_2_ = bf16[8,14,2,240,128]{4,3,2,1,0:T(8,128)(2,1)} all-to-all(bf16[8,14,2,240,128]{4,3,2,1,0:T(8,128)(2,1)} %gate.2), channel_id=1, replica_groups=mesh['beam'=2,'inp'=8,'span'=2] {'inp'}, dimensions={0} | all-to-all | bytes 27525120 | tf_op jit(solution)/shard_map/all_to_all | solution.py:356
  338.1 0.0 collective-permute-start.1
  338.1 0.5 collective-permute-start
  338.6 4.4 %all-to-all-start = ((bf16[8,2,2,256,128]{4,3,2,1,0:T(8,128)(2,1)}), bf16[8,2,2,256,128]{4,3,2,1,0:T(8,128)(2,1)}, u32[]{:S(2)}, u32[]{:S(2)}) async-start(bf16[8,2,2,256,128]{4,3,2,1,0:T(8,128)(2,1)} %get-tuple-element.9), calls=%async_computation | async-start | bytes 4194304 | tf_op jit(solution)/shard_map/all_to_all | solution.py:356
  343.0 17.6 %collective-permute-done.rest_1_ = bf16[8,14,2,16,128]{4,3,2,1,0:T(8,128)(2,1)} collective-permute-done((bf16[8,14,2,16,128]{4,3,2,1,0:T(8,128)(2,1)}, bf16[8,14,2,16,128]{4,3,2,1,0:T(8,128)(2,1)}, u32[]{:S(2)}, u32[]{:S(2)}) %collective-permute-start) | collective-permute-done | bytes 917536 | tf_op jit(solution)/shard_map/ppermute | solution.py:360
  360.6 0.0 collective-permute-done.1.rest_3_
  360.6 28.4 %correlate.3.__1_ = bf16[16,512,1024]{2,1,0:T(8,128)(2,1)} custom-call(s32[1]{0:T(128)} %bitcast.where_ref, bf16[8,14,2,16,128]{4,3,2,1,0:T(8,128)(2,1)} %all-to-all-done.1.__1_.rest_0_, bf16[8,14,2,16,128]{4,3,2,1,0:T(8,128)(2,1)} %collective-permute-done.rest_1_, bf16[8,14,2,240,128]{4,3,2,1,0:T(8,128)(2,1)} %all_to_all.15.rest_2_, ...), custom_call_target="tpu_custom_call" | custom-call | flops 60129542144 | bytes 234881024 | tf_op jit(solution)/shard_map/correlate/pallas_call | solution.py:316
  389.0 2.6 all-to-all-done.__0_
  391.7 0.0 collective-permute-start.2
  391.7 4.6 %correlate.4.rest_1_ = f32[2,512,1024]{2,1,0:T(8,128)} custom-call(s32[1]{0:T(128)} %bitcast.where_ref, bf16[8,2,2,256,128]{4,3,2,1,0:T(8,128)(2,1)} %get-tuple-element.11.rest_0_), custom_call_target="tpu_custom_call" | custom-call | flops 4294967296 | bytes 16777216 | tf_op jit(solution)/shard_map/correlate/pallas_call | solution.py:316
  396.2 0.0 collective-permute-done.2.rest_0_
  396.2 4.9 %correlate.5 = bf16[16,512,1024]{2,1,0:T(8,128)(2,1)} custom-call(s32[1]{0:T(128)} %bitcast.where_ref, bf16[8,2,2,256,128]{4,3,2,1,0:T(8,128)(2,1)} %collective-permute-done.2.rest_0_, f32[2,512,1024]{2,1,0:T(8,128)} %correlate.4.rest_1_, bf16[16,512,1024]{2,1,0:T(8,128)(2,1)} %get-tuple-element.12.rest_2_), custom_call_target="tpu_custom_call", output_to_operand_aliasing={{}: (3, {})} | custom-call | flops 4294967296 | bytes 16777216 | tf_op jit(solution)/shard_map/correlate/pallas_call | solution.py:316
  (2 shorter events, 0.0 us)
Async XLA Ops:
  3.4 30.4 %all-to-all-start.1 = ((bf16[8,14,2,16,128]{4,3,2,1,0:T(8,128)(2,1)}), bf16[8,14,2,16,128]{4,3,2,1,0:T(8,128)(2,1)}, u32[]{:S(2)}, u32[]{:S(2)}) async-start(bf16[8,14,2,16,128]{4,3,2,1,0:T(8,128)(2,1)} %filter_bank.2.rest_0_), calls=%async_computation.1 | async-start | bytes 1835008 | tf_op jit(solution)/shard_map/all_to_all | solution.py:356
  338.1 22.5 %collective-permute-start.1 = (bf16[8,14,2,240,128]{4,3,2,1,0:T(8,128)(2,1)}, bf16[8,14,2,240,128]{4,3,2,1,0:T(8,128)(2,1)}, u32[]{:S(2)}, u32[]{:S(2)}) collective-permute-start(bf16[8,14,2,240,128]{4,3,2,1,0:T(8,128)(2,1)} %all_to_all.15.rest_2_), channel_id=1, source_target_pairs={{0,1},{1,0},{2,3},{3,2},{4,5},{5,4},{6,7},{7,6},{8,9},{9,8},{10,11... | collective-permute-start | bytes 41287688 | tf_op jit(solution)/shard_map/ppermute | solution.py:360
  338.1 22.5 %collective-permute-start = (bf16[8,14,2,16,128]{4,3,2,1,0:T(8,128)(2,1)}, bf16[8,14,2,16,128]{4,3,2,1,0:T(8,128)(2,1)}, u32[]{:S(2)}, u32[]{:S(2)}) collective-permute-start(bf16[8,14,2,16,128]{4,3,2,1,0:T(8,128)(2,1)} %all-to-all-done.1.__1_.rest_0_), channel_id=1, source_target_pairs={{0,1},{1,0},{2,3},{3,2},{4,5},{5,4},{6,7},{7,6},{8,9},{9,8},{10,11... | collective-permute-start | bytes 2752520 | tf_op jit(solution)/shard_map/ppermute | solution.py:360
  338.6 53.1 %all-to-all-start = ((bf16[8,2,2,256,128]{4,3,2,1,0:T(8,128)(2,1)}), bf16[8,2,2,256,128]{4,3,2,1,0:T(8,128)(2,1)}, u32[]{:S(2)}, u32[]{:S(2)}) async-start(bf16[8,2,2,256,128]{4,3,2,1,0:T(8,128)(2,1)} %get-tuple-element.9), calls=%async_computation | async-start | bytes 4194304 | tf_op jit(solution)/shard_map/all_to_all | solution.py:356
  391.7 4.6 %collective-permute-start.2 = (bf16[8,2,2,256,128]{4,3,2,1,0:T(8,128)(2,1)}, bf16[8,2,2,256,128]{4,3,2,1,0:T(8,128)(2,1)}, u32[]{:S(2)}, u32[]{:S(2)}) collective-permute-start(bf16[8,2,2,256,128]{4,3,2,1,0:T(8,128)(2,1)} %get-tuple-element.11.rest_0_), channel_id=1, source_target_pairs={{0,1},{1,0},{2,3},{3,2},{4,5},{5,4},{6,7},{7,6},{8,9},{9,8},{10,11... | collective-permute-start | bytes 6291464 | tf_op jit(solution)/shard_map/ppermute | solution.py:360

commit v8 on v7

--- a/solution.py
+++ b/solution.py
@@ -236,9 +236,10 @@
     )(*released, *waits)
 
 
-def correlate_kernel(pieces, tile, scale, added, where_ref, *rest):
+def correlate_kernel(pieces, tile, scale, added, whole, where_ref, *rest):
     blocks = rest[:pieces]
     added_ref = rest[pieces] if added else None
+    channel = pl.program_id(0)
     out_ref, rows_ref = rest[-2:]
     inputs = blocks[0].shape[4]
     row_count, total = out_ref.shape[1:]
@@ -275,8 +276,8 @@
 
     def store(at, column_at, sums):
         if added:
-            sums = sums + added_ref[0, at, column_at]
-        out_ref[0, at, column_at] = (sums * scale if scale != 1.0 else sums).astype(out_ref.dtype)
+            sums = sums + added_ref[channel, at, column_at]
+        out_ref[channel if whole else 0, at, column_at] = (sums * scale if scale != 1.0 else sums).astype(out_ref.dtype)
 
     before = first_tile > 0
     start = jnp.where(before, 0, row_count)
@@ -307,24 +308,27 @@
     ]
     if added is not None:
         operands.append(added)
-        in_specs.append(pl.BlockSpec((1, row_count, total), lambda q, w: (q, 0, 0)))
+        in_specs.append(pl.BlockSpec(memory_space=pltpu.VMEM))
+    whole = dtype == jnp.float32
     aliases = {}
     if held is not None:
         aliases = {1 + len(operands): 0}
         operands.append(held)
         in_specs.append(pl.BlockSpec(memory_space=pl.ANY))
     return pl.pallas_call(
-        functools.partial(correlate_kernel, len(pieces), tile, scale, added is not None),
+        functools.partial(correlate_kernel, len(pieces), tile, scale, added is not None, whole),
         out_shape=jax.ShapeDtypeStruct((channels, row_count, total), dtype),
         grid_spec=pltpu.PrefetchScalarGridSpec(
             num_scalar_prefetch=1,
             grid=(count,),
             in_specs=in_specs,
-            out_specs=pl.BlockSpec((1, row_count, total), lambda q, w: (first + q, 0, 0)),
+            out_specs=pl.BlockSpec(memory_space=pltpu.VMEM)
+            if whole
+            else pl.BlockSpec((1, row_count, total), lambda q, w: (first + q, 0, 0)),
             scratch_shapes=[pltpu.VMEM((2 * row_count, depth), jnp.bfloat16)],
         ),
         input_output_aliases=aliases,
-        compiler_params=pltpu.CompilerParams(vmem_limit_bytes=VMEM),
+        compiler_params=pltpu.CompilerParams(vmem_limit_bytes=VMEM * 5 // 8 if whole or added is not None else VMEM),
         cost_estimate=pl.CostEstimate(
             flops=count * 8 * row_count * total * depth,
             bytes_accessed=count * 16 * total * depth,

time: 402 us -> 400 us (level)
  transfers between devices with their start and end apart: 5 -> 5, of which waited for: 3 -> 4; matrix products, arithmetic and copies ran while one was open for 0% -> 0% of each run, Pallas kernels for 14% -> 13%
where the time goes in v8:
time: 400 us; the launch traced here: 399 us
  blocking collectives  304 us (76%)
  Pallas kernels  59.6 us (15%)
  waiting for transfers between devices  23.1 us (6%)
  starting transfers between devices  12.1 us (3%)
    all_to_all x1, blocking collectives, across(): return lax.all_to_all(array, 'inp', split_axis=0, concat_axis=0, tiled=True)  304 us
    pallas_call x3, Pallas kernels, correlate(): pl.pallas_call(functools.partial(correlate_kernel, len(pieces), tile, sca...  34.9 us
    pallas_call x2, Pallas kernels, filter_bank(): pl.pallas_call(functools.partial(filter_kernel, halves, chunks, [first //...  24.8 us
    ppermute x3, waiting for transfers between devices, other_spans(): lax.ppermute(array, 'span', [(i, i ^ other) for i in range(spans)])  18.7 us
    all_to_all x2, starting transfers between devices, across(): return lax.all_to_all(array, 'inp', split_axis=0, concat_axis=0, tiled=True)  11.6 us
  transfers between devices with their start and end apart: 5, of which 4 were waited for; matrix products, arithmetic and copies ran while one was open for 0% of the time, Pallas kernels for 13%

profile of v8, /device:TPU:0, one launch (start us, length us, event | category | flops | bytes accessed | tf_op | source)
XLA Modules:
  0.0 399.2 jit_solution(8030881129444250315)
XLA Ops:
  0.0 3.4 filter_bank.2.rest_0_
  3.4 7.3 %all-to-all-start.1 = ((bf16[8,14,2,16,128]{4,3,2,1,0:T(8,128)(2,1)}), bf16[8,14,2,16,128]{4,3,2,1,0:T(8,128)(2,1)}, u32[]{:S(2)}, u32[]{:S(2)}) async-start(bf16[8,14,2,16,128]{4,3,2,1,0:T(8,128)(2,1)} %filter_bank.2.rest_0_), calls=%async_computation.1 | async-start | bytes 1835008 | tf_op jit(solution)/shard_map/all_to_all | solution.py:360
  10.6 21.4 %filter_bank.3 = (bf16[8,14,2,240,128]{4,3,2,1,0:T(8,128)(2,1)}, bf16[8,2,2,256,128]{4,3,2,1,0:T(8,128)(2,1)}) custom-call(bf16[2,4,128,8192]{3,2,1,0:T(8,128)(2,1)} %volt_ref.3, f32[2,4,32,128]{3,2,1,0:T(8,128)} %bitcast.3, bf16[512,768]{1,0:T(8,128)(2,1)} %constant.6.clone.table_ref, bf16[8,14,2,16,128]{4,3,2,1,0:T(8,128)(2,1)} %filter_bank.2.rest_0_), custom_call_target="tpu_custom_call" | custom-call | flops 25769803776 | bytes 67108864 | tf_op jit(solution)/shard_map/filter_bank/pallas_call | solution.py:187
  32.0 1.7 all-to-all-done.1.__1_.rest_0_
  33.8 304.3 %all_to_all.15.rest_2_ = bf16[8,14,2,240,128]{4,3,2,1,0:T(8,128)(2,1)} all-to-all(bf16[8,14,2,240,128]{4,3,2,1,0:T(8,128)(2,1)} %gate.2), channel_id=1, replica_groups=mesh['beam'=2,'inp'=8,'span'=2] {'inp'}, dimensions={0} | all-to-all | bytes 27525120 | tf_op jit(solution)/shard_map/all_to_all | solution.py:360
  338.1 0.0 collective-permute-start.1
  338.1 0.5 collective-permute-start
  338.6 4.4 %all-to-all-start = ((bf16[8,2,2,256,128]{4,3,2,1,0:T(8,128)(2,1)}), bf16[8,2,2,256,128]{4,3,2,1,0:T(8,128)(2,1)}, u32[]{:S(2)}, u32[]{:S(2)}) async-start(bf16[8,2,2,256,128]{4,3,2,1,0:T(8,128)(2,1)} %get-tuple-element.9), calls=%async_computation | async-start | bytes 4194304 | tf_op jit(solution)/shard_map/all_to_all | solution.py:360
  343.0 17.6 %collective-permute-done.rest_1_ = bf16[8,14,2,16,128]{4,3,2,1,0:T(8,128)(2,1)} collective-permute-done((bf16[8,14,2,16,128]{4,3,2,1,0:T(8,128)(2,1)}, bf16[8,14,2,16,128]{4,3,2,1,0:T(8,128)(2,1)}, u32[]{:S(2)}, u32[]{:S(2)}) %collective-permute-start) | collective-permute-done | bytes 917536 | tf_op jit(solution)/shard_map/ppermute | solution.py:364
  360.6 0.0 collective-permute-done.1.rest_3_
  360.6 28.4 %correlate.3.__1_ = bf16[16,512,1024]{2,1,0:T(8,128)(2,1)} custom-call(s32[1]{0:T(128)} %bitcast.where_ref, bf16[8,14,2,16,128]{4,3,2,1,0:T(8,128)(2,1)} %all-to-all-done.1.__1_.rest_0_, bf16[8,14,2,16,128]{4,3,2,1,0:T(8,128)(2,1)} %collective-permute-done.rest_1_, bf16[8,14,2,240,128]{4,3,2,1,0:T(8,128)(2,1)} %all_to_all.15.rest_2_, ...), custom_call_target="tpu_custom_call" | custom-call | flops 60129542144 | bytes 234881024 | tf_op jit(solution)/shard_map/correlate/pallas_call | solution.py:318
  389.0 2.6 all-to-all-done.__0_
  391.7 0.0 collective-permute-start.2
  391.7 3.3 correlate.4.rest_1_
  395.0 1.1 collective-permute-done.2.rest_0_
  396.0 3.2 correlate.5
  (2 shorter events, 0.0 us)
Async XLA Ops:
  3.4 30.4 %all-to-all-start.1 = ((bf16[8,14,2,16,128]{4,3,2,1,0:T(8,128)(2,1)}), bf16[8,14,2,16,128]{4,3,2,1,0:T(8,128)(2,1)}, u32[]{:S(2)}, u32[]{:S(2)}) async-start(bf16[8,14,2,16,128]{4,3,2,1,0:T(8,128)(2,1)} %filter_bank.2.rest_0_), calls=%async_computation.1 | async-start | bytes 1835008 | tf_op jit(solution)/shard_map/all_to_all | solution.py:360
  338.1 22.5 %collective-permute-start.1 = (bf16[8,14,2,240,128]{4,3,2,1,0:T(8,128)(2,1)}, bf16[8,14,2,240,128]{4,3,2,1,0:T(8,128)(2,1)}, u32[]{:S(2)}, u32[]{:S(2)}) collective-permute-start(bf16[8,14,2,240,128]{4,3,2,1,0:T(8,128)(2,1)} %all_to_all.15.rest_2_), channel_id=1, source_target_pairs={{0,1},{1,0},{2,3},{3,2},{4,5},{5,4},{6,7},{7,6},{8,9},{9,8},{10,11... | collective-permute-start | bytes 41287688 | tf_op jit(solution)/shard_map/ppermute | solution.py:364
  338.1 22.5 %collective-permute-start = (bf16[8,14,2,16,128]{4,3,2,1,0:T(8,128)(2,1)}, bf16[8,14,2,16,128]{4,3,2,1,0:T(8,128)(2,1)}, u32[]{:S(2)}, u32[]{:S(2)}) collective-permute-start(bf16[8,14,2,16,128]{4,3,2,1,0:T(8,128)(2,1)} %all-to-all-done.1.__1_.rest_0_), channel_id=1, source_target_pairs={{0,1},{1,0},{2,3},{3,2},{4,5},{5,4},{6,7},{7,6},{8,9},{9,8},{10,11... | collective-permute-start | bytes 2752520 | tf_op jit(solution)/shard_map/ppermute | solution.py:364
  338.6 53.1 %all-to-all-start = ((bf16[8,2,2,256,128]{4,3,2,1,0:T(8,128)(2,1)}), bf16[8,2,2,256,128]{4,3,2,1,0:T(8,128)(2,1)}, u32[]{:S(2)}, u32[]{:S(2)}) async-start(bf16[8,2,2,256,128]{4,3,2,1,0:T(8,128)(2,1)} %get-tuple-element.9), calls=%async_computation | async-start | bytes 4194304 | tf_op jit(solution)/shard_map/all_to_all | solution.py:360
  391.7 4.4 %collective-permute-start.2 = (bf16[8,2,2,256,128]{4,3,2,1,0:T(8,128)(2,1)}, bf16[8,2,2,256,128]{4,3,2,1,0:T(8,128)(2,1)S(1)}, u32[]{:S(2)}, u32[]{:S(2)}) collective-permute-start(bf16[8,2,2,256,128]{4,3,2,1,0:T(8,128)(2,1)} %get-tuple-element.11.rest_0_), channel_id=1, source_target_pairs={{0,1},{1,0},{2,3},{3,2},{4,5},{5,4},{6,7},{7,6},{8,9},{9,8},{10,11... | collective-permute-start | bytes 6291464 | tf_op jit(solution)/shard_map/ppermute | solution.py:364

commit v9 on v8

--- a/solution.py
+++ b/solution.py
@@ -250,7 +250,7 @@
     def columns_of(position):
         sources = [position * per_tile + index for index in range(per_tile)]
         parts = [
-            jnp.concatenate([block[source, 0, part] for source in sources], axis=1)
+            jnp.concatenate([block[source, channel if added else 0, part] for source in sources], axis=1)
             for part in range(2)
             for block in blocks
         ]
@@ -307,6 +307,7 @@
         for array, start in pieces
     ]
     if added is not None:
+        in_specs = [pl.BlockSpec(memory_space=pltpu.VMEM) for _ in pieces]
         operands.append(added)
         in_specs.append(pl.BlockSpec(memory_space=pltpu.VMEM))
     whole = dtype == jnp.float32

time: 400 us -> 400 us (level)
  no operation moved by 1% of the time
where the time goes in v9:
time: 400 us; the launch traced here: 399 us
  blocking collectives  304 us (76%)
  Pallas kernels  59.5 us (15%)
  waiting for transfers between devices  23.1 us (6%)
  starting transfers between devices  12.1 us (3%)
    all_to_all x1, blocking collectives, across(): return lax.all_to_all(array, 'inp', split_axis=0, concat_axis=0, tiled=True)  304 us
    pallas_call x3, Pallas kernels, correlate(): pl.pallas_call(functools.partial(correlate_kernel, len(pieces), tile, sca...  34.7 us
    pallas_call x2, Pallas kernels, filter_bank(): pl.pallas_call(functools.partial(filter_kernel, halves, chunks, [first //...  24.8 us
    ppermute x3, waiting for transfers between devices, other_spans(): lax.ppermute(array, 'span', [(i, i ^ other) for i in range(spans)])  18.7 us
    all_to_all x2, starting transfers between devices, across(): return lax.all_to_all(array, 'inp', split_axis=0, concat_axis=0, tiled=True)  11.6 us
  transfers between devices with their start and end apart: 5, of which 4 were waited for; matrix products, arithmetic and copies ran while one was open for 0% of the time, Pallas kernels for 13%

profile of v9, /device:TPU:0, one launch (start us, length us, event | category | flops | bytes accessed | tf_op | source)
XLA Modules:
  0.0 399.0 jit_solution(2367991557248410597)
XLA Ops:
  0.0 3.4 filter_bank.2.rest_0_
  3.4 7.3 %all-to-all-start.1 = ((bf16[8,14,2,16,128]{4,3,2,1,0:T(8,128)(2,1)}), bf16[8,14,2,16,128]{4,3,2,1,0:T(8,128)(2,1)}, u32[]{:S(2)}, u32[]{:S(2)}) async-start(bf16[8,14,2,16,128]{4,3,2,1,0:T(8,128)(2,1)} %filter_bank.2.rest_0_), calls=%async_computation.1 | async-start | bytes 1835008 | tf_op jit(solution)/shard_map/all_to_all | solution.py:361
  10.6 21.4 %filter_bank.3 = (bf16[8,14,2,240,128]{4,3,2,1,0:T(8,128)(2,1)}, bf16[8,2,2,256,128]{4,3,2,1,0:T(8,128)(2,1)}) custom-call(bf16[2,4,128,8192]{3,2,1,0:T(8,128)(2,1)} %volt_ref.3, f32[2,4,32,128]{3,2,1,0:T(8,128)} %bitcast.3, bf16[512,768]{1,0:T(8,128)(2,1)} %constant.6.clone.table_ref, bf16[8,14,2,16,128]{4,3,2,1,0:T(8,128)(2,1)} %filter_bank.2.rest_0_), custom_call_target="tpu_custom_call" | custom-call | flops 25769803776 | bytes 67108864 | tf_op jit(solution)/shard_map/filter_bank/pallas_call | solution.py:187
  32.0 1.7 all-to-all-done.1.__1_.rest_0_
  33.8 304.3 %all_to_all.15.rest_2_ = bf16[8,14,2,240,128]{4,3,2,1,0:T(8,128)(2,1)} all-to-all(bf16[8,14,2,240,128]{4,3,2,1,0:T(8,128)(2,1)} %gate.2), channel_id=1, replica_groups=mesh['beam'=2,'inp'=8,'span'=2] {'inp'}, dimensions={0} | all-to-all | bytes 27525120 | tf_op jit(solution)/shard_map/all_to_all | solution.py:361
  338.1 0.0 collective-permute-start.1
  338.1 0.5 collective-permute-start
  338.6 4.4 %all-to-all-start = ((bf16[8,2,2,256,128]{4,3,2,1,0:T(8,128)(2,1)}), bf16[8,2,2,256,128]{4,3,2,1,0:T(8,128)(2,1)}, u32[]{:S(2)}, u32[]{:S(2)}) async-start(bf16[8,2,2,256,128]{4,3,2,1,0:T(8,128)(2,1)} %get-tuple-element.9), calls=%async_computation | async-start | bytes 4194304 | tf_op jit(solution)/shard_map/all_to_all | solution.py:361
  343.0 17.6 %collective-permute-done.rest_1_ = bf16[8,14,2,16,128]{4,3,2,1,0:T(8,128)(2,1)} collective-permute-done((bf16[8,14,2,16,128]{4,3,2,1,0:T(8,128)(2,1)}, bf16[8,14,2,16,128]{4,3,2,1,0:T(8,128)(2,1)}, u32[]{:S(2)}, u32[]{:S(2)}) %collective-permute-start) | collective-permute-done | bytes 917536 | tf_op jit(solution)/shard_map/ppermute | solution.py:365
  360.6 0.0 collective-permute-done.1.rest_3_
  360.6 28.4 %correlate.3.__1_ = bf16[16,512,1024]{2,1,0:T(8,128)(2,1)} custom-call(s32[1]{0:T(128)} %bitcast.where_ref, bf16[8,14,2,16,128]{4,3,2,1,0:T(8,128)(2,1)} %all-to-all-done.1.__1_.rest_0_, bf16[8,14,2,16,128]{4,3,2,1,0:T(8,128)(2,1)} %collective-permute-done.rest_1_, bf16[8,14,2,240,128]{4,3,2,1,0:T(8,128)(2,1)} %all_to_all.15.rest_2_, ...), custom_call_target="tpu_custom_call" | custom-call | flops 60129542144 | bytes 234881024 | tf_op jit(solution)/shard_map/correlate/pallas_call | solution.py:319
  389.0 2.6 all-to-all-done.__0_
  391.7 0.0 collective-permute-start.2
  391.7 3.3 correlate.4.rest_1_
  395.0 1.1 collective-permute-done.2.rest_0_
  396.0 3.0 correlate.5
  (2 shorter events, 0.0 us)
Async XLA Ops:
  3.4 30.4 %all-to-all-start.1 = ((bf16[8,14,2,16,128]{4,3,2,1,0:T(8,128)(2,1)}), bf16[8,14,2,16,128]{4,3,2,1,0:T(8,128)(2,1)}, u32[]{:S(2)}, u32[]{:S(2)}) async-start(bf16[8,14,2,16,128]{4,3,2,1,0:T(8,128)(2,1)} %filter_bank.2.rest_0_), calls=%async_computation.1 | async-start | bytes 1835008 | tf_op jit(solution)/shard_map/all_to_all | solution.py:361
  338.1 22.5 %collective-permute-start.1 = (bf16[8,14,2,240,128]{4,3,2,1,0:T(8,128)(2,1)}, bf16[8,14,2,240,128]{4,3,2,1,0:T(8,128)(2,1)}, u32[]{:S(2)}, u32[]{:S(2)}) collective-permute-start(bf16[8,14,2,240,128]{4,3,2,1,0:T(8,128)(2,1)} %all_to_all.15.rest_2_), channel_id=1, source_target_pairs={{0,1},{1,0},{2,3},{3,2},{4,5},{5,4},{6,7},{7,6},{8,9},{9,8},{10,11... | collective-permute-start | bytes 41287688 | tf_op jit(solution)/shard_map/ppermute | solution.py:365
  338.1 22.5 %collective-permute-start = (bf16[8,14,2,16,128]{4,3,2,1,0:T(8,128)(2,1)}, bf16[8,14,2,16,128]{4,3,2,1,0:T(8,128)(2,1)}, u32[]{:S(2)}, u32[]{:S(2)}) collective-permute-start(bf16[8,14,2,16,128]{4,3,2,1,0:T(8,128)(2,1)} %all-to-all-done.1.__1_.rest_0_), channel_id=1, source_target_pairs={{0,1},{1,0},{2,3},{3,2},{4,5},{5,4},{6,7},{7,6},{8,9},{9,8},{10,11... | collective-permute-start | bytes 2752520 | tf_op jit(solution)/shard_map/ppermute | solution.py:365
  338.6 53.1 %all-to-all-start = ((bf16[8,2,2,256,128]{4,3,2,1,0:T(8,128)(2,1)}), bf16[8,2,2,256,128]{4,3,2,1,0:T(8,128)(2,1)}, u32[]{:S(2)}, u32[]{:S(2)}) async-start(bf16[8,2,2,256,128]{4,3,2,1,0:T(8,128)(2,1)} %get-tuple-element.9), calls=%async_computation | async-start | bytes 4194304 | tf_op jit(solution)/shard_map/all_to_all | solution.py:361
  391.7 4.4 %collective-permute-start.2 = (bf16[8,2,2,256,128]{4,3,2,1,0:T(8,128)(2,1)}, bf16[8,2,2,256,128]{4,3,2,1,0:T(8,128)(2,1)S(1)}, u32[]{:S(2)}, u32[]{:S(2)}) collective-permute-start(bf16[8,2,2,256,128]{4,3,2,1,0:T(8,128)(2,1)} %get-tuple-element.11.rest_0_), channel_id=1, source_target_pairs={{0,1},{1,0},{2,3},{3,2},{4,5},{5,4},{6,7},{7,6},{8,9},{9,8},{10,11... | collective-permute-start | bytes 6291464 | tf_op jit(solution)/shard_map/ppermute | solution.py:365
